TPU v7x, 32 devices: a whole 2x2x4 slice. The times are simulated.
32 devices in a mesh: groups: 2 (over y), expert: 4 (over x, core), tensor: 4 (over z).
Axes of the slice: x: 2, y: 2, z: 4, core: 2. Of those that a mesh axis runs over, the one named last changes fastest.
Arguments:
- tokens: bfloat16 [2, 8, 4096], P(None, 'groups', 'expert'), parts along dimension 1, may hold values from -6 to 6
- proj_gate: bfloat16 [4096, 8192], P('expert', 'tensor'), may hold values from -0.09375 to 0.09375
- proj_input: bfloat16 [4096, 8192], P('expert', 'tensor'), may hold values from -0.09375 to 0.09375
- proj_write: bfloat16 [4096, 1024], P('expert', 'tensor'), may hold values from -0.09375 to 0.09375
- proj_read: bfloat16 [4096, 1024], P('expert', 'tensor'), may hold values from -0.09375 to 0.09375
- proj_step: bfloat16 [4096, 128], P('expert', 'tensor'), may hold values from -0.09375 to 0.09375
- conv_input: float32 [4, 8192], P(None, 'tensor'), may hold values from -3 to 3
- conv_write: float32 [4, 1024], P(None, 'tensor'), may hold values from -3 to 3
- conv_read: float32 [4, 1024], P(None, 'tensor'), may hold values from -3 to 3
- window_input: bfloat16 [8, 3, 8192], P(('groups', 'expert'), None, 'tensor'), parts along dimension 0, may hold values from -6 to 6
- window_write: bfloat16 [8, 3, 1024], P(('groups', 'expert'), None, 'tensor'), parts along dimension 0, may hold values from -6 to 6
- window_read: bfloat16 [8, 3, 1024], P(('groups', 'expert'), None, 'tensor'), parts along dimension 0, may hold values from -6 to 6
- step_bias: float32 [128], P('tensor'), may hold values from -4.5 to -1.5
- decay_log: float32 [128], P('tensor'), may hold values from 0 to 2.7
- skip_gain: float32 [128], P('tensor'), may hold values from 0.5 to 1.5
- norm_gain: float32 [8192], P('tensor'), may hold values from 0.1 to 1.9
- ssm_state: float32 [8, 128, 64, 128], P(('groups', 'expert'), 'tensor'), parts along dimension 0, may hold values from -1.6 to 1.6
- out_proj: bfloat16 [8192, 4096], P('tensor', 'expert'), may hold values from -0.0625 to 0.0625
- expert_up: bfloat16 [16, 4096, 1024], P('expert', None, 'tensor'), may hold values from -0.09375 to 0.09375
- expert_down: bfloat16 [16, 1024, 4096], P('expert', 'tensor'), may hold values from -0.1875 to 0.1875
- expert_ids: int32 [2, 8, 8], P(None, 'groups'), parts along dimension 1, may hold values from 0 to 15, all different within a row; in each aligned block of 4 rows (0 to 3, 4 to 7, ..., all dimensions but the last counted through in order) at most 4 rows name the same one
- route_gates: float32 [2, 8, 8], P(None, 'groups'), parts along dimension 1, may hold values from 0.05 to 0.35
Outputs:
- mixed_out: bfloat16 [2, 8, 4096], P(None, 'groups', 'expert'), parts along dimension 1
- ssm_final: float32 [8, 128, 64, 128], P(('groups', 'expert'), 'tensor'), parts along dimension 0
- input_final: bfloat16 [8, 3, 8192], P(('groups', 'expert'), None, 'tensor'), parts along dimension 0
- write_final: bfloat16 [8, 3, 1024], P(('groups', 'expert'), None, 'tensor'), parts along dimension 0
- read_final: bfloat16 [8, 3, 1024], P(('groups', 'expert'), None, 'tensor'), parts along dimension 0
There are 2 independent parts, one for each index of `groups`. A program takes and returns all parts, laid end to end along the dimension named above; an argument that names none is the same for every part. Nothing has to cross between parts.
Inputs may be any that keep to these rules, and one draw needn't show every extreme that they name: `expert_ids`: each row names 8 different experts. In each step no expert is named by more than 4 rows, and in some step some expert is named by exactly 4 rows.
All inputs are finite; a program needn't handle non-finite values.
Results may differ from a plain program's by a relative error of at most 0.0066.
Values may be sent and summed in bfloat16 or wider, within the bound.
No kernel may reach another device: no remote copies, remote signals or barrier semaphores. Data moves between devices by JAX's collectives and lax.ppermute only.
A program may use at most 128 MiB of HBM per device.

v0:
```python
import jax
import jax.numpy as jnp
from jax import lax
from jax.sharding import PartitionSpec as P


def silu_float(values):
    return values / (1.0 + jnp.exp(-values))


def convolve(window_state, newest, kernel):
    window = jnp.concatenate([window_state, newest[:, None, :]], axis=1)
    summed = jnp.sum(window.astype(jnp.float32) * kernel[None, :, :], axis=1)
    return (silu_float(summed), window[:, 1:, :])


def sum_heads(values):
    return lax.psum(values, "tensor")


def send_back(values):
    return lax.all_to_all(values, "expert", split_axis=3, concat_axis=0, tiled=True)


def mamba_step(current, carried, weights_in, params):
    window_input, window_write, window_read, ssm_now = carried
    conv_input, conv_write, conv_read, step_bias, decay_log, skip_gain, norm_gain, out_proj = params
    own_rows = ssm_now.shape[0]
    head_dim = ssm_now.shape[2]
    state_size = ssm_now.shape[3]
    inner_local = conv_input.shape[1]
    write_width = conv_write.shape[1]
    heads_local = step_bias.shape[0]
    groups_local = write_width // state_size
    heads_group = heads_local // groups_local
    projected = lax.psum_scatter(
        jnp.dot(current, weights_in, preferred_element_type=jnp.float32),
        "expert",
        scatter_dimension=0,
        tiled=True,
    ).astype(jnp.bfloat16)
    gate_pre = projected[:, :inner_local]
    input_pre = projected[:, inner_local : 2 * inner_local]
    write_pre = projected[:, 2 * inner_local : 2 * inner_local + write_width]
    read_pre = projected[:, 2 * inner_local + write_width : 2 * inner_local + 2 * write_width]
    step_pre = projected[:, 2 * inner_local + 2 * write_width :]
    input_act, window_input = convolve(window_input, input_pre, conv_input)
    write_act, window_write = convolve(window_write, write_pre, conv_write)
    read_act, window_read = convolve(window_read, read_pre, conv_read)
    step_size = jax.nn.softplus(step_pre.astype(jnp.float32) + step_bias[None, :])
    decay_rate = jnp.exp(-step_size * jnp.exp(decay_log)[None, :])
    heads_input = input_act.reshape(own_rows, groups_local, heads_group, head_dim)
    write_grouped = write_act.reshape(own_rows, groups_local, 1, 1, state_size)
    read_grouped = read_act.reshape(own_rows, groups_local, 1, 1, state_size)
    grouped = ssm_now.reshape(own_rows, groups_local, heads_group, head_dim, state_size)
    grouped = (
        decay_rate.reshape(own_rows, groups_local, heads_group, 1, 1) * grouped
        + step_size.reshape(own_rows, groups_local, heads_group, 1, 1)
        * heads_input[..., None]
        * write_grouped
    )
    ssm_read = (
        jnp.sum(grouped * read_grouped, axis=-1)
        + skip_gain.reshape(groups_local, heads_group, 1) * heads_input
    )
    ssm_now = grouped.reshape(own_rows, heads_local, head_dim, state_size)
    gated_out = ssm_read.reshape(own_rows, groups_local, heads_group * head_dim) * silu_float(
        gate_pre.astype(jnp.float32)
    ).reshape(own_rows, groups_local, heads_group * head_dim)
    normed = (
        gated_out
        * lax.rsqrt(jnp.mean(gated_out * gated_out, axis=-1, keepdims=True) + 1e-05)
        * norm_gain.reshape(groups_local, heads_group * head_dim)
    )
    normed = normed.reshape(own_rows, inner_local).astype(jnp.bfloat16)
    partial_out = jnp.dot(
        lax.all_gather(normed, "expert", axis=0, tiled=True),
        out_proj,
        preferred_element_type=jnp.float32,
    )
    residual = current.astype(jnp.float32) + sum_heads(partial_out)
    return (residual, (window_input, window_write, window_read, ssm_now))


def mixture(residual, route_ids, route_weights, expert_up, expert_down):
    steps_here, rows_all, top_count = route_ids.shape
    owners = lax.axis_size("expert")
    local_experts = expert_up.shape[0]
    experts_all = local_experts * owners
    own_rows = rows_all // owners
    capacity = min(rows_all, 2 * own_rows * top_count // local_experts)
    slots_all = experts_all * capacity
    moe_in = residual.astype(jnp.bfloat16)
    expert_iota = jnp.arange(experts_all, dtype=jnp.int32)
    onehot = (
        (route_ids[..., None] == expert_iota)
        .astype(jnp.int32)
        .reshape(steps_here, rows_all * top_count, experts_all)
    )
    before = jnp.cumsum(onehot, axis=1) - onehot
    position = jnp.sum(before * onehot, axis=2).reshape(steps_here, rows_all, top_count)
    slot_of = route_ids * capacity + position
    slot_iota = jnp.arange(slots_all, dtype=jnp.int32)
    matches = slot_of[:, :, :, None] == slot_iota
    placing = jnp.any(matches, axis=2).astype(jnp.bfloat16)
    combine = jnp.sum(jnp.where(matches, route_weights[..., None], 0.0), axis=2)
    packed = jnp.einsum("srq,srd->qsd", placing, moe_in, preferred_element_type=jnp.float32).astype(
        jnp.bfloat16
    )
    packed = packed.reshape(owners, local_experts * capacity, steps_here, packed.shape[2])
    arrived = lax.all_to_all(packed, "expert", split_axis=0, concat_axis=3, tiled=True)
    width_all = arrived.shape[3]
    arrived = arrived.reshape(local_experts, capacity, steps_here, width_all)
    hidden = jnp.einsum("ecsd,edh->ecsh", arrived, expert_up, preferred_element_type=jnp.float32)
    hidden = jnp.maximum(hidden, 0.0)
    hidden = (hidden * hidden).astype(jnp.bfloat16)
    partial_out = jnp.einsum(
        "ecsh,ehd->ecsd", hidden, expert_down, preferred_element_type=jnp.float32
    )
    partial_out = partial_out.reshape(1, local_experts * capacity, steps_here, width_all)
    returned = send_back(sum_heads(partial_out)).reshape(slots_all, steps_here, width_all // owners)
    moe_out = jnp.einsum("srq,qsd->srd", combine, returned, precision=lax.Precision.HIGHEST)
    return (residual + moe_out).astype(jnp.bfloat16)


def per_device(
    tokens,
    proj_gate,
    proj_input,
    proj_write,
    proj_read,
    proj_step,
    conv_input,
    conv_write,
    conv_read,
    window_input,
    window_write,
    window_read,
    step_bias,
    decay_log,
    skip_gain,
    norm_gain,
    ssm_state,
    out_proj,
    expert_up,
    expert_down,
    expert_ids,
    route_gates,
):
    weights_in = jnp.concatenate([proj_gate, proj_input, proj_write, proj_read, proj_step], axis=1)
    params = (
        conv_input,
        conv_write,
        conv_read,
        step_bias,
        decay_log,
        skip_gain,
        norm_gain,
        out_proj,
    )
    carried = (window_input, window_write, window_read, ssm_state)
    step_count = tokens.shape[0]
    results = []
    for step_index in range(step_count):
        residual, carried = mamba_step(tokens[step_index], carried, weights_in, params)
        results.append(
            mixture(
                residual[None],
                expert_ids[step_index : step_index + 1],
                route_gates[step_index : step_index + 1],
                expert_up,
                expert_down,
            )
        )
    mixed_out = jnp.concatenate(results, axis=0)
    input_final, write_final, read_final, ssm_final = carried
    return (mixed_out, ssm_final, input_final, write_final, read_final)


def solution(mesh):
    placed = (
        P(None, "groups", "expert"),
        P("expert", "tensor"),
        P("expert", "tensor"),
        P("expert", "tensor"),
        P("expert", "tensor"),
        P("expert", "tensor"),
        P(None, "tensor"),
        P(None, "tensor"),
        P(None, "tensor"),
        P(("groups", "expert"), None, "tensor"),
        P(("groups", "expert"), None, "tensor"),
        P(("groups", "expert"), None, "tensor"),
        P("tensor"),
        P("tensor"),
        P("tensor"),
        P("tensor"),
        P(("groups", "expert"), "tensor", None, None),
        P("tensor", "expert"),
        P("expert", None, "tensor"),
        P("expert", "tensor", None),
        P(None, "groups", None),
        P(None, "groups", None),
    )
    return jax.shard_map(
        per_device,
        mesh=mesh,
        in_specs=placed,
        out_specs=(
            P(None, "groups", "expert"),
            P(("groups", "expert"), "tensor", None, None),
            P(("groups", "expert"), None, "tensor"),
            P(("groups", "expert"), None, "tensor"),
            P(("groups", "expert"), None, "tensor"),
        ),
        check_vma=False,
    )
```

profile of v0, /device:TPU:0, one launch (start us, length us, event | category | flops | bytes accessed | tf_op | source)
XLA Modules:
  0.0 345.9 jit_solution(2757268130801530455)
XLA Ops:
  7.2 4.9 %constant_dynamic-update-slice_fusion.4 = bf16[1024,4640]{1,0:T(8,128)(2,1)} fusion(bf16[1024,2048]{1,0:T(8,128)(2,1)} %param.23), kind=kLoop, calls=%fused_computation.49 | loop fusion | bytes 8388608
  12.3 4.9 %constant_dynamic-update-slice_fusion.3 = bf16[1024,4640]{1,0:T(8,128)(2,1)} fusion(bf16[1024,4640]{1,0:T(8,128)(2,1)} %constant_dynamic-update-slice_fusion.4, bf16[1024,2048]{1,0:T(8,128)(2,1)} %param.24), kind=kLoop, calls=%fused_computation.48 | loop fusion | bytes 8388608
  17.2 0.9 constant_dynamic-update-slice_fusion.2
  18.1 0.9 constant_dynamic-update-slice_fusion.1
  19.8 5.3 %convolution_bitcast_fusion = f32[4,4640]{1,0:T(4,128)S(1)} fusion(bf16[1024,4640]{1,0:T(8,128)(2,1)} %constant_dynamic-update-slice_fusion, bf16[2,4,1024]{2,1,0:T(4,128)(2,1)S(1)} %copy-done.4), kind=kOutput, calls=%fused_computation | convolution fusion | flops 38010880 | bytes 9585152 | tf_op jit(solution)/shard_map/dot_general | solution.py:37
  25.0 1.2 copy-done
  26.4 1.4 convolution_bitcast_fusion.1
  27.7 15.0 %all-reduce.9 = (bf16[4,4640]{1,0:T(4,128)(2,1)S(1)}, bf16[4,4640]{1,0:T(4,128)(2,1)S(1)}) all-reduce(f32[4,4640]{1,0:T(4,128)S(1)} %convolution_bitcast_fusion.1, f32[4,4640]{1,0:T(4,128)S(1)} %convolution_bitcast_fusion), channel_id=4, replica_groups=mesh['groups'=2,'expert'=4,'tensor'=4] {'expert'}, use_global_device_ids=true, to_apply=%region_0.0.clone | all-reduce | flops 37120 | bytes 222720
  45.4 2.2 multiply_reduce_fusion
  49.9 5.2 %all-gather = bf16[8192]{0:T(1024)(128)(2,1)S(1)} all-gather(bf16[2048]{0:T(1024)(128)(2,1)S(1)} %get-tuple-element.42), channel_id=2, replica_groups=mesh['groups'=2,'expert'=4,'tensor'=4] {'expert'}, dimensions={0}, use_global_device_ids=true | all-gather | bytes 20480 | tf_op jit(solution)/shard_map/all_gather | solution.py:77
  55.1 5.2 %all-gather.1 = bf16[8192]{0:T(1024)(128)(2,1)S(1)} all-gather(bf16[2048]{0:T(1024)(128)(2,1)S(1)} %get-tuple-element.43), channel_id=3, replica_groups=mesh['groups'=2,'expert'=4,'tensor'=4] {'expert'}, dimensions={0}, use_global_device_ids=true | all-gather | bytes 20480 | tf_op jit(solution)/shard_map/all_gather | solution.py:77
  60.2 2.8 fusion.47
  63.1 2.8 fusion.48
  66.9 19.3 %all-reduce.2 = (f32[4,1024]{1,0:T(4,128)S(1)}, f32[4,1024]{1,0:T(4,128)S(1)}) all-reduce(f32[4,1024]{1,0:T(4,128)S(1)} %fusion.48, f32[4,1024]{1,0:T(4,128)S(1)} %fusion.47), channel_id=1, replica_groups=mesh['groups'=2,'expert'=4,'tensor'=4] {'tensor'}, use_global_device_ids=true, to_apply=%region_18.19 | all-reduce | flops 8192 | bytes 65536 | tf_op jit(solution)/shard_map/psum | solution.py:18
  87.2 3.3 all-to-all-start
  91.4 3.7 %all-to-all-done = bf16[4,16,1,1024]{3,1,2,0:T(8,128)(2,1)S(1)} async-done(((bf16[4,16,1,1024]{3,1,2,0:T(8,128)(2,1)}), bf16[4,16,1,1024]{3,1,2,0:T(8,128)(2,1)S(1)}, u32[]{:S(2)}, u32[]{:S(2)}) %all-to-all-start) | async-done | bytes 131104 | tf_op jit(solution)/shard_map/all_to_all | solution.py:111
  95.1 3.3 all-to-all-start.2
  98.9 8.0 %fusion.9 = f32[4,4,4096]{2,1,0:T(4,128)S(1)} fusion(bf16[4,256,4096]{2,1,0:T(8,128)(2,1)} %param.41, bf16[4,4,4096]{2,1,0:T(4,128)(2,1)S(1)} %reshape.840, bf16[4,4096,256]{2,1,0:T(8,128)(2,1)} %param.40), kind=kOutput, calls=%fused_computation.21 | convolution fusion | flops 67121152 | bytes 17170432 | tf_op jit(solution)/shard_map/ecsh,ehd->ecsd/dot_general | solution.py:117
  107.0 3.7 %copy.50 = f32[1,16,1,4096]{1,2,0,3:T(1,128)} copy(f32[1,16,1,4096]{3,1,2,0:T(8,128)S(1)} %reshape.841) | data formatting | bytes 524288 | tf_op jit(solution)/shard_map/reshape | solution.py:120
  111.0 8.0 %fusion.8 = f32[4,4,4096]{2,1,0:T(4,128)S(1)} fusion(bf16[4,256,4096]{2,1,0:T(8,128)(2,1)} %param.41, bf16[4,4,4096]{2,1,0:T(4,128)(2,1)S(1)} %reshape.847, bf16[4,4096,256]{2,1,0:T(8,128)(2,1)} %param.40), kind=kOutput, calls=%fused_computation.20 | convolution fusion | flops 67121152 | bytes 17170432 | tf_op jit(solution)/shard_map/ecsh,ehd->ecsd/dot_general | solution.py:117
  119.1 3.7 %copy.55 = f32[1,16,1,4096]{1,2,0,3:T(1,128)} copy(f32[1,16,1,4096]{3,1,2,0:T(8,128)S(1)} %reshape.848) | data formatting | bytes 524288 | tf_op jit(solution)/shard_map/reshape | solution.py:120
  123.6 153.3 %all-reduce.8.cloned.1.call-done = (f32[1,16,1,4096]{1,2,0,3:T(1,128)}, f32[1,16,1,4096]{1,2,0,3:T(1,128)}) async-done(((f32[1,16,1,4096]{1,2,0,3:T(1,128)}, f32[1,16,1,4096]{1,2,0,3:T(1,128)}), (f32[1,16,1,4096]{1,2,0,3:T(1,128)}, f32[1,16,1,4096]{1,2,0,3:T(1,128)})) %all-reduce.8.cloned.1.call-update) | async-done | bytes 524304 | tf_op jit(solution)/shard_map/psum | solution.py:18
  277.3 19.1 %reduce.36 = f32[4096,16]{1,0:T(8,128)S(1)} reduce(f32[4096,1,1,16]{3,2,1,0:T(1,128)} %bitcast.179, f32[]{:T(128)} %broadcast.448), dimensions={1,2}, to_apply=%bitcast.151.reduce_sub_computation | reduce | bytes 524292
  296.4 1.5 reshape.872
  297.9 3.6 %all-to-all-start.1 = ((f32[4,1,16384]{2,1,0:T(1,128)}), f32[4,1,16384]{2,1,0:T(1,128)S(1)}, u32[]{:S(2)}, u32[]{:S(2)}) async-start(f32[4,1,16384]{2,1,0:T(1,128)} %reshape.872), calls=%async_computation.1 | async-start | bytes 524288 | tf_op jit(solution)/shard_map/all_to_all | solution.py:22
  301.6 19.1 %reduce.34 = f32[4096,16]{1,0:T(8,128)S(1)} reduce(f32[4096,1,1,16]{3,2,1,0:T(1,128)} %bitcast.178, f32[]{:T(128)} %broadcast.448), dimensions={1,2}, to_apply=%bitcast.149.reduce_sub_computation | reduce | bytes 524292
  320.6 1.4 reshape.870
  322.1 3.4 all-to-all-start.3
  326.1 1.4 reduce.37
  327.5 3.7 %reshape.873 = f32[4096,1,1,16]{3,2,1,0:T(1,128)S(1)} reshape(f32[4,16384]{1,0:T(4,128)S(1)} %reduce.37) | data formatting | bytes 524288
  332.0 1.4 reduce.35
  333.4 3.7 %reshape.871 = f32[4096,1,1,16]{3,2,1,0:T(1,128)S(1)} reshape(f32[4,16384]{1,0:T(4,128)S(1)} %reduce.35) | data formatting | bytes 524288
  (126 shorter events, 14.0 us)
Async XLA Ops:
  7.2 5.0 %copy-start.6 = (bf16[1024,32]{0,1:T(8,128)(2,1)S(1)}, bf16[1024,32]{0,1:T(8,128)(2,1)}, u32[]{:S(2)}) copy-start(bf16[1024,32]{0,1:T(8,128)(2,1)} %param.27) | copy-start | bytes 196612
  7.2 10.0 %copy-start.2 = (bf16[1024,256]{1,0:T(8,128)(2,1)S(1)}, bf16[1024,256]{1,0:T(8,128)(2,1)}, u32[]{:S(2)}) copy-start(bf16[1024,256]{1,0:T(8,128)(2,1)} %param.25) | copy-start | bytes 1572868
  7.2 10.9 %copy-start.3 = (bf16[1024,256]{1,0:T(8,128)(2,1)S(1)}, bf16[1024,256]{1,0:T(8,128)(2,1)}, u32[]{:S(2)}) copy-start(bf16[1024,256]{1,0:T(8,128)(2,1)} %param.26) | copy-start | bytes 1572868
  7.2 12.6 %copy-start.4 = (bf16[2,4,1024]{2,1,0:T(4,128)(2,1)S(1)}, bf16[2,4,1024]{2,1,0:T(4,128)(2,1)}, u32[]{:S(2)}) copy-start(bf16[2,4,1024]{2,1,0:T(4,128)(2,1)} %param.22) | copy-start | bytes 49156
  19.8 6.5 %copy-start = (bf16[1024,4640]{1,0:T(8,128)(2,1)S(1)}, bf16[1024,4640]{1,0:T(8,128)(2,1)}, u32[]{:S(2)}) copy-start(bf16[1024,4640]{1,0:T(8,128)(2,1)} %constant_dynamic-update-slice_fusion) | copy-start | bytes 28508164
  26.3 16.4 %copy-start.18 = (u32[32]{0:T(128)S(1)}, u32[32]{0:T(128)}, u32[]{:S(2)}) copy-start(u32[32]{0:T(128)} %constant.33) | copy-start | bytes 388
  26.3 18.5 %copy-start.5 = (bf16[1,3,2048]{2,1,0:T(4,128)(2,1)S(1)}, bf16[1,3,2048]{2,1,0:T(4,128)(2,1)}, u32[]{:S(2)}) copy-start(bf16[1,3,2048]{2,1,0:T(4,128)(2,1)} %param.31) | copy-start | bytes 36868
  26.3 18.5 %copy-start.7 = (f32[4,2048]{1,0:T(4,128)S(1)}, f32[4,2048]{1,0:T(4,128)}, u32[]{:S(2)}) copy-start(f32[4,2048]{1,0:T(4,128)} %param.28) | copy-start | bytes 98308
  26.3 18.8 %copy-start.9 = (bf16[1,3,256]{2,1,0:T(4,128)(2,1)S(1)}, bf16[1,3,256]{2,1,0:T(4,128)(2,1)}, u32[]{:S(2)}) copy-start(bf16[1,3,256]{2,1,0:T(4,128)(2,1)} %param.32) | copy-start | bytes 4612
  26.3 18.8 %copy-start.8 = (bf16[1,3,256]{2,1,0:T(4,128)(2,1)S(1)}, bf16[1,3,256]{2,1,0:T(4,128)(2,1)}, u32[]{:S(2)}) copy-start(bf16[1,3,256]{2,1,0:T(4,128)(2,1)} %param.33) | copy-start | bytes 4612
  26.3 18.8 %copy-start.13 = (f32[4,256]{1,0:T(4,128)S(1)}, f32[4,256]{1,0:T(4,128)}, u32[]{:S(2)}) copy-start(f32[4,256]{1,0:T(4,128)} %param.30) | copy-start | bytes 12292
  26.3 18.8 %copy-start.14 = (f32[4,256]{1,0:T(4,128)S(1)}, f32[4,256]{1,0:T(4,128)}, u32[]{:S(2)}) copy-start(f32[4,256]{1,0:T(4,128)} %param.29) | copy-start | bytes 12292
  26.3 18.9 %copy-start.15 = (f32[32]{0:T(128)S(1)}, f32[32]{0:T(128)}, u32[]{:S(2)}) copy-start(f32[32]{0:T(128)} %param.35) | copy-start | bytes 388
  26.3 18.9 %copy-start.16 = (f32[32]{0:T(128)S(1)}, f32[32]{0:T(128)}, u32[]{:S(2)}) copy-start(f32[32]{0:T(128)} %param.34) | copy-start | bytes 388
  26.3 19.1 %copy-start.1 = (f32[1,32,64,128]{3,2,1,0:T(8,128)S(1)}, f32[1,32,64,128]{3,2,1,0:T(8,128)}, u32[]{:S(2)}) copy-start(f32[1,32,64,128]{3,2,1,0:T(8,128)} %param.38) | copy-start | bytes 3145732
  26.4 21.5 %copy-start.17 = (f32[32]{0:T(128)S(1)}, f32[32]{0:T(128)}, u32[]{:S(2)}) copy-start(f32[32]{0:T(128)} %param.36) | copy-start | bytes 388
  26.4 23.4 %copy-start.11 = (f32[2048]{0:T(1024)S(1)}, f32[2048]{0:T(1024)}, u32[]{:S(2)}) copy-start(f32[2048]{0:T(1024)} %param.37) | copy-start | bytes 24580
  27.7 38.2 %copy-start.10 = (s32[2,4,8]{2,1,0:T(4,128)S(1)}, s32[2,4,8]{2,1,0:T(4,128)}, u32[]{:S(2)}) copy-start(s32[2,4,8]{2,1,0:T(4,128)} %param.42) | copy-start | bytes 772
  87.2 7.9 %all-to-all-start = ((bf16[4,16,1,1024]{3,1,2,0:T(8,128)(2,1)}), bf16[4,16,1,1024]{3,1,2,0:T(8,128)(2,1)S(1)}, u32[]{:S(2)}, u32[]{:S(2)}) async-start(bf16[4,16,1,1024]{3,1,2,0:T(8,128)(2,1)} %bitcast.20), calls=%async_computation | async-start | bytes 262144 | tf_op jit(solution)/shard_map/all_to_all | solution.py:111
  95.1 15.6 %all-to-all-start.2 = ((bf16[4,16,1,1024]{3,1,2,0:T(8,128)(2,1)}), bf16[4,16,1,1024]{3,1,2,0:T(8,128)(2,1)S(1)}, u32[]{:S(2)}, u32[]{:S(2)}) async-start(bf16[4,16,1,1024]{3,1,2,0:T(8,128)(2,1)} %bitcast.48), calls=%async_computation.2 | async-start | bytes 262144 | tf_op jit(solution)/shard_map/all_to_all | solution.py:111
  98.4 178.4 %all-reduce.8.cloned.1.call-start = ((), (), s32[]{:S(2)}) async-start(), calls=%async_computation.4 | async-start | bytes 8388608 | tf_op jit(solution)/shard_map/psum | solution.py:18
  111.0 12.5 %copy-start.12 = (f32[2,4,8]{2,1,0:T(4,128)S(1)}, f32[2,4,8]{2,1,0:T(4,128)}, u32[]{:S(2)}) copy-start(f32[2,4,8]{2,1,0:T(4,128)} %param.43) | copy-start | bytes 772
  297.9 24.2 %all-to-all-start.1 = ((f32[4,1,16384]{2,1,0:T(1,128)}), f32[4,1,16384]{2,1,0:T(1,128)S(1)}, u32[]{:S(2)}, u32[]{:S(2)}) async-start(f32[4,1,16384]{2,1,0:T(1,128)} %reshape.872), calls=%async_computation.1 | async-start | bytes 524288 | tf_op jit(solution)/shard_map/all_to_all | solution.py:22
  322.1 9.9 %all-to-all-start.3 = ((f32[4,1,16384]{2,1,0:T(1,128)}), f32[4,1,16384]{2,1,0:T(1,128)S(1)}, u32[]{:S(2)}, u32[]{:S(2)}) async-start(f32[4,1,16384]{2,1,0:T(1,128)} %reshape.870), calls=%async_computation.3 | async-start | bytes 524288 | tf_op jit(solution)/shard_map/all_to_all | solution.py:22
Sparse Core Ops, SparseCore 0:
  123.0 153.8 all-reduce.7
where the time goes:
time: 347 us; the launch traced here: 346 us
  waiting for transfers between devices  157 us (45%)
  other arithmetic  47 us (14%)
  blocking collectives  44.6 us (13%)
  local copies, waits for them, and re-layouts  38.1 us (11%)
  matrix products  30.6 us (9%)
  between operations  14.6 us (4%)
  starting transfers between devices  13.9 us (4%)
    psum x1, waiting for transfers between devices, sum_heads(): return lax.psum(values, 'tensor')  153 us
    unnamed x2, other arithmetic  38.1 us
    unnamed x49, local copies, waits for them, and re-layouts  24.5 us
    psum x1, blocking collectives, sum_heads(): return lax.psum(values, 'tensor')  19.3 us
    dot_general x2, matrix products, mixture(): jnp.einsum('ecsh,ehd->ecsd', hidden, expert_down, preferred_element_type=...  16.1 us
    unnamed x1, blocking collectives  15 us
    all_gather x2, blocking collectives, mamba_step(): lax.all_gather(normed, 'expert', axis=0, tiled=True)  10.4 us
    reshape x4, local copies, waits for them, and re-layouts, mixture(): partial_out.reshape(1, local_experts * capacity, steps_here, width_all)  7.59 us
  transfers between devices with their start and end apart: 5, of which 2 were waited for; matrix products, arithmetic and copies ran while one was open for 12% of the time, Pallas kernels for 0%

commit v1 on v0

v1 whole, which is shorter than its diff:
```python
import jax
import jax.numpy as jnp
from jax import lax
from jax.sharding import PartitionSpec as P


def silu_float(values):
    return values / (1.0 + jnp.exp(-values))


def pairwise(axis):
    size = lax.axis_size(axis)
    return size <= 4 and size & (size - 1) == 0


def swap(values, axis, distance):
    size = lax.axis_size(axis)
    return lax.ppermute(values, axis, [(i, i ^ distance) for i in range(size)])


def gather(values, axis):
    size = lax.axis_size(axis)
    if not pairwise(axis):
        return lax.all_gather(values, axis, axis=0)
    held = [values] + [swap(values, axis, d) for d in range(1, size)]
    me = lax.axis_index(axis)
    bit = 1
    while bit < size:
        flip = (me & bit) != 0
        held = [jnp.where(flip, held[i ^ bit], held[i]) for i in range(size)]
        bit *= 2
    return jnp.stack(held)


def scatter_sum(blocks, axis):
    size = lax.axis_size(axis)
    if not pairwise(axis):
        return lax.psum_scatter(blocks, axis, scatter_dimension=0, tiled=False)
    me = lax.axis_index(axis)
    total = lax.dynamic_index_in_dim(blocks, me, 0, keepdims=False)
    sent = [
        swap(lax.dynamic_index_in_dim(blocks, me ^ d, 0, keepdims=False), axis, d)
        for d in range(1, size)
    ]
    for part in sent:
        total = total + part
    return total


def sum_over(values, axis):
    if not pairwise(axis):
        return lax.psum(values, axis)
    sent = [swap(values, axis, d) for d in range(1, lax.axis_size(axis))]
    total = values
    for part in sent:
        total = total + part
    return total


def convolve(window_state, newest, kernel):
    taps = kernel.shape[0]
    steps = newest.shape[1]
    window = jnp.concatenate([window_state, newest], axis=1)
    wide = window.astype(jnp.float32)
    acts = []
    for s in range(steps):
        acts.append(silu_float(jnp.sum(wide[:, s : s + taps] * kernel[None], axis=1)))
    return acts, window[:, steps:]


def per_device(
    tokens,
    proj_gate,
    proj_input,
    proj_write,
    proj_read,
    proj_step,
    conv_input,
    conv_write,
    conv_read,
    window_input,
    window_write,
    window_read,
    step_bias,
    decay_log,
    skip_gain,
    norm_gain,
    ssm_state,
    out_proj,
    expert_up,
    expert_down,
    expert_ids,
    route_gates,
):
    steps, rows, features = tokens.shape
    owners = lax.axis_size("expert")
    own_rows, heads, head_dim, state_size = ssm_state.shape
    inner = conv_input.shape[1]
    write_width = conv_write.shape[1]
    groups = write_width // state_size
    heads_group = heads // groups
    local_experts = expert_up.shape[0]
    many = rows * steps

    current = tokens.transpose(1, 0, 2).reshape(many, features)
    projected = jnp.concatenate(
        [
            jnp.dot(current, w, preferred_element_type=jnp.float32)
            for w in (proj_gate, proj_input, proj_write, proj_read, proj_step)
        ],
        axis=1,
    )
    projected = scatter_sum(projected.reshape(owners, own_rows, steps, -1), "expert")
    projected = projected.astype(jnp.bfloat16)
    edges = (inner, 2 * inner, 2 * inner + write_width, 2 * inner + 2 * write_width)
    gate_pre, input_pre, write_pre, read_pre, step_pre = jnp.split(projected, edges, axis=2)
    input_acts, input_final = convolve(window_input, input_pre, conv_input)
    write_acts, write_final = convolve(window_write, write_pre, conv_write)
    read_acts, read_final = convolve(window_read, read_pre, conv_read)

    state = ssm_state.reshape(own_rows, groups, heads_group, head_dim, state_size)
    normed = []
    for s in range(steps):
        step_size = jax.nn.softplus(step_pre[:, s].astype(jnp.float32) + step_bias[None, :])
        decay_rate = jnp.exp(-step_size * jnp.exp(decay_log)[None, :])
        heads_input = input_acts[s].reshape(own_rows, groups, heads_group, head_dim)
        write_grouped = write_acts[s].reshape(own_rows, groups, 1, 1, state_size)
        read_grouped = read_acts[s].reshape(own_rows, groups, 1, 1, state_size)
        state = (
            decay_rate.reshape(own_rows, groups, heads_group, 1, 1) * state
            + step_size.reshape(own_rows, groups, heads_group, 1, 1)
            * heads_input[..., None]
            * write_grouped
        )
        ssm_read = (
            jnp.sum(state * read_grouped, axis=-1)
            + skip_gain.reshape(groups, heads_group, 1) * heads_input
        )
        gated = ssm_read.reshape(own_rows, groups, -1) * silu_float(
            gate_pre[:, s].astype(jnp.float32)
        ).reshape(own_rows, groups, -1)
        scaled = (
            gated
            * lax.rsqrt(jnp.mean(gated * gated, axis=-1, keepdims=True) + 1e-05)
            * norm_gain.reshape(groups, -1)
        )
        normed.append(scaled.reshape(own_rows, inner).astype(jnp.bfloat16))
    ssm_final = state.reshape(ssm_state.shape)

    normed = gather(jnp.stack(normed, axis=1), "expert").reshape(many, inner)
    partial = jnp.dot(normed, out_proj, preferred_element_type=jnp.float32)
    residual = current.astype(jnp.float32) + sum_over(partial, "tensor")
    moe_in = gather(residual.astype(jnp.bfloat16), "expert")
    moe_in = moe_in.transpose(1, 0, 2).reshape(many, owners * features)

    first = lax.axis_index("expert") * local_experts
    chosen = expert_ids.transpose(1, 0, 2).reshape(many, -1)
    weights = route_gates.transpose(1, 0, 2).reshape(many, -1)
    moe_sum = jnp.zeros((many, owners * features), jnp.float32)
    for e in range(local_experts):
        hidden = jnp.dot(moe_in, expert_up[e], preferred_element_type=jnp.float32)
        hidden = jnp.maximum(hidden, 0.0)
        hidden = (hidden * hidden).astype(jnp.bfloat16)
        expert_out = jnp.dot(hidden, expert_down[e], preferred_element_type=jnp.float32)
        row_weight = jnp.sum(jnp.where(chosen == first + e, weights, 0.0), axis=1)
        moe_sum = moe_sum + row_weight[:, None] * expert_out
    blocks = moe_sum.reshape(many, owners, features).transpose(1, 0, 2)
    moe_sum = sum_over(scatter_sum(blocks, "expert"), "tensor")
    mixed = (residual + moe_sum).astype(jnp.bfloat16)
    mixed_out = mixed.reshape(rows, steps, features).transpose(1, 0, 2)
    return (mixed_out, ssm_final, input_final, write_final, read_final)


def solution(mesh):
    placed = (
        P(None, "groups", "expert"),
        P("expert", "tensor"),
        P("expert", "tensor"),
        P("expert", "tensor"),
        P("expert", "tensor"),
        P("expert", "tensor"),
        P(None, "tensor"),
        P(None, "tensor"),
        P(None, "tensor"),
        P(("groups", "expert"), None, "tensor"),
        P(("groups", "expert"), None, "tensor"),
        P(("groups", "expert"), None, "tensor"),
        P("tensor"),
        P("tensor"),
        P("tensor"),
        P("tensor"),
        P(("groups", "expert"), "tensor", None, None),
        P("tensor", "expert"),
        P("expert", None, "tensor"),
        P("expert", "tensor", None),
        P(None, "groups", None),
        P(None, "groups", None),
    )
    return jax.shard_map(
        per_device,
        mesh=mesh,
        in_specs=placed,
        out_specs=(
            P(None, "groups", "expert"),
            P(("groups", "expert"), "tensor", None, None),
            P(("groups", "expert"), None, "tensor"),
            P(("groups", "expert"), None, "tensor"),
            P(("groups", "expert"), None, "tensor"),
        ),
        check_vma=False,
    )
```

time: 347 us -> 62.9 us (0.18)
  waiting for transfers between devices: 157 us -> 14.5 us
  blocking collectives: 44.6 us -> 0 us
  other arithmetic: 47 us -> 4.51 us
  local copies, waits for them, and re-layouts: 38.1 us -> 3.81 us
  between operations: 14.6 us -> 1.08 us
  matrix products: 30.6 us -> 21 us
  starting transfers between devices: 13.9 us -> 17.7 us
    psum x1 -> x0, waiting for transfers between devices: 153 us -> none  [sum_heads(): return lax.psum(values, 'tensor')]
    unnamed x2 -> x0, other arithmetic: 38.1 us -> none
    unnamed x49 -> x34, local copies, waits for them, and re-layouts: 24.5 us -> 0.51 us
    psum x1 -> x0, blocking collectives: 19.3 us -> none  [sum_heads(): return lax.psum(values, 'tensor')]
    ppermute x0 -> x18, starting transfers between devices: none -> 17.7 us  [swap(): return lax.ppermute(values, axis, [(i, i ^ distance) for i in range(size)])]
    unnamed x1 -> x0, blocking collectives: 15 us -> none
    ppermute x0 -> x18, waiting for transfers between devices: none -> 14.5 us  [swap(): return lax.ppermute(values, axis, [(i, i ^ distance) for i in range(size)])]
    all_to_all x4 -> x0, starting transfers between devices: 13.7 us -> none  [the longest x2 7.03 us: send_back(): lax.all_to_all(values, 'expert', split_axis=3, concat_axis=0, tiled=True)]
  transfers between devices with their start and end apart: 5 -> 18, of which waited for: 2 -> 13; matrix products, arithmetic and copies ran while one was open for 12% -> 4% of each run, Pallas kernels for 0% -> 0%
where the time goes in v1:
time: 62.9 us; the launch traced here: 62.6 us
  matrix products  21 us (33%)
  starting transfers between devices  17.7 us (28%)
  waiting for transfers between devices  14.5 us (23%)
  other arithmetic  4.51 us (7%)
  local copies, waits for them, and re-layouts  3.81 us (6%)
  between operations  1.08 us (2%)
    ppermute x18, starting transfers between devices, swap(): return lax.ppermute(values, axis, [(i, i ^ distance) for i in range(size)])  17.7 us
    ppermute x18, waiting for transfers between devices, swap(): return lax.ppermute(values, axis, [(i, i ^ distance) for i in range(size)])  14.5 us
    dot_general x4, matrix products, per_device(): jnp.dot(hidden, expert_down[e], preferred_element_type=jnp.float32)  14 us
    dot_general x5, matrix products, per_device(): jnp.dot(current, w, preferred_element_type=jnp.float32)  4.14 us
    dot_general x1, matrix products, per_device(): partial = jnp.dot(normed, out_proj, preferred_element_type=jnp.float32)  2.84 us
    reduce_sum x1, other arithmetic, per_device(): jnp.sum(state * read_grouped, axis=-1)  2.17 us
  transfers between devices with their start and end apart: 18, of which 13 were waited for; matrix products, arithmetic and copies ran while one was open for 4% of the time, Pallas kernels for 0%

profile of v1, /device:TPU:0, one launch (start us, length us, event | category | flops | bytes accessed | tf_op | source)
XLA Modules:
  0.0 62.6 jit_solution(18022563158517228152)
XLA Ops:
  0.7 0.8 %copy.31 = bf16[4,2,1024]{2,1,0:T(2,128)(2,1)S(1)} copy(bf16[4,2,1024]{2,0,1:T(4,128)(2,1)} %bitcast.213) | data formatting | bytes 32768 | tf_op jit(solution)/shard_map/transpose | solution.py:105
  1.5 3.0 %convolution_dynamic-update-slice_fusion.1 = f32[8,4640]{1,0:T(8,128)S(1)} fusion(bf16[8,1024]{1,0:T(8,128)(2,1)S(1)} %reshape.584, bf16[1024,2048]{1,0:T(8,128)(2,1)} %param.23), kind=kOutput, calls=%fused_computation.8 | convolution fusion | flops 33554432 | bytes 4276224 | tf_op jit(solution)/shard_map/dot_general | solution.py:108
  5.0 0.7 %convolution_dynamic-update-slice_fusion = f32[8,4640]{1,0:T(8,128)S(1)} fusion(f32[8,4640]{1,0:T(8,128)S(1)} %convolution_dynamic-update-slice_fusion.1, bf16[8,1024]{1,0:T(8,128)(2,1)S(1)} %reshape.584, bf16[1024,2048]{1,0:T(8,128)(2,1)S(1)} %copy-done.1), kind=kOutput, calls=%fused_computation.7 | convolution fusion | flops 33554432 | bytes 4276224 | tf_op jit(solution)/shard_map/dot_general | solution.py:108
  6.3 2.4 %collective-permute-start.2 = (f32[1,2,4640]{2,1,0:T(2,128)S(1)}, f32[1,2,4640]{2,1,0:T(2,128)S(1)}, u32[]{:S(2)}, u32[]{:S(2)}) collective-permute-start(f32[1,2,4640]{2,1,0:T(2,128)S(1)} %get-tuple-element.29), channel_id=1, source_target_pairs={{0,12},{4,8},{8,4},{12,0},{1,13},{5,9},{9,5},{13,1},{2,14},{6,10},... | collective-permute-start | bytes 111368 | tf_op jit(solution)/shard_map/ppermute | solution.py:18
  8.8 0.6 %collective-permute-start.1 = (f32[1,2,4640]{2,1,0:T(2,128)S(1)}, f32[1,2,4640]{2,1,0:T(2,128)S(1)}, u32[]{:S(2)}, u32[]{:S(2)}) collective-permute-start(f32[1,2,4640]{2,1,0:T(2,128)S(1)} %get-tuple-element.30), channel_id=1, source_target_pairs={{0,8},{4,12},{8,0},{12,4},{1,9},{5,13},{9,1},{13,5},{2,10},{6,14},... | collective-permute-start | bytes 111368 | tf_op jit(solution)/shard_map/ppermute | solution.py:18
  9.7 1.0 %collective-permute-done.2 = f32[1,2,4640]{2,1,0:T(2,128)S(1)} collective-permute-done((f32[1,2,4640]{2,1,0:T(2,128)S(1)}, f32[1,2,4640]{2,1,0:T(2,128)S(1)}, u32[]{:S(2)}, u32[]{:S(2)}) %collective-permute-start.2) | collective-permute-done | bytes 37152 | tf_op jit(solution)/shard_map/ppermute | solution.py:18
  10.7 2.2 %collective-permute-done.1 = f32[1,2,4640]{2,1,0:T(2,128)S(1)} collective-permute-done((f32[1,2,4640]{2,1,0:T(2,128)S(1)}, f32[1,2,4640]{2,1,0:T(2,128)S(1)}, u32[]{:S(2)}, u32[]{:S(2)}) %collective-permute-start.1) | collective-permute-done | bytes 37152 | tf_op jit(solution)/shard_map/ppermute | solution.py:18
  13.7 2.2 %multiply_reduce_fusion = (f32[32,64]{1,0:T(8,128)S(1)}, f32[1,32,64,128]{3,2,1,0:T(8,128)}, f32[32,64]{1,0:T(8,128)S(1)}) fusion(f32[32,128]{1,0:T(8,128)S(1)} %bitcast.205, f32[32,128]{1,0:T(8,128)S(1)} %bitcast.206, f32[32,64]{1,0:T(8,128)S(1)} %get-tuple-element.54, f32[32,128]{1,0:T(8,128)S(1)} %bitcast.207, f32[32,64]{1,0:T(8,128)S(1)} %get-tuple-element.55, ...), kind=kLoop, calls=%fused_computation.44 | loop fusion | flops 2617344 | bytes 2195712 | tf_op jit(solution)/shard_map/reduce_sum | solution.py:136
  16.9 0.9 %collective-permute-start.3 = (bf16[1,2,2048]{2,1,0:T(2,128)(2,1)S(1)}, bf16[1,2,2048]{2,1,0:T(2,128)(2,1)S(1)}, u32[]{:S(2)}, u32[]{:S(2)}) collective-permute-start(bf16[1,2,2048]{2,1,0:T(2,128)(2,1)S(1)} %pad_maximum_fusion.3), channel_id=1, source_target_pairs={{0,12},{4,8},{8,4},{12,0},{1,13},{5,9},{9,5},{13,1},{2,14},{6,10},... | collective-permute-start | bytes 24584 | tf_op jit(solution)/shard_map/ppermute | solution.py:18
  17.7 0.7 %collective-permute-start.4 = (bf16[1,2,2048]{2,1,0:T(2,128)(2,1)S(1)}, bf16[1,2,2048]{2,1,0:T(2,128)(2,1)S(1)}, u32[]{:S(2)}, u32[]{:S(2)}) collective-permute-start(bf16[1,2,2048]{2,1,0:T(2,128)(2,1)S(1)} %pad_maximum_fusion.3), channel_id=1, source_target_pairs={{0,8},{4,12},{8,0},{12,4},{1,9},{5,13},{9,1},{13,5},{2,10},{6,14},... | collective-permute-start | bytes 24584 | tf_op jit(solution)/shard_map/ppermute | solution.py:18
  18.8 1.3 %collective-permute-done.3 = bf16[1,2,2048]{2,1,0:T(2,128)(2,1)S(1)} collective-permute-done((bf16[1,2,2048]{2,1,0:T(2,128)(2,1)S(1)}, bf16[1,2,2048]{2,1,0:T(2,128)(2,1)S(1)}, u32[]{:S(2)}, u32[]{:S(2)}) %collective-permute-start.3) | collective-permute-done | bytes 8224 | tf_op jit(solution)/shard_map/ppermute | solution.py:18
  20.1 1.3 %collective-permute-done.4 = bf16[1,2,2048]{2,1,0:T(2,128)(2,1)S(1)} collective-permute-done((bf16[1,2,2048]{2,1,0:T(2,128)(2,1)S(1)}, bf16[1,2,2048]{2,1,0:T(2,128)(2,1)S(1)}, u32[]{:S(2)}, u32[]{:S(2)}) %collective-permute-start.4) | collective-permute-done | bytes 8224 | tf_op jit(solution)/shard_map/ppermute | solution.py:18
  21.5 2.8 %fusion.112 = f32[8,1024]{1,0:T(8,128)S(1)} fusion(bf16[8,2048]{1,0:T(8,128)(2,1)S(1)} %reshape.586, bf16[2048,1024]{1,0:T(8,128)(2,1)} %param.39), kind=kOutput, calls=%fused_computation.168 | convolution fusion | flops 33554432 | bytes 4259840 | tf_op jit(solution)/shard_map/dot_general | solution.py:151
  24.4 3.6 %collective-permute-start.8 = (f32[8,1024]{1,0:T(8,128)S(1)}, f32[8,1024]{1,0:T(8,128)S(1)}, u32[]{:S(2)}, u32[]{:S(2)}) collective-permute-start(f32[8,1024]{1,0:T(8,128)S(1)} %fusion.112), channel_id=1, source_target_pairs={{0,3},{1,2},{2,1},{3,0},{4,7},{5,6},{6,5},{7,4},{8,11},{9,10},{10,... | collective-permute-start | bytes 98312 | tf_op jit(solution)/shard_map/ppermute | solution.py:18
  28.0 0.8 %collective-permute-start.6 = (f32[8,1024]{1,0:T(8,128)S(1)}, f32[8,1024]{1,0:T(8,128)S(1)}, u32[]{:S(2)}, u32[]{:S(2)}) collective-permute-start(f32[8,1024]{1,0:T(8,128)S(1)} %fusion.112), channel_id=1, source_target_pairs={{0,1},{1,0},{2,3},{3,2},{4,5},{5,4},{6,7},{7,6},{8,9},{9,8},{10,11... | collective-permute-start | bytes 98312 | tf_op jit(solution)/shard_map/ppermute | solution.py:18
  28.8 1.5 %collective-permute-done.8 = f32[8,1024]{1,0:T(8,128)S(1)} collective-permute-done((f32[8,1024]{1,0:T(8,128)S(1)}, f32[8,1024]{1,0:T(8,128)S(1)}, u32[]{:S(2)}, u32[]{:S(2)}) %collective-permute-start.8) | collective-permute-done | bytes 32800 | tf_op jit(solution)/shard_map/ppermute | solution.py:18
  30.3 2.5 %collective-permute-done.7 = f32[8,1024]{1,0:T(8,128)S(1)} collective-permute-done((f32[8,1024]{1,0:T(8,128)S(1)}, f32[8,1024]{1,0:T(8,128)S(1)}, u32[]{:S(2)}, u32[]{:S(2)}) %collective-permute-start.7) | collective-permute-done | bytes 32800 | tf_op jit(solution)/shard_map/ppermute | solution.py:18
  32.9 0.7 %collective-permute-start.10 = (bf16[8,1024]{1,0:T(8,128)(2,1)S(1)}, bf16[8,1024]{1,0:T(8,128)(2,1)S(1)}, u32[]{:S(2)}, u32[]{:S(2)}) collective-permute-start(bf16[8,1024]{1,0:T(8,128)(2,1)S(1)} %get-tuple-element.19), channel_id=1, source_target_pairs={{0,8},{4,12},{8,0},{12,4},{1,9},{5,13},{9,1},{13,5},{2,10},{6,14},... | collective-permute-start | bytes 49160 | tf_op jit(solution)/shard_map/ppermute | solution.py:18
  33.6 1.1 %collective-permute-start.11 = (bf16[8,1024]{1,0:T(8,128)(2,1)S(1)}, bf16[8,1024]{1,0:T(8,128)(2,1)S(1)}, u32[]{:S(2)}, u32[]{:S(2)}) collective-permute-start(bf16[8,1024]{1,0:T(8,128)(2,1)S(1)} %get-tuple-element.19), channel_id=1, source_target_pairs={{0,4},{4,0},{8,12},{12,8},{1,5},{5,1},{9,13},{13,9},{2,6},{6,2},{1... | collective-permute-start | bytes 49160 | tf_op jit(solution)/shard_map/ppermute | solution.py:18
  36.1 0.7 %collective-permute-done.10 = bf16[8,1024]{1,0:T(8,128)(2,1)S(1)} collective-permute-done((bf16[8,1024]{1,0:T(8,128)(2,1)S(1)}, bf16[8,1024]{1,0:T(8,128)(2,1)S(1)}, u32[]{:S(2)}, u32[]{:S(2)}) %collective-permute-start.10) | collective-permute-done | bytes 16416 | tf_op jit(solution)/shard_map/ppermute | solution.py:18
  36.8 3.5 %convolution_multiply_fusion.3 = f32[8,4096]{1,0:T(8,128)S(1)} fusion(bf16[4,256,4096]{2,1,0:T(8,128)(2,1)} %param.41, bf16[8,4096]{1,0:T(8,128)(2,1)S(1)} %bitcast.199, bf16[4,4096,256]{2,1,0:T(8,128)(2,1)} %param.40, f32[8]{0:T(128)S(1)} %mul.406), kind=kOutput, calls=%fused_computation.6 | convolution fusion | flops 33593344 | bytes 4390944 | tf_op jit(solution)/shard_map/dot_general | solution.py:164
  40.2 3.5 %fusion.2 = f32[8,4096]{1,0:T(8,128)S(1)} fusion(f32[8,4096]{1,0:T(8,128)S(1)} %convolution_multiply_fusion.3, bf16[4,256,4096]{2,1,0:T(8,128)(2,1)} %param.41, bf16[8,4096]{1,0:T(8,128)(2,1)S(1)} %bitcast.200, bf16[4,4096,256]{2,1,0:T(8,128)(2,1)} %param.40, f32[8]{0:T(128)S(1)} %mul.410), kind=kOutput, calls=%fused_computation.5 | convolution fusion | flops 33626112 | bytes 4522016 | tf_op jit(solution)/shard_map/dot_general | solution.py:164
  43.7 3.5 %fusion.1 = f32[8,4096]{1,0:T(8,128)S(1)} fusion(f32[8,4096]{1,0:T(8,128)S(1)} %fusion.2, bf16[4,256,4096]{2,1,0:T(8,128)(2,1)} %param.41, bf16[8,4096]{1,0:T(8,128)(2,1)S(1)} %bitcast.201, bf16[4,4096,256]{2,1,0:T(8,128)(2,1)} %param.40, f32[8]{0:T(128)S(1)} %mul.414), kind=kOutput, calls=%fused_computation.3 | convolution fusion | flops 33626112 | bytes 4522016 | tf_op jit(solution)/shard_map/dot_general | solution.py:164
  47.2 3.5 %fusion = f32[8,4096]{1,0:T(8,128)S(1)} fusion(f32[8,4096]{1,0:T(8,128)S(1)} %fusion.1, bf16[4,256,4096]{2,1,0:T(8,128)(2,1)} %param.41, bf16[8,4096]{1,0:T(8,128)(2,1)S(1)} %bitcast.202, bf16[4,4096,256]{2,1,0:T(8,128)(2,1)} %param.40, f32[8]{0:T(128)S(1)} %mul.418), kind=kOutput, calls=%fused_computation.1 | convolution fusion | flops 33626112 | bytes 4522016 | tf_op jit(solution)/shard_map/dot_general | solution.py:164
  51.3 0.7 %collective-permute-start.13 = (f32[8,1024]{1,0:T(8,128)S(1)}, f32[8,1024]{1,0:T(8,128)S(1)}, u32[]{:S(2)}, u32[]{:S(2)}) collective-permute-start(f32[8,1024]{1,0:T(8,128)S(1)} %get-tuple-element.33), channel_id=1, source_target_pairs={{0,8},{4,12},{8,0},{12,4},{1,9},{5,13},{9,1},{13,5},{2,10},{6,14},... | collective-permute-start | bytes 98312 | tf_op jit(solution)/shard_map/ppermute | solution.py:18
  52.0 0.7 %collective-permute-start.12 = (f32[8,1024]{1,0:T(8,128)S(1)}, f32[8,1024]{1,0:T(8,128)S(1)}, u32[]{:S(2)}, u32[]{:S(2)}) collective-permute-start(f32[8,1024]{1,0:T(8,128)S(1)} %get-tuple-element.31), channel_id=1, source_target_pairs={{0,4},{4,0},{8,12},{12,8},{1,5},{5,1},{9,13},{13,9},{2,6},{6,2},{1... | collective-permute-start | bytes 98312 | tf_op jit(solution)/shard_map/ppermute | solution.py:18
  53.3 0.9 %collective-permute-done.14 = f32[8,1024]{1,0:T(8,128)S(1)} collective-permute-done((f32[8,1024]{1,0:T(8,128)S(1)}, f32[8,1024]{1,0:T(8,128)S(1)}, u32[]{:S(2)}, u32[]{:S(2)}) %collective-permute-start.14) | collective-permute-done | bytes 32800 | tf_op jit(solution)/shard_map/ppermute | solution.py:18
  54.2 1.0 %collective-permute-done.13 = f32[8,1024]{1,0:T(8,128)S(1)} collective-permute-done((f32[8,1024]{1,0:T(8,128)S(1)}, f32[8,1024]{1,0:T(8,128)S(1)}, u32[]{:S(2)}, u32[]{:S(2)}) %collective-permute-start.13) | collective-permute-done | bytes 32800 | tf_op jit(solution)/shard_map/ppermute | solution.py:18
  55.3 1.5 %collective-permute-start.17 = (f32[8,1024]{1,0:T(8,128)S(1)}, f32[8,1024]{1,0:T(8,128)S(1)}, u32[]{:S(2)}, u32[]{:S(2)}) collective-permute-start(f32[8,1024]{1,0:T(8,128)S(1)} %fusion.74), channel_id=1, source_target_pairs={{0,3},{1,2},{2,1},{3,0},{4,7},{5,6},{6,5},{7,4},{8,11},{9,10},{10,... | collective-permute-start | bytes 98312 | tf_op jit(solution)/shard_map/ppermute | solution.py:18
  56.8 0.6 %collective-permute-start.16 = (f32[8,1024]{1,0:T(8,128)S(1)}, f32[8,1024]{1,0:T(8,128)S(1)}, u32[]{:S(2)}, u32[]{:S(2)}) collective-permute-start(f32[8,1024]{1,0:T(8,128)S(1)} %fusion.74), channel_id=1, source_target_pairs={{0,2},{1,3},{2,0},{3,1},{4,6},{5,7},{6,4},{7,5},{8,10},{9,11},{10,... | collective-permute-start | bytes 98312 | tf_op jit(solution)/shard_map/ppermute | solution.py:18
  57.5 2.3 %collective-permute-start.15 = (f32[8,1024]{1,0:T(8,128)S(1)}, f32[8,1024]{1,0:T(8,128)S(1)}, u32[]{:S(2)}, u32[]{:S(2)}) collective-permute-start(f32[8,1024]{1,0:T(8,128)S(1)} %fusion.74), channel_id=1, source_target_pairs={{0,1},{1,0},{2,3},{3,2},{4,5},{5,4},{6,7},{7,6},{8,9},{9,8},{10,11... | collective-permute-start | bytes 98312 | tf_op jit(solution)/shard_map/ppermute | solution.py:18
  60.3 0.7 %collective-permute-done.17 = f32[8,1024]{1,0:T(8,128)S(1)} collective-permute-done((f32[8,1024]{1,0:T(8,128)S(1)}, f32[8,1024]{1,0:T(8,128)S(1)}, u32[]{:S(2)}, u32[]{:S(2)}) %collective-permute-start.17) | collective-permute-done | bytes 32800 | tf_op jit(solution)/shard_map/ppermute | solution.py:18
  (117 shorter events, 8.4 us)
Async XLA Ops:
  0.6 5.0 %copy-start = (bf16[1024,256]{1,0:T(8,128)(2,1)S(1)}, bf16[1024,256]{1,0:T(8,128)(2,1)}, u32[]{:S(2)}) copy-start(bf16[1024,256]{1,0:T(8,128)(2,1)} %param.25) | copy-start | bytes 1572868
  1.5 8.0 %copy-start.14 = (f32[32]{0:T(128)S(1)}, f32[32]{0:T(128)}, u32[]{:S(2)}) copy-start(f32[32]{0:T(128)} %param.36) | copy-start | bytes 388
  4.9 8.2 %copy-start.7 = (bf16[1,3,256]{2,1,0:T(4,128)(2,1)S(1)}, bf16[1,3,256]{2,1,0:T(4,128)(2,1)}, u32[]{:S(2)}) copy-start(bf16[1,3,256]{2,1,0:T(4,128)(2,1)} %param.33) | copy-start | bytes 4612
  4.9 8.2 %copy-start.8 = (bf16[1,3,256]{2,1,0:T(4,128)(2,1)S(1)}, bf16[1,3,256]{2,1,0:T(4,128)(2,1)}, u32[]{:S(2)}) copy-start(bf16[1,3,256]{2,1,0:T(4,128)(2,1)} %param.32) | copy-start | bytes 4612
  4.9 8.2 %copy-start.10 = (f32[4,256]{1,0:T(4,128)S(1)}, f32[4,256]{1,0:T(4,128)}, u32[]{:S(2)}) copy-start(f32[4,256]{1,0:T(4,128)} %param.30) | copy-start | bytes 12292
  4.9 8.2 %copy-start.11 = (f32[4,256]{1,0:T(4,128)S(1)}, f32[4,256]{1,0:T(4,128)}, u32[]{:S(2)}) copy-start(f32[4,256]{1,0:T(4,128)} %param.29) | copy-start | bytes 12292
  4.9 8.3 %copy-start.5 = (bf16[1,3,2048]{2,1,0:T(4,128)(2,1)S(1)}, bf16[1,3,2048]{2,1,0:T(4,128)(2,1)}, u32[]{:S(2)}) copy-start(bf16[1,3,2048]{2,1,0:T(4,128)(2,1)} %param.31) | copy-start | bytes 36868
  4.9 8.3 %copy-start.6 = (f32[4,2048]{1,0:T(4,128)S(1)}, f32[4,2048]{1,0:T(4,128)}, u32[]{:S(2)}) copy-start(f32[4,2048]{1,0:T(4,128)} %param.28) | copy-start | bytes 98308
  5.0 8.6 %copy-start.15 = (f32[32]{0:T(128)S(1)}, f32[32]{0:T(128)}, u32[]{:S(2)}) copy-start(f32[32]{0:T(128)} %param.35) | copy-start | bytes 388
  5.0 8.6 %copy-start.16 = (f32[32]{0:T(128)S(1)}, f32[32]{0:T(128)}, u32[]{:S(2)}) copy-start(f32[32]{0:T(128)} %param.34) | copy-start | bytes 388
  5.0 8.7 %copy-start.2 = (f32[1,32,64,128]{3,2,1,0:T(8,128)S(1)}, f32[1,32,64,128]{3,2,1,0:T(8,128)}, u32[]{:S(2)}) copy-start(f32[1,32,64,128]{3,2,1,0:T(8,128)} %param.38) | copy-start | bytes 3145732
  5.0 11.8 %copy-start.9 = (f32[2048]{0:T(1024)S(1)}, f32[2048]{0:T(1024)}, u32[]{:S(2)}) copy-start(f32[2048]{0:T(1024)} %param.37) | copy-start | bytes 24580
  6.3 28.5 %copy-start.12 = (f32[2,4,8]{2,1,0:T(4,128)S(1)}, f32[2,4,8]{2,1,0:T(4,128)}, u32[]{:S(2)}) copy-start(f32[2,4,8]{2,1,0:T(4,128)} %param.43) | copy-start | bytes 772
  6.3 28.5 %copy-start.13 = (s32[2,4,8]{2,1,0:T(4,128)S(1)}, s32[2,4,8]{2,1,0:T(4,128)}, u32[]{:S(2)}) copy-start(s32[2,4,8]{2,1,0:T(4,128)} %param.42) | copy-start | bytes 772
  6.3 4.3 %collective-permute-start.2 = (f32[1,2,4640]{2,1,0:T(2,128)S(1)}, f32[1,2,4640]{2,1,0:T(2,128)S(1)}, u32[]{:S(2)}, u32[]{:S(2)}) collective-permute-start(f32[1,2,4640]{2,1,0:T(2,128)S(1)} %get-tuple-element.29), channel_id=1, source_target_pairs={{0,12},{4,8},{8,4},{12,0},{1,13},{5,9},{9,5},{13,1},{2,14},{6,10},... | collective-permute-start | bytes 111368 | tf_op jit(solution)/shard_map/ppermute | solution.py:18
  8.8 4.1 %collective-permute-start.1 = (f32[1,2,4640]{2,1,0:T(2,128)S(1)}, f32[1,2,4640]{2,1,0:T(2,128)S(1)}, u32[]{:S(2)}, u32[]{:S(2)}) collective-permute-start(f32[1,2,4640]{2,1,0:T(2,128)S(1)} %get-tuple-element.30), channel_id=1, source_target_pairs={{0,8},{4,12},{8,0},{12,4},{1,9},{5,13},{9,1},{13,5},{2,10},{6,14},... | collective-permute-start | bytes 111368 | tf_op jit(solution)/shard_map/ppermute | solution.py:18
  9.4 3.4 %collective-permute-start = (f32[1,2,4640]{2,1,0:T(2,128)S(1)}, f32[1,2,4640]{2,1,0:T(2,128)S(1)}, u32[]{:S(2)}, u32[]{:S(2)}) collective-permute-start(f32[1,2,4640]{2,1,0:T(2,128)S(1)} %get-tuple-element.28), channel_id=1, source_target_pairs={{0,4},{4,0},{8,12},{12,8},{1,5},{5,1},{9,13},{13,9},{2,6},{6,2},{1... | collective-permute-start | bytes 111368 | tf_op jit(solution)/shard_map/ppermute | solution.py:18
  16.9 3.2 %collective-permute-start.3 = (bf16[1,2,2048]{2,1,0:T(2,128)(2,1)S(1)}, bf16[1,2,2048]{2,1,0:T(2,128)(2,1)S(1)}, u32[]{:S(2)}, u32[]{:S(2)}) collective-permute-start(bf16[1,2,2048]{2,1,0:T(2,128)(2,1)S(1)} %pad_maximum_fusion.3), channel_id=1, source_target_pairs={{0,12},{4,8},{8,4},{12,0},{1,13},{5,9},{9,5},{13,1},{2,14},{6,10},... | collective-permute-start | bytes 24584 | tf_op jit(solution)/shard_map/ppermute | solution.py:18
  17.7 3.7 %collective-permute-start.4 = (bf16[1,2,2048]{2,1,0:T(2,128)(2,1)S(1)}, bf16[1,2,2048]{2,1,0:T(2,128)(2,1)S(1)}, u32[]{:S(2)}, u32[]{:S(2)}) collective-permute-start(bf16[1,2,2048]{2,1,0:T(2,128)(2,1)S(1)} %pad_maximum_fusion.3), channel_id=1, source_target_pairs={{0,8},{4,12},{8,0},{12,4},{1,9},{5,13},{9,1},{13,5},{2,10},{6,14},... | collective-permute-start | bytes 24584 | tf_op jit(solution)/shard_map/ppermute | solution.py:18
  18.4 3.0 %collective-permute-start.5 = (bf16[1,2,2048]{2,1,0:T(2,128)(2,1)S(1)}, bf16[1,2,2048]{2,1,0:T(2,128)(2,1)S(1)}, u32[]{:S(2)}, u32[]{:S(2)}) collective-permute-start(bf16[1,2,2048]{2,1,0:T(2,128)(2,1)S(1)} %pad_maximum_fusion.3), channel_id=1, source_target_pairs={{0,4},{4,0},{8,12},{12,8},{1,5},{5,1},{9,13},{13,9},{2,6},{6,2},{1... | collective-permute-start | bytes 24584 | tf_op jit(solution)/shard_map/ppermute | solution.py:18
  24.4 5.9 %collective-permute-start.8 = (f32[8,1024]{1,0:T(8,128)S(1)}, f32[8,1024]{1,0:T(8,128)S(1)}, u32[]{:S(2)}, u32[]{:S(2)}) collective-permute-start(f32[8,1024]{1,0:T(8,128)S(1)} %fusion.112), channel_id=1, source_target_pairs={{0,3},{1,2},{2,1},{3,0},{4,7},{5,6},{6,5},{7,4},{8,11},{9,10},{10,... | collective-permute-start | bytes 98312 | tf_op jit(solution)/shard_map/ppermute | solution.py:18
  28.0 4.8 %collective-permute-start.7 = (f32[8,1024]{1,0:T(8,128)S(1)}, f32[8,1024]{1,0:T(8,128)S(1)}, u32[]{:S(2)}, u32[]{:S(2)}) collective-permute-start(f32[8,1024]{1,0:T(8,128)S(1)} %fusion.112), channel_id=1, source_target_pairs={{0,2},{1,3},{2,0},{3,1},{4,6},{5,7},{6,4},{7,5},{8,10},{9,11},{10,... | collective-permute-start | bytes 98312 | tf_op jit(solution)/shard_map/ppermute | solution.py:18
  28.0 4.8 %collective-permute-start.6 = (f32[8,1024]{1,0:T(8,128)S(1)}, f32[8,1024]{1,0:T(8,128)S(1)}, u32[]{:S(2)}, u32[]{:S(2)}) collective-permute-start(f32[8,1024]{1,0:T(8,128)S(1)} %fusion.112), channel_id=1, source_target_pairs={{0,1},{1,0},{2,3},{3,2},{4,5},{5,4},{6,7},{7,6},{8,9},{9,8},{10,11... | collective-permute-start | bytes 98312 | tf_op jit(solution)/shard_map/ppermute | solution.py:18
  32.8 3.2 %collective-permute-start.9 = (bf16[8,1024]{1,0:T(8,128)(2,1)S(1)}, bf16[8,1024]{1,0:T(8,128)(2,1)S(1)}, u32[]{:S(2)}, u32[]{:S(2)}) collective-permute-start(bf16[8,1024]{1,0:T(8,128)(2,1)S(1)} %get-tuple-element.19), channel_id=1, source_target_pairs={{0,12},{4,8},{8,4},{12,0},{1,13},{5,9},{9,5},{13,1},{2,14},{6,10},... | collective-permute-start | bytes 49160 | tf_op jit(solution)/shard_map/ppermute | solution.py:18
  32.9 3.8 %collective-permute-start.10 = (bf16[8,1024]{1,0:T(8,128)(2,1)S(1)}, bf16[8,1024]{1,0:T(8,128)(2,1)S(1)}, u32[]{:S(2)}, u32[]{:S(2)}) collective-permute-start(bf16[8,1024]{1,0:T(8,128)(2,1)S(1)} %get-tuple-element.19), channel_id=1, source_target_pairs={{0,8},{4,12},{8,0},{12,4},{1,9},{5,13},{9,1},{13,5},{2,10},{6,14},... | collective-permute-start | bytes 49160 | tf_op jit(solution)/shard_map/ppermute | solution.py:18
  33.6 3.1 %collective-permute-start.11 = (bf16[8,1024]{1,0:T(8,128)(2,1)S(1)}, bf16[8,1024]{1,0:T(8,128)(2,1)S(1)}, u32[]{:S(2)}, u32[]{:S(2)}) collective-permute-start(bf16[8,1024]{1,0:T(8,128)(2,1)S(1)} %get-tuple-element.19), channel_id=1, source_target_pairs={{0,4},{4,0},{8,12},{12,8},{1,5},{5,1},{9,13},{13,9},{2,6},{6,2},{1... | collective-permute-start | bytes 49160 | tf_op jit(solution)/shard_map/ppermute | solution.py:18
  50.8 3.5 %collective-permute-start.14 = (f32[8,1024]{1,0:T(8,128)S(1)}, f32[8,1024]{1,0:T(8,128)S(1)}, u32[]{:S(2)}, u32[]{:S(2)}) collective-permute-start(f32[8,1024]{1,0:T(8,128)S(1)} %get-tuple-element.32), channel_id=1, source_target_pairs={{0,12},{4,8},{8,4},{12,0},{1,13},{5,9},{9,5},{13,1},{2,14},{6,10},... | collective-permute-start | bytes 98312 | tf_op jit(solution)/shard_map/ppermute | solution.py:18
  51.3 3.9 %collective-permute-start.13 = (f32[8,1024]{1,0:T(8,128)S(1)}, f32[8,1024]{1,0:T(8,128)S(1)}, u32[]{:S(2)}, u32[]{:S(2)}) collective-permute-start(f32[8,1024]{1,0:T(8,128)S(1)} %get-tuple-element.33), channel_id=1, source_target_pairs={{0,8},{4,12},{8,0},{12,4},{1,9},{5,13},{9,1},{13,5},{2,10},{6,14},... | collective-permute-start | bytes 98312 | tf_op jit(solution)/shard_map/ppermute | solution.py:18
  52.0 3.3 %collective-permute-start.12 = (f32[8,1024]{1,0:T(8,128)S(1)}, f32[8,1024]{1,0:T(8,128)S(1)}, u32[]{:S(2)}, u32[]{:S(2)}) collective-permute-start(f32[8,1024]{1,0:T(8,128)S(1)} %get-tuple-element.31), channel_id=1, source_target_pairs={{0,4},{4,0},{8,12},{12,8},{1,5},{5,1},{9,13},{13,9},{2,6},{6,2},{1... | collective-permute-start | bytes 98312 | tf_op jit(solution)/shard_map/ppermute | solution.py:18
  55.3 5.8 %collective-permute-start.17 = (f32[8,1024]{1,0:T(8,128)S(1)}, f32[8,1024]{1,0:T(8,128)S(1)}, u32[]{:S(2)}, u32[]{:S(2)}) collective-permute-start(f32[8,1024]{1,0:T(8,128)S(1)} %fusion.74), channel_id=1, source_target_pairs={{0,3},{1,2},{2,1},{3,0},{4,7},{5,6},{6,5},{7,4},{8,11},{9,10},{10,... | collective-permute-start | bytes 98312 | tf_op jit(solution)/shard_map/ppermute | solution.py:18
  56.8 4.9 %collective-permute-start.16 = (f32[8,1024]{1,0:T(8,128)S(1)}, f32[8,1024]{1,0:T(8,128)S(1)}, u32[]{:S(2)}, u32[]{:S(2)}) collective-permute-start(f32[8,1024]{1,0:T(8,128)S(1)} %fusion.74), channel_id=1, source_target_pairs={{0,2},{1,3},{2,0},{3,1},{4,6},{5,7},{6,4},{7,5},{8,10},{9,11},{10,... | collective-permute-start | bytes 98312 | tf_op jit(solution)/shard_map/ppermute | solution.py:18
  57.5 4.5 %collective-permute-start.15 = (f32[8,1024]{1,0:T(8,128)S(1)}, f32[8,1024]{1,0:T(8,128)S(1)}, u32[]{:S(2)}, u32[]{:S(2)}) collective-permute-start(f32[8,1024]{1,0:T(8,128)S(1)} %fusion.74), channel_id=1, source_target_pairs={{0,1},{1,0},{2,3},{3,2},{4,5},{5,4},{6,7},{7,6},{8,9},{9,8},{10,11... | collective-permute-start | bytes 98312 | tf_op jit(solution)/shard_map/ppermute | solution.py:18
  (3 other events, 12.4 us)

commit v2 on v1

--- a/solution.py
+++ b/solution.py
@@ -1,6 +1,8 @@
 import jax
 import jax.numpy as jnp
 from jax import lax
+from jax.experimental import pallas as pl
+from jax.experimental.pallas import tpu as pltpu
 from jax.sharding import PartitionSpec as P
 
 
@@ -32,21 +34,6 @@
     return jnp.stack(held)
 
 
-def scatter_sum(blocks, axis):
-    size = lax.axis_size(axis)
-    if not pairwise(axis):
-        return lax.psum_scatter(blocks, axis, scatter_dimension=0, tiled=False)
-    me = lax.axis_index(axis)
-    total = lax.dynamic_index_in_dim(blocks, me, 0, keepdims=False)
-    sent = [
-        swap(lax.dynamic_index_in_dim(blocks, me ^ d, 0, keepdims=False), axis, d)
-        for d in range(1, size)
-    ]
-    for part in sent:
-        total = total + part
-    return total
-
-
 def sum_over(values, axis):
     if not pairwise(axis):
         return lax.psum(values, axis)
@@ -55,6 +42,173 @@
     for part in sent:
         total = total + part
     return total
+
+
+def scatter_sum(blocks, axis):
+    if not pairwise(axis):
+        return lax.psum_scatter(jnp.stack(blocks), axis, scatter_dimension=0, tiled=False)
+    total = blocks[0]
+    for part in [swap(blocks[d], axis, d) for d in range(1, len(blocks))]:
+        total = total + part
+    return total
+
+
+def owner_of(slot, axis):
+    return lax.axis_index(axis) ^ slot if pairwise(axis) else slot
+
+
+VMEM_LIMIT = 20 * 1024 * 1024
+IN_VMEM = pl.BlockSpec(memory_space=pltpu.VMEM)
+IN_HBM = pl.BlockSpec(memory_space=pl.ANY)
+CHUNK = 512
+
+
+def project(owners, tokens, weights, step_weights):
+    steps, rows, depth = tokens.shape
+    own_rows = rows // owners
+    widths = [w.shape[1] for w in weights]
+    heads = step_weights.shape[0]
+    columns = sum(widths) + heads
+    block = own_rows * steps
+    pieces = []
+    base = 0
+    for index, width in enumerate(widths):
+        for start in range(0, width, CHUNK):
+            size = min(CHUNK, width - start)
+            pieces.append((index, start, base + start, size))
+        base += width
+
+    def body(*refs):
+        tokens_ref, step_ref = refs[:2]
+        weight_refs = refs[2 : 2 + len(weights)]
+        outs = refs[2 + len(weights) : 2 + len(weights) + owners]
+        held, wide, lhs, sems = refs[2 + len(weights) + owners :]
+        copies = [
+            pltpu.make_async_copy(
+                weight_refs[index].at[:, pl.ds(start, size)],
+                held.at[:, pl.ds(place, size)],
+                sems.at[i],
+            )
+            for i, (index, start, place, size) in enumerate(pieces)
+        ]
+        for copy in copies:
+            copy.start()
+        wide[...] = tokens_ref[...].astype(jnp.float32)
+        for slot in range(owners):
+            owner = owner_of(slot, "expert")
+            for own in range(own_rows):
+                for s in range(steps):
+                    row = slot * block + own * steps + s
+                    lhs[pl.ds(row, 1), :] = wide[s, pl.ds(owner * own_rows + own, 1), :]
+        rows_in = lhs[...].astype(jnp.bfloat16)
+
+        def put(place, size, result):
+            for slot in range(owners):
+                outs[slot][:, pl.ds(place, size)] = result[slot * block : (slot + 1) * block]
+
+        put(
+            columns - heads,
+            heads,
+            lax.dot_general(
+                rows_in,
+                step_ref[...],
+                (((1,), (1,)), ((), ())),
+                preferred_element_type=jnp.float32,
+            ),
+        )
+        for copy, (_, _, place, size) in zip(copies, pieces):
+            copy.wait()
+            put(
+                place,
+                size,
+                jnp.dot(
+                    rows_in, held[:, pl.ds(place, size)], preferred_element_type=jnp.float32
+                ),
+            )
+
+    return pl.pallas_call(
+        body,
+        out_shape=[jax.ShapeDtypeStruct((block, columns), jnp.float32)] * owners,
+        in_specs=[IN_VMEM, IN_VMEM] + [IN_HBM] * len(weights),
+        out_specs=[IN_VMEM] * owners,
+        scratch_shapes=[
+            pltpu.VMEM((depth, sum(widths)), jnp.bfloat16),
+            pltpu.VMEM((steps, rows, depth), jnp.float32),
+            pltpu.VMEM((owners * block, depth), jnp.float32),
+            pltpu.SemaphoreType.DMA((len(pieces),)),
+        ],
+        compiler_params=pltpu.CompilerParams(vmem_limit_bytes=VMEM_LIMIT),
+        name="project",
+    )(tokens, step_weights, *weights)
+
+
+def times_resident(lhs, weights):
+    def body(lhs_ref, weights_ref, out_ref):
+        out_ref[...] = jnp.dot(lhs_ref[...], weights_ref[...], preferred_element_type=jnp.float32)
+
+    return pl.pallas_call(
+        body,
+        out_shape=jax.ShapeDtypeStruct((lhs.shape[0], weights.shape[1]), jnp.float32),
+        in_specs=[IN_VMEM, IN_VMEM],
+        out_specs=IN_VMEM,
+        compiler_params=pltpu.CompilerParams(vmem_limit_bytes=VMEM_LIMIT),
+        name="out_projection",
+    )(lhs, pltpu.with_memory_space_constraint(weights, pltpu.VMEM))
+
+
+def experts(moe_in, chosen, gates, expert_up, expert_down):
+    owners, many, width = moe_in.shape
+    local_experts, _, hidden_width = expert_up.shape
+
+    def body(in_ref, chosen_ref, gates_ref, up_ref, down_ref, *refs):
+        outs, hidden_ref = refs[:-1], refs[-1]
+        first = lax.axis_index("expert") * local_experts
+        row_weights = []
+        for e in range(local_experts):
+            total = jnp.zeros((many, hidden_width), jnp.float32)
+            for j in range(owners):
+                total += jnp.dot(
+                    in_ref[j],
+                    up_ref[e, pl.ds(j * width, width), :],
+                    preferred_element_type=jnp.float32,
+                )
+            total = jnp.maximum(total, 0.0)
+            hidden_ref[e] = (total * total).astype(jnp.bfloat16)
+            row_weights.append(
+                jnp.sum(
+                    jnp.where(chosen_ref[...] == first + e, gates_ref[...], 0.0),
+                    axis=1,
+                    keepdims=True,
+                )
+            )
+        for slot in range(owners):
+            start = owner_of(slot, "expert") * width
+            if pairwise("expert"):
+                start = pl.multiple_of(start, width)
+            total = jnp.zeros((many, width), jnp.float32)
+            for e in range(local_experts):
+                total += row_weights[e] * jnp.dot(
+                    hidden_ref[e],
+                    down_ref[e, :, pl.ds(start, width)],
+                    preferred_element_type=jnp.float32,
+                )
+            outs[slot][...] = total
+
+    return pl.pallas_call(
+        body,
+        out_shape=[jax.ShapeDtypeStruct((many, width), jnp.float32)] * owners,
+        in_specs=[IN_VMEM] * 5,
+        out_specs=[IN_VMEM] * owners,
+        scratch_shapes=[pltpu.VMEM((local_experts, many, hidden_width), jnp.bfloat16)],
+        compiler_params=pltpu.CompilerParams(vmem_limit_bytes=VMEM_LIMIT),
+        name="experts",
+    )(
+        moe_in,
+        chosen,
+        gates,
+        pltpu.with_memory_space_constraint(expert_up, pltpu.VMEM),
+        pltpu.with_memory_space_constraint(expert_down, pltpu.VMEM),
+    )
 
 
 def convolve(window_state, newest, kernel):
@@ -99,19 +253,13 @@
     write_width = conv_write.shape[1]
     groups = write_width // state_size
     heads_group = heads // groups
-    local_experts = expert_up.shape[0]
     many = rows * steps
 
-    current = tokens.transpose(1, 0, 2).reshape(many, features)
-    projected = jnp.concatenate(
-        [
-            jnp.dot(current, w, preferred_element_type=jnp.float32)
-            for w in (proj_gate, proj_input, proj_write, proj_read, proj_step)
-        ],
-        axis=1,
-    )
-    projected = scatter_sum(projected.reshape(owners, own_rows, steps, -1), "expert")
-    projected = projected.astype(jnp.bfloat16)
+    projected = project(
+        owners, tokens, (proj_gate, proj_input, proj_write, proj_read), proj_step.T
+    )
+    projected = scatter_sum(projected, "expert").astype(jnp.bfloat16)
+    projected = projected.reshape(own_rows, steps, -1)
     edges = (inner, 2 * inner, 2 * inner + write_width, 2 * inner + 2 * write_width)
     gate_pre, input_pre, write_pre, read_pre, step_pre = jnp.split(projected, edges, axis=2)
     input_acts, input_final = convolve(window_input, input_pre, conv_input)
@@ -147,27 +295,21 @@
         normed.append(scaled.reshape(own_rows, inner).astype(jnp.bfloat16))
     ssm_final = state.reshape(ssm_state.shape)
 
-    normed = gather(jnp.stack(normed, axis=1), "expert").reshape(many, inner)
-    partial = jnp.dot(normed, out_proj, preferred_element_type=jnp.float32)
-    residual = current.astype(jnp.float32) + sum_over(partial, "tensor")
+    normed = gather(jnp.stack(normed), "expert")
+    normed = normed.transpose(1, 0, 2, 3).reshape(many, inner)
+    partial = times_resident(normed, out_proj)
+    current = tokens.reshape(many, features).astype(jnp.float32)
+    residual = current + sum_over(partial, "tensor")
     moe_in = gather(residual.astype(jnp.bfloat16), "expert")
-    moe_in = moe_in.transpose(1, 0, 2).reshape(many, owners * features)
-
-    first = lax.axis_index("expert") * local_experts
-    chosen = expert_ids.transpose(1, 0, 2).reshape(many, -1)
-    weights = route_gates.transpose(1, 0, 2).reshape(many, -1)
-    moe_sum = jnp.zeros((many, owners * features), jnp.float32)
-    for e in range(local_experts):
-        hidden = jnp.dot(moe_in, expert_up[e], preferred_element_type=jnp.float32)
-        hidden = jnp.maximum(hidden, 0.0)
-        hidden = (hidden * hidden).astype(jnp.bfloat16)
-        expert_out = jnp.dot(hidden, expert_down[e], preferred_element_type=jnp.float32)
-        row_weight = jnp.sum(jnp.where(chosen == first + e, weights, 0.0), axis=1)
-        moe_sum = moe_sum + row_weight[:, None] * expert_out
-    blocks = moe_sum.reshape(many, owners, features).transpose(1, 0, 2)
-    moe_sum = sum_over(scatter_sum(blocks, "expert"), "tensor")
-    mixed = (residual + moe_sum).astype(jnp.bfloat16)
-    mixed_out = mixed.reshape(rows, steps, features).transpose(1, 0, 2)
+    moe_sum = experts(
+        moe_in,
+        expert_ids.reshape(many, -1),
+        route_gates.reshape(many, -1),
+        expert_up,
+        expert_down,
+    )
+    moe_sum = sum_over(scatter_sum(moe_sum, "expert"), "tensor")
+    mixed_out = (residual + moe_sum).astype(jnp.bfloat16).reshape(tokens.shape)
     return (mixed_out, ssm_final, input_final, write_final, read_final)
 
 

time: 62.9 us -> 67.2 us (1.068)
  matrix products: 21 us -> 0 us
  local copies, waits for them, and re-layouts: 3.81 us -> 18.7 us
  Pallas kernels: 0 us -> 7.11 us
  waiting for transfers between devices: 14.5 us -> 17.4 us
    dot_general x10 -> x0, matrix products: 21 us -> none  [the longest x4 14 us: per_device(): jnp.dot(hidden, expert_down[e], preferred_element_type=jnp.float32)]
    unnamed x34 -> x46, local copies, waits for them, and re-layouts: 0.51 us -> 17 us
    pallas_call x0 -> x3, Pallas kernels: none -> 7.11 us  [the longest x1 4.18 us: project(): pl.pallas_call(body, out_shape=[jax.ShapeDtypeStruct((block, columns), jn...]
    ppermute x18, waiting for transfers between devices: 14.5 us -> 17.4 us  [swap(): return lax.ppermute(values, axis, [(i, i ^ distance) for i in range(size)])]
    transpose x1, local copies, waits for them, and re-layouts: 0.79 us -> 0.02 us  [per_device(): normed = normed.transpose(1, 0, 2, 3).reshape(many, inner)]
  transfers between devices with their start and end apart: 18 -> 18, of which waited for: 13 -> 11; matrix products, arithmetic and copies ran while one was open for 4% -> 2% of each run, Pallas kernels for 0% -> 0%
where the time goes in v2:
time: 67.2 us; the launch traced here: 66.7 us
  local copies, waits for them, and re-layouts  18.7 us (28%)
  starting transfers between devices  18.1 us (27%)
  waiting for transfers between devices  17.4 us (26%)
  Pallas kernels  7.11 us (11%)
  other arithmetic  4.42 us (7%)
  between operations  1.04 us (2%)
    ppermute x18, starting transfers between devices, swap(): return lax.ppermute(values, axis, [(i, i ^ distance) for i in range(size)])  18.1 us
    ppermute x18, waiting for transfers between devices, swap(): return lax.ppermute(values, axis, [(i, i ^ distance) for i in range(size)])  17.4 us
    unnamed x46, local copies, waits for them, and re-layouts  17 us
    pallas_call x1, Pallas kernels, project(): pl.pallas_call(body, out_shape=[jax.ShapeDtypeStruct((block, columns), jn...  4.18 us
    pallas_call x1, Pallas kernels, experts(): pl.pallas_call(body, out_shape=[jax.ShapeDtypeStruct((many, width), jnp.f...  2.29 us
    reduce_sum x1, other arithmetic, per_device(): jnp.sum(state * read_grouped, axis=-1)  2.17 us
  transfers between devices with their start and end apart: 18, of which 11 were waited for; matrix products, arithmetic and copies ran while one was open for 2% of the time, Pallas kernels for 0%

profile of v2, /device:TPU:0, one launch (start us, length us, event | category | flops | bytes accessed | tf_op | source)
XLA Modules:
  0.0 66.7 jit_solution(16453579227955570640)
XLA Ops:
  0.6 2.2 %copy-done.2 = bf16[1024,2048]{1,0:T(8,128)(2,1)S(1)} copy-done((bf16[1024,2048]{1,0:T(8,128)(2,1)S(1)}, bf16[1024,2048]{1,0:T(8,128)(2,1)}, u32[]{:S(2)}) %copy-start.2) | copy-done | bytes 4194328
  2.8 2.2 %copy-done.3 = bf16[1024,2048]{1,0:T(8,128)(2,1)S(1)} copy-done((bf16[1024,2048]{1,0:T(8,128)(2,1)S(1)}, bf16[1024,2048]{1,0:T(8,128)(2,1)}, u32[]{:S(2)}) %copy-start.3) | copy-done | bytes 4194328
  5.0 1.0 %copy-done.5 = bf16[1024,256]{1,0:T(8,128)(2,1)S(1)} copy-done((bf16[1024,256]{1,0:T(8,128)(2,1)S(1)}, bf16[1024,256]{1,0:T(8,128)(2,1)}, u32[]{:S(2)}) %copy-start.5) | copy-done | bytes 524312
  6.1 1.0 %copy-done.6 = bf16[1024,256]{1,0:T(8,128)(2,1)S(1)} copy-done((bf16[1024,256]{1,0:T(8,128)(2,1)S(1)}, bf16[1024,256]{1,0:T(8,128)(2,1)}, u32[]{:S(2)}) %copy-start.6) | copy-done | bytes 524312
  7.1 0.8 %copy-done.7 = bf16[1024,32]{0,1:T(8,128)(2,1)S(1)} copy-done((bf16[1024,32]{0,1:T(8,128)(2,1)S(1)}, bf16[1024,32]{0,1:T(8,128)(2,1)}, u32[]{:S(2)}) %copy-start.7) | copy-done | bytes 65560
  7.9 0.7 %copy-done.8 = bf16[2,4,1024]{2,1,0:T(4,128)(2,1)S(1)} copy-done((bf16[2,4,1024]{2,1,0:T(4,128)(2,1)S(1)}, bf16[2,4,1024]{2,1,0:T(4,128)(2,1)}, u32[]{:S(2)}) %copy-start.8) | copy-done | bytes 16408
  8.7 4.2 %project.1 = (f32[2,4640]{1,0:T(2,128)S(1)}, f32[2,4640]{1,0:T(2,128)S(1)}, f32[2,4640]{1,0:T(2,128)S(1)}, f32[2,4640]{1,0:T(2,128)S(1)}) custom-call(bf16[2,4,1024]{2,1,0:T(4,128)(2,1)S(1)} %copy-done.8, bf16[32,1024]{1,0:T(8,128)(2,1)S(1)} %bitcast.98, bf16[1024,2048]{1,0:T(8,128)(2,1)S(1)} %copy-done.2, bf16[1024,2048]{1,0:T(8,128)(2,1)S(1)} %copy-done.3, ...), custom_call_target="tpu_custom_call" | custom-call | tf_op jit(solution)/shard_map/project/pallas_call | solution.py:129
  13.5 2.6 %collective-permute-start.1 = (f32[2,4640]{1,0:T(2,128)S(1)}, f32[2,4640]{1,0:T(2,128)S(1)}, u32[]{:S(2)}, u32[]{:S(2)}) collective-permute-start(f32[2,4640]{1,0:T(2,128)S(1)} %get-tuple-element.15), channel_id=1, source_target_pairs={{0,8},{4,12},{8,0},{12,4},{1,9},{5,13},{9,1},{13,5},{2,10},{6,14},... | collective-permute-start | bytes 111368 | tf_op jit(solution)/shard_map/ppermute | solution.py:20
  16.3 1.8 %collective-permute-done.1 = f32[2,4640]{1,0:T(2,128)S(1)} collective-permute-done((f32[2,4640]{1,0:T(2,128)S(1)}, f32[2,4640]{1,0:T(2,128)S(1)}, u32[]{:S(2)}, u32[]{:S(2)}) %collective-permute-start.1) | collective-permute-done | bytes 37152 | tf_op jit(solution)/shard_map/ppermute | solution.py:20
  18.1 1.4 %collective-permute-done.2 = f32[2,4640]{1,0:T(2,128)S(1)} collective-permute-done((f32[2,4640]{1,0:T(2,128)S(1)}, f32[2,4640]{1,0:T(2,128)S(1)}, u32[]{:S(2)}, u32[]{:S(2)}) %collective-permute-start.2) | collective-permute-done | bytes 37152 | tf_op jit(solution)/shard_map/ppermute | solution.py:20
  20.3 2.2 %multiply_reduce_fusion = (f32[32,64]{1,0:T(8,128)S(1)}, f32[1,32,64,128]{3,2,1,0:T(8,128)}, f32[32,64]{1,0:T(8,128)S(1)}) fusion(f32[32,128]{1,0:T(8,128)S(1)} %bitcast.102, f32[32,128]{1,0:T(8,128)S(1)} %bitcast.101, f32[32,64]{1,0:T(8,128)S(1)} %get-tuple-element.60, f32[32,128]{1,0:T(8,128)S(1)} %bitcast.103, f32[32,64]{1,0:T(8,128)S(1)} %get-tuple-element.61, ...), kind=kLoop, calls=%fused_computation | loop fusion | flops 2617344 | bytes 2195712 | tf_op jit(solution)/shard_map/reduce_sum | solution.py:284
  23.5 0.7 %collective-permute-start.3 = (bf16[2,1,2048]{2,0,1:T(2,128)(2,1)S(1)}, bf16[2,1,2048]{2,0,1:T(2,128)(2,1)S(1)}, u32[]{:S(2)}, u32[]{:S(2)}) collective-permute-start(bf16[2,1,2048]{2,0,1:T(2,128)(2,1)S(1)} %pad_maximum_fusion.2), channel_id=1, source_target_pairs={{0,12},{4,8},{8,4},{12,0},{1,13},{5,9},{9,5},{13,1},{2,14},{6,10},... | collective-permute-start | bytes 24584 | tf_op jit(solution)/shard_map/ppermute | solution.py:20
  24.2 1.2 %collective-permute-start.4 = (bf16[2,1,2048]{2,0,1:T(2,128)(2,1)S(1)}, bf16[2,1,2048]{2,0,1:T(2,128)(2,1)S(1)}, u32[]{:S(2)}, u32[]{:S(2)}) collective-permute-start(bf16[2,1,2048]{2,0,1:T(2,128)(2,1)S(1)} %pad_maximum_fusion.2), channel_id=1, source_target_pairs={{0,8},{4,12},{8,0},{12,4},{1,9},{5,13},{9,1},{13,5},{2,10},{6,14},... | collective-permute-start | bytes 24584 | tf_op jit(solution)/shard_map/ppermute | solution.py:20
  25.4 1.2 %collective-permute-done.3 = bf16[2,1,2048]{2,0,1:T(2,128)(2,1)S(1)} collective-permute-done((bf16[2,1,2048]{2,0,1:T(2,128)(2,1)S(1)}, bf16[2,1,2048]{2,0,1:T(2,128)(2,1)S(1)}, u32[]{:S(2)}, u32[]{:S(2)}) %collective-permute-start.3) | collective-permute-done | bytes 8224 | tf_op jit(solution)/shard_map/ppermute | solution.py:20
  26.6 1.2 %collective-permute-done.4 = bf16[2,1,2048]{2,0,1:T(2,128)(2,1)S(1)} collective-permute-done((bf16[2,1,2048]{2,0,1:T(2,128)(2,1)S(1)}, bf16[2,1,2048]{2,0,1:T(2,128)(2,1)S(1)}, u32[]{:S(2)}, u32[]{:S(2)}) %collective-permute-start.4) | collective-permute-done | bytes 8224 | tf_op jit(solution)/shard_map/ppermute | solution.py:20
  28.0 2.2 %copy-done.4 = bf16[2048,1024]{1,0:T(8,128)(2,1)S(1)} copy-done((bf16[2048,1024]{1,0:T(8,128)(2,1)S(1)}, bf16[2048,1024]{1,0:T(8,128)(2,1)}, u32[]{:S(2)}) %copy-start.4) | copy-done | bytes 4194328
  30.2 0.6 out_projection.1
  30.9 1.7 %collective-permute-start.6 = (f32[8,1024]{1,0:T(8,128)S(1)}, f32[8,1024]{1,0:T(8,128)S(1)}, u32[]{:S(2)}, u32[]{:S(2)}) collective-permute-start(f32[8,1024]{1,0:T(8,128)S(1)} %out_projection.1), channel_id=1, source_target_pairs={{0,1},{1,0},{2,3},{3,2},{4,5},{5,4},{6,7},{7,6},{8,9},{9,8},{10,11... | collective-permute-start | bytes 98312 | tf_op jit(solution)/shard_map/ppermute | solution.py:20
  32.5 2.6 %collective-permute-start.7 = (f32[8,1024]{1,0:T(8,128)S(1)}, f32[8,1024]{1,0:T(8,128)S(1)}, u32[]{:S(2)}, u32[]{:S(2)}) collective-permute-start(f32[8,1024]{1,0:T(8,128)S(1)} %out_projection.1), channel_id=1, source_target_pairs={{0,2},{1,3},{2,0},{3,1},{4,6},{5,7},{6,4},{7,5},{8,10},{9,11},{10,... | collective-permute-start | bytes 98312 | tf_op jit(solution)/shard_map/ppermute | solution.py:20
  35.3 2.3 %collective-permute-done.7 = f32[8,1024]{1,0:T(8,128)S(1)} collective-permute-done((f32[8,1024]{1,0:T(8,128)S(1)}, f32[8,1024]{1,0:T(8,128)S(1)}, u32[]{:S(2)}, u32[]{:S(2)}) %collective-permute-start.7) | collective-permute-done | bytes 32800 | tf_op jit(solution)/shard_map/ppermute | solution.py:20
  37.6 3.2 %collective-permute-done.8 = f32[8,1024]{1,0:T(8,128)S(1)} collective-permute-done((f32[8,1024]{1,0:T(8,128)S(1)}, f32[8,1024]{1,0:T(8,128)S(1)}, u32[]{:S(2)}, u32[]{:S(2)}) %collective-permute-start.8) | collective-permute-done | bytes 32800 | tf_op jit(solution)/shard_map/ppermute | solution.py:20
  40.8 1.1 %collective-permute-start.10 = (bf16[8,1024]{1,0:T(8,128)(2,1)S(1)}, bf16[8,1024]{1,0:T(8,128)(2,1)S(1)}, u32[]{:S(2)}, u32[]{:S(2)}) collective-permute-start(bf16[8,1024]{1,0:T(8,128)(2,1)S(1)} %get-tuple-element.31), channel_id=1, source_target_pairs={{0,8},{4,12},{8,0},{12,4},{1,9},{5,13},{9,1},{13,5},{2,10},{6,14},... | collective-permute-start | bytes 49160 | tf_op jit(solution)/shard_map/ppermute | solution.py:20
  42.0 1.1 %collective-permute-start.9 = (bf16[8,1024]{1,0:T(8,128)(2,1)S(1)}, bf16[8,1024]{1,0:T(8,128)(2,1)S(1)}, u32[]{:S(2)}, u32[]{:S(2)}) collective-permute-start(bf16[8,1024]{1,0:T(8,128)(2,1)S(1)} %get-tuple-element.31), channel_id=1, source_target_pairs={{0,12},{4,8},{8,4},{12,0},{1,13},{5,9},{9,5},{13,1},{2,14},{6,10},... | collective-permute-start | bytes 49160 | tf_op jit(solution)/shard_map/ppermute | solution.py:20
  43.1 1.6 %collective-permute-done.10 = bf16[8,1024]{1,0:T(8,128)(2,1)S(1)} collective-permute-done((bf16[8,1024]{1,0:T(8,128)(2,1)S(1)}, bf16[8,1024]{1,0:T(8,128)(2,1)S(1)}, u32[]{:S(2)}, u32[]{:S(2)}) %collective-permute-start.10) | collective-permute-done | bytes 16416 | tf_op jit(solution)/shard_map/ppermute | solution.py:20
  45.2 3.4 %copy-done = bf16[4,4096,256]{2,1,0:T(8,128)(2,1)S(1)} copy-done((bf16[4,4096,256]{2,1,0:T(8,128)(2,1)S(1)}, bf16[4,4096,256]{2,1,0:T(8,128)(2,1)}, u32[]{:S(2)}) %copy-start) | copy-done | bytes 8388632
  48.6 3.4 %copy-done.1 = bf16[4,256,4096]{2,1,0:T(8,128)(2,1)S(1)} copy-done((bf16[4,256,4096]{2,1,0:T(8,128)(2,1)S(1)}, bf16[4,256,4096]{2,1,0:T(8,128)(2,1)}, u32[]{:S(2)}) %copy-start.1) | copy-done | bytes 8388632
  52.0 2.3 %experts.1 = (f32[8,1024]{1,0:T(8,128)S(1)}, f32[8,1024]{1,0:T(8,128)S(1)}, f32[8,1024]{1,0:T(8,128)S(1)}, f32[8,1024]{1,0:T(8,128)S(1)}) custom-call(bf16[4,8,1024]{2,1,0:T(8,128)(2,1)S(1)} %pad_maximum_fusion.in_ref, s32[8,8]{1,0:T(8,128)S(1)} %bitcast.99, f32[8,8]{1,0:T(8,128)S(1)} %bitcast.100, bf16[4,4096,256]{2,1,0:T(8,128)(2,1)S(1)} %copy-done, ...), custom_call_target="tpu_custom_call" | custom-call | tf_op jit(solution)/shard_map/experts/pallas_call | solution.py:197
  54.8 0.9 %collective-permute-start.13 = (f32[8,1024]{1,0:T(8,128)S(1)}, f32[8,1024]{1,0:T(8,128)S(1)}, u32[]{:S(2)}, u32[]{:S(2)}) collective-permute-start(f32[8,1024]{1,0:T(8,128)S(1)} %get-tuple-element.19), channel_id=1, source_target_pairs={{0,8},{4,12},{8,0},{12,4},{1,9},{5,13},{9,1},{13,5},{2,10},{6,14},... | collective-permute-start | bytes 98312 | tf_op jit(solution)/shard_map/ppermute | solution.py:20
  56.9 1.9 %collective-permute-done.13 = f32[8,1024]{1,0:T(8,128)S(1)} collective-permute-done((f32[8,1024]{1,0:T(8,128)S(1)}, f32[8,1024]{1,0:T(8,128)S(1)}, u32[]{:S(2)}, u32[]{:S(2)}) %collective-permute-start.13) | collective-permute-done | bytes 32800 | tf_op jit(solution)/shard_map/ppermute | solution.py:20
  59.4 0.9 %collective-permute-start.16 = (f32[8,1024]{1,0:T(8,128)S(1)}, f32[8,1024]{1,0:T(8,128)S(1)}, u32[]{:S(2)}, u32[]{:S(2)}) collective-permute-start(f32[8,1024]{1,0:T(8,128)S(1)} %add_add_fusion), channel_id=1, source_target_pairs={{0,2},{1,3},{2,0},{3,1},{4,6},{5,7},{6,4},{7,5},{8,10},{9,11},{10,... | collective-permute-start | bytes 98312 | tf_op jit(solution)/shard_map/ppermute | solution.py:20
  60.3 3.5 %collective-permute-start.17 = (f32[8,1024]{1,0:T(8,128)S(1)}, f32[8,1024]{1,0:T(8,128)S(1)}, u32[]{:S(2)}, u32[]{:S(2)}) collective-permute-start(f32[8,1024]{1,0:T(8,128)S(1)} %add_add_fusion), channel_id=1, source_target_pairs={{0,3},{1,2},{2,1},{3,0},{4,7},{5,6},{6,5},{7,4},{8,11},{9,10},{10,... | collective-permute-start | bytes 98312 | tf_op jit(solution)/shard_map/ppermute | solution.py:20
  64.4 1.7 %collective-permute-done.17 = f32[8,1024]{1,0:T(8,128)S(1)} collective-permute-done((f32[8,1024]{1,0:T(8,128)S(1)}, f32[8,1024]{1,0:T(8,128)S(1)}, u32[]{:S(2)}, u32[]{:S(2)}) %collective-permute-start.17) | collective-permute-done | bytes 32800 | tf_op jit(solution)/shard_map/ppermute | solution.py:20
  (109 shorter events, 7.0 us)
Async XLA Ops:
  8.7 7.4 %copy-start.20 = (f32[32]{0:T(128)S(1)}, f32[32]{0:T(128)}, u32[]{:S(2)}) copy-start(f32[32]{0:T(128)} %param.36) | copy-start | bytes 388
  8.7 11.0 %copy-start.13 = (bf16[1,3,2048]{2,1,0:T(4,128)(2,1)S(1)}, bf16[1,3,2048]{2,1,0:T(4,128)(2,1)}, u32[]{:S(2)}) copy-start(bf16[1,3,2048]{2,1,0:T(4,128)(2,1)} %param.31) | copy-start | bytes 36868
  8.7 11.0 %copy-start.14 = (f32[4,2048]{1,0:T(4,128)S(1)}, f32[4,2048]{1,0:T(4,128)}, u32[]{:S(2)}) copy-start(f32[4,2048]{1,0:T(4,128)} %param.28) | copy-start | bytes 98308
  8.7 11.2 %copy-start.15 = (bf16[1,3,256]{2,1,0:T(4,128)(2,1)S(1)}, bf16[1,3,256]{2,1,0:T(4,128)(2,1)}, u32[]{:S(2)}) copy-start(bf16[1,3,256]{2,1,0:T(4,128)(2,1)} %param.33) | copy-start | bytes 4612
  8.7 11.2 %copy-start.16 = (bf16[1,3,256]{2,1,0:T(4,128)(2,1)S(1)}, bf16[1,3,256]{2,1,0:T(4,128)(2,1)}, u32[]{:S(2)}) copy-start(bf16[1,3,256]{2,1,0:T(4,128)(2,1)} %param.32) | copy-start | bytes 4612
  8.7 11.2 %copy-start.18 = (f32[4,256]{1,0:T(4,128)S(1)}, f32[4,256]{1,0:T(4,128)}, u32[]{:S(2)}) copy-start(f32[4,256]{1,0:T(4,128)} %param.29) | copy-start | bytes 12292
  8.7 11.3 %copy-start.19 = (f32[4,256]{1,0:T(4,128)S(1)}, f32[4,256]{1,0:T(4,128)}, u32[]{:S(2)}) copy-start(f32[4,256]{1,0:T(4,128)} %param.30) | copy-start | bytes 12292
  8.7 11.5 %copy-start.21 = (f32[32]{0:T(128)S(1)}, f32[32]{0:T(128)}, u32[]{:S(2)}) copy-start(f32[32]{0:T(128)} %param.35) | copy-start | bytes 388
  8.7 11.5 %copy-start.22 = (f32[32]{0:T(128)S(1)}, f32[32]{0:T(128)}, u32[]{:S(2)}) copy-start(f32[32]{0:T(128)} %param.34) | copy-start | bytes 388
  8.7 11.6 %copy-start.12 = (f32[1,32,64,128]{3,2,1,0:T(8,128)S(1)}, f32[1,32,64,128]{3,2,1,0:T(8,128)}, u32[]{:S(2)}) copy-start(f32[1,32,64,128]{3,2,1,0:T(8,128)} %param.38) | copy-start | bytes 3145732
  8.7 14.7 %copy-start.17 = (f32[2048]{0:T(1024)S(1)}, f32[2048]{0:T(1024)}, u32[]{:S(2)}) copy-start(f32[2048]{0:T(1024)} %param.37) | copy-start | bytes 24580
  12.9 22.3 %copy-start.9 = (bf16[2,4,1024]{2,1,0:T(4,128)(2,1)S(1)}, bf16[2,4,1024]{2,1,0:T(4,128)(2,1)}, u32[]{:S(2)}) copy-start(bf16[2,4,1024]{2,1,0:T(4,128)(2,1)} %refs_0_.1) | copy-start | bytes 49156
  12.9 3.4 %collective-permute-start = (f32[2,4640]{1,0:T(2,128)S(1)}, f32[2,4640]{1,0:T(2,128)S(1)}, u32[]{:S(2)}, u32[]{:S(2)}) collective-permute-start(f32[2,4640]{1,0:T(2,128)S(1)} %get-tuple-element.14), channel_id=1, source_target_pairs={{0,4},{4,0},{8,12},{12,8},{1,5},{5,1},{9,13},{13,9},{2,6},{6,2},{1... | collective-permute-start | bytes 111368 | tf_op jit(solution)/shard_map/ppermute | solution.py:20
  13.5 4.7 %collective-permute-start.1 = (f32[2,4640]{1,0:T(2,128)S(1)}, f32[2,4640]{1,0:T(2,128)S(1)}, u32[]{:S(2)}, u32[]{:S(2)}) collective-permute-start(f32[2,4640]{1,0:T(2,128)S(1)} %get-tuple-element.15), channel_id=1, source_target_pairs={{0,8},{4,12},{8,0},{12,4},{1,9},{5,13},{9,1},{13,5},{2,10},{6,14},... | collective-permute-start | bytes 111368 | tf_op jit(solution)/shard_map/ppermute | solution.py:20
  16.0 3.5 %collective-permute-start.2 = (f32[2,4640]{1,0:T(2,128)S(1)}, f32[2,4640]{1,0:T(2,128)S(1)}, u32[]{:S(2)}, u32[]{:S(2)}) collective-permute-start(f32[2,4640]{1,0:T(2,128)S(1)} %get-tuple-element.16), channel_id=1, source_target_pairs={{0,12},{4,8},{8,4},{12,0},{1,13},{5,9},{9,5},{13,1},{2,14},{6,10},... | collective-permute-start | bytes 111368 | tf_op jit(solution)/shard_map/ppermute | solution.py:20
  19.5 25.7 %copy-start.10 = (s32[2,4,8]{2,1,0:T(4,128)S(1)}, s32[2,4,8]{2,1,0:T(4,128)}, u32[]{:S(2)}) copy-start(s32[2,4,8]{2,1,0:T(4,128)} %param.42) | copy-start | bytes 772
  19.5 25.7 %copy-start.11 = (f32[2,4,8]{2,1,0:T(4,128)S(1)}, f32[2,4,8]{2,1,0:T(4,128)}, u32[]{:S(2)}) copy-start(f32[2,4,8]{2,1,0:T(4,128)} %param.43) | copy-start | bytes 772
  23.5 3.1 %collective-permute-start.3 = (bf16[2,1,2048]{2,0,1:T(2,128)(2,1)S(1)}, bf16[2,1,2048]{2,0,1:T(2,128)(2,1)S(1)}, u32[]{:S(2)}, u32[]{:S(2)}) collective-permute-start(bf16[2,1,2048]{2,0,1:T(2,128)(2,1)S(1)} %pad_maximum_fusion.2), channel_id=1, source_target_pairs={{0,12},{4,8},{8,4},{12,0},{1,13},{5,9},{9,5},{13,1},{2,14},{6,10},... | collective-permute-start | bytes 24584 | tf_op jit(solution)/shard_map/ppermute | solution.py:20
  24.2 3.7 %collective-permute-start.4 = (bf16[2,1,2048]{2,0,1:T(2,128)(2,1)S(1)}, bf16[2,1,2048]{2,0,1:T(2,128)(2,1)S(1)}, u32[]{:S(2)}, u32[]{:S(2)}) collective-permute-start(bf16[2,1,2048]{2,0,1:T(2,128)(2,1)S(1)} %pad_maximum_fusion.2), channel_id=1, source_target_pairs={{0,8},{4,12},{8,0},{12,4},{1,9},{5,13},{9,1},{13,5},{2,10},{6,14},... | collective-permute-start | bytes 24584 | tf_op jit(solution)/shard_map/ppermute | solution.py:20
  25.4 2.5 %collective-permute-start.5 = (bf16[2,1,2048]{2,0,1:T(2,128)(2,1)S(1)}, bf16[2,1,2048]{2,0,1:T(2,128)(2,1)S(1)}, u32[]{:S(2)}, u32[]{:S(2)}) collective-permute-start(bf16[2,1,2048]{2,0,1:T(2,128)(2,1)S(1)} %pad_maximum_fusion.2), channel_id=1, source_target_pairs={{0,4},{4,0},{8,12},{12,8},{1,5},{5,1},{9,13},{13,9},{2,6},{6,2},{1... | collective-permute-start | bytes 24584 | tf_op jit(solution)/shard_map/ppermute | solution.py:20
  30.9 4.4 %collective-permute-start.6 = (f32[8,1024]{1,0:T(8,128)S(1)}, f32[8,1024]{1,0:T(8,128)S(1)}, u32[]{:S(2)}, u32[]{:S(2)}) collective-permute-start(f32[8,1024]{1,0:T(8,128)S(1)} %out_projection.1), channel_id=1, source_target_pairs={{0,1},{1,0},{2,3},{3,2},{4,5},{5,4},{6,7},{7,6},{8,9},{9,8},{10,11... | collective-permute-start | bytes 98312 | tf_op jit(solution)/shard_map/ppermute | solution.py:20
  32.5 5.1 %collective-permute-start.7 = (f32[8,1024]{1,0:T(8,128)S(1)}, f32[8,1024]{1,0:T(8,128)S(1)}, u32[]{:S(2)}, u32[]{:S(2)}) collective-permute-start(f32[8,1024]{1,0:T(8,128)S(1)} %out_projection.1), channel_id=1, source_target_pairs={{0,2},{1,3},{2,0},{3,1},{4,6},{5,7},{6,4},{7,5},{8,10},{9,11},{10,... | collective-permute-start | bytes 98312 | tf_op jit(solution)/shard_map/ppermute | solution.py:20
  35.1 5.7 %collective-permute-start.8 = (f32[8,1024]{1,0:T(8,128)S(1)}, f32[8,1024]{1,0:T(8,128)S(1)}, u32[]{:S(2)}, u32[]{:S(2)}) collective-permute-start(f32[8,1024]{1,0:T(8,128)S(1)} %out_projection.1), channel_id=1, source_target_pairs={{0,3},{1,2},{2,1},{3,0},{4,7},{5,6},{6,5},{7,4},{8,11},{9,10},{10,... | collective-permute-start | bytes 98312 | tf_op jit(solution)/shard_map/ppermute | solution.py:20
  40.8 3.8 %collective-permute-start.10 = (bf16[8,1024]{1,0:T(8,128)(2,1)S(1)}, bf16[8,1024]{1,0:T(8,128)(2,1)S(1)}, u32[]{:S(2)}, u32[]{:S(2)}) collective-permute-start(bf16[8,1024]{1,0:T(8,128)(2,1)S(1)} %get-tuple-element.31), channel_id=1, source_target_pairs={{0,8},{4,12},{8,0},{12,4},{1,9},{5,13},{9,1},{13,5},{2,10},{6,14},... | collective-permute-start | bytes 49160 | tf_op jit(solution)/shard_map/ppermute | solution.py:20
  42.0 2.7 %collective-permute-start.11 = (bf16[8,1024]{1,0:T(8,128)(2,1)S(1)}, bf16[8,1024]{1,0:T(8,128)(2,1)S(1)}, u32[]{:S(2)}, u32[]{:S(2)}) collective-permute-start(bf16[8,1024]{1,0:T(8,128)(2,1)S(1)} %get-tuple-element.31), channel_id=1, source_target_pairs={{0,4},{4,0},{8,12},{12,8},{1,5},{5,1},{9,13},{13,9},{2,6},{6,2},{1... | collective-permute-start | bytes 49160 | tf_op jit(solution)/shard_map/ppermute | solution.py:20
  42.0 3.2 %collective-permute-start.9 = (bf16[8,1024]{1,0:T(8,128)(2,1)S(1)}, bf16[8,1024]{1,0:T(8,128)(2,1)S(1)}, u32[]{:S(2)}, u32[]{:S(2)}) collective-permute-start(bf16[8,1024]{1,0:T(8,128)(2,1)S(1)} %get-tuple-element.31), channel_id=1, source_target_pairs={{0,12},{4,8},{8,4},{12,0},{1,13},{5,9},{9,5},{13,1},{2,14},{6,10},... | collective-permute-start | bytes 49160 | tf_op jit(solution)/shard_map/ppermute | solution.py:20
  54.3 2.6 %collective-permute-start.12 = (f32[8,1024]{1,0:T(8,128)S(1)}, f32[8,1024]{1,0:T(8,128)S(1)}, u32[]{:S(2)}, u32[]{:S(2)}) collective-permute-start(f32[8,1024]{1,0:T(8,128)S(1)} %get-tuple-element.18), channel_id=1, source_target_pairs={{0,4},{4,0},{8,12},{12,8},{1,5},{5,1},{9,13},{13,9},{2,6},{6,2},{1... | collective-permute-start | bytes 98312 | tf_op jit(solution)/shard_map/ppermute | solution.py:20
  54.8 3.9 %collective-permute-start.13 = (f32[8,1024]{1,0:T(8,128)S(1)}, f32[8,1024]{1,0:T(8,128)S(1)}, u32[]{:S(2)}, u32[]{:S(2)}) collective-permute-start(f32[8,1024]{1,0:T(8,128)S(1)} %get-tuple-element.19), channel_id=1, source_target_pairs={{0,8},{4,12},{8,0},{12,4},{1,9},{5,13},{9,1},{13,5},{2,10},{6,14},... | collective-permute-start | bytes 98312 | tf_op jit(solution)/shard_map/ppermute | solution.py:20
  55.7 3.6 %collective-permute-start.14 = (f32[8,1024]{1,0:T(8,128)S(1)}, f32[8,1024]{1,0:T(8,128)S(1)}, u32[]{:S(2)}, u32[]{:S(2)}) collective-permute-start(f32[8,1024]{1,0:T(8,128)S(1)} %get-tuple-element.20), channel_id=1, source_target_pairs={{0,12},{4,8},{8,4},{12,0},{1,13},{5,9},{9,5},{13,1},{2,14},{6,10},... | collective-permute-start | bytes 98312 | tf_op jit(solution)/shard_map/ppermute | solution.py:20
  59.4 5.0 %collective-permute-start.15 = (f32[8,1024]{1,0:T(8,128)S(1)}, f32[8,1024]{1,0:T(8,128)S(1)}, u32[]{:S(2)}, u32[]{:S(2)}) collective-permute-start(f32[8,1024]{1,0:T(8,128)S(1)} %add_add_fusion), channel_id=1, source_target_pairs={{0,1},{1,0},{2,3},{3,2},{4,5},{5,4},{6,7},{7,6},{8,9},{9,8},{10,11... | collective-permute-start | bytes 98312 | tf_op jit(solution)/shard_map/ppermute | solution.py:20
  59.4 5.0 %collective-permute-start.16 = (f32[8,1024]{1,0:T(8,128)S(1)}, f32[8,1024]{1,0:T(8,128)S(1)}, u32[]{:S(2)}, u32[]{:S(2)}) collective-permute-start(f32[8,1024]{1,0:T(8,128)S(1)} %add_add_fusion), channel_id=1, source_target_pairs={{0,2},{1,3},{2,0},{3,1},{4,6},{5,7},{6,4},{7,5},{8,10},{9,11},{10,... | collective-permute-start | bytes 98312 | tf_op jit(solution)/shard_map/ppermute | solution.py:20
  60.3 5.7 %collective-permute-start.17 = (f32[8,1024]{1,0:T(8,128)S(1)}, f32[8,1024]{1,0:T(8,128)S(1)}, u32[]{:S(2)}, u32[]{:S(2)}) collective-permute-start(f32[8,1024]{1,0:T(8,128)S(1)} %add_add_fusion), channel_id=1, source_target_pairs={{0,3},{1,2},{2,1},{3,0},{4,7},{5,6},{6,5},{7,4},{8,11},{9,10},{10,... | collective-permute-start | bytes 98312 | tf_op jit(solution)/shard_map/ppermute | solution.py:20
  (9 other events, 17.0 us)

commit v3 on v2

v3 whole, which is shorter than its diff:
```python
import jax
import jax.numpy as jnp
from jax import lax
from jax.experimental import pallas as pl
from jax.experimental.pallas import tpu as pltpu
from jax.sharding import PartitionSpec as P


def silu_float(values):
    return values / (1.0 + jnp.exp(-values))


def pairwise(axis):
    size = lax.axis_size(axis)
    return size <= 4 and size & (size - 1) == 0


def swap(values, axis, distance):
    size = lax.axis_size(axis)
    return lax.ppermute(values, axis, [(i, i ^ distance) for i in range(size)])


def gather(values, axis):
    size = lax.axis_size(axis)
    if not pairwise(axis):
        held = lax.all_gather(values, axis, axis=0)
        return [held[j] for j in range(size)]
    return [values] + [swap(values, axis, d) for d in range(1, size)]


def sum_parts(values, axis):
    return gather(values, axis) if pairwise(axis) else [lax.psum(values, axis)]


def scatter_parts(blocks, axis):
    if not pairwise(axis):
        return [lax.psum_scatter(jnp.stack(blocks), axis, scatter_dimension=0, tiled=False)]
    return [blocks[0]] + [swap(blocks[d], axis, d) for d in range(1, len(blocks))]


def added(parts):
    total = parts[0]
    for part in parts[1:]:
        total = total + part
    return total


def owner_of(slot, axis):
    return lax.axis_index(axis) ^ slot if pairwise(axis) else slot


VMEM_LIMIT = 16 * 1024 * 1024
IN_VMEM = pl.BlockSpec(memory_space=pltpu.VMEM)
IN_HBM = pl.BlockSpec(memory_space=pltpu.HBM)
CHUNK = 512


def local_kernel(body, name, out_shape, ins, scratch=(), bytes_accessed=1 << 20):
    return pl.pallas_call(
        body,
        out_shape=out_shape,
        in_specs=[spec for _, spec in ins],
        out_specs=jax.tree.map(lambda _: IN_VMEM, out_shape),
        scratch_shapes=list(scratch),
        compiler_params=pltpu.CompilerParams(vmem_limit_bytes=VMEM_LIMIT),
        cost_estimate=pl.CostEstimate(
            flops=bytes_accessed, bytes_accessed=bytes_accessed, transcendentals=0
        ),
        name=name,
    )(*[held(array, spec) for array, spec in ins])


def held(array, spec):
    if spec is IN_HBM:
        return pltpu.with_memory_space_constraint(array, pltpu.HBM)
    return array


def resident(array):
    return pltpu.with_memory_space_constraint(array, pltpu.VMEM)


def shaped(shape, dtype=jnp.float32):
    return jax.ShapeDtypeStruct(tuple(shape), dtype)


def project(owners, tokens, weights, step_weights):
    steps, rows, depth = tokens.shape
    own_rows = rows // owners
    widths = [w.shape[1] for w in weights]
    heads = step_weights.shape[0]
    columns = sum(widths) + heads
    block = own_rows * steps
    pieces = []
    base = 0
    for index, width in enumerate(widths):
        for start in range(0, width, CHUNK):
            size = min(CHUNK, width - start)
            pieces.append((index, start, base + start, size))
        base += width
    count = len(weights)

    def body(*refs):
        tokens_ref, step_ref = refs[:2]
        weight_refs = refs[2 : 2 + count]
        outs = refs[2 + count : 2 + count + owners]
        current_ref, tokens_in, step_in, weights_in, wide, lhs, sems = refs[2 + count + owners :]
        first = [
            pltpu.make_async_copy(tokens_ref, tokens_in, sems.at[0]),
            pltpu.make_async_copy(step_ref, step_in, sems.at[1]),
        ]
        copies = [
            pltpu.make_async_copy(
                weight_refs[index].at[:, pl.ds(start, size)],
                weights_in.at[:, pl.ds(place, size)],
                sems.at[2 + i],
            )
            for i, (index, start, place, size) in enumerate(pieces)
        ]
        for copy in first + copies:
            copy.start()
        first[0].wait()
        for s in range(steps):
            wide[s] = tokens_in[s].astype(jnp.float32)
            current_ref[pl.ds(s * rows, rows), :] = wide[s]
        for slot in range(owners):
            owner = owner_of(slot, "expert")
            for own in range(own_rows):
                for s in range(steps):
                    row = slot * block + own * steps + s
                    lhs[pl.ds(row, 1), :] = wide[s, pl.ds(owner * own_rows + own, 1), :]
        rows_in = lhs[...].astype(jnp.bfloat16)

        def put(place, size, result):
            for slot in range(owners):
                outs[slot][:, pl.ds(place, size)] = result[slot * block : (slot + 1) * block]

        first[1].wait()
        put(
            columns - heads,
            heads,
            lax.dot_general(
                rows_in,
                step_in[...],
                (((1,), (1,)), ((), ())),
                preferred_element_type=jnp.float32,
            ),
        )
        for copy, (_, _, place, size) in zip(copies, pieces):
            copy.wait()
            put(
                place,
                size,
                jnp.dot(
                    rows_in, weights_in[:, pl.ds(place, size)], preferred_element_type=jnp.float32
                ),
            )

    *blocks, current = local_kernel(
        body,
        "project",
        [shaped((block, columns))] * owners + [shaped((steps * rows, depth))],
        [(tokens, IN_HBM), (step_weights, IN_HBM)] + [(w, IN_HBM) for w in weights],
        [
            pltpu.VMEM(tokens.shape, jnp.bfloat16),
            pltpu.VMEM(step_weights.shape, jnp.bfloat16),
            pltpu.VMEM((depth, sum(widths)), jnp.bfloat16),
            pltpu.VMEM(tokens.shape, jnp.float32),
            pltpu.VMEM((owners * block, depth), jnp.float32),
            pltpu.SemaphoreType.DMA((2 + len(pieces),)),
        ],
        bytes_accessed=10 << 20,
    )
    return blocks, current


def split_in(values, terms):
    parts = []
    for _ in range(terms):
        part = values.astype(jnp.bfloat16)
        parts.append(part)
        values = values - part.astype(jnp.float32)
    return parts


def spread_heads(step_bias, decay_log, skip_gain, inner):
    heads = step_bias.shape[1]
    head_dim = inner // heads

    def body(bias_ref, decay_ref, skip_ref, params_ref, spread_ref):
        head = lax.broadcasted_iota(jnp.int32, (heads, inner), 0) * head_dim
        channel = lax.broadcasted_iota(jnp.int32, (heads, inner), 1)
        inside = (channel >= head) & (channel < head + head_dim)
        spread = jnp.where(inside, 1.0, 0.0).astype(jnp.bfloat16)
        spread_ref[...] = spread
        rows = jnp.concatenate([bias_ref[...], jnp.exp(decay_ref[...]), skip_ref[...]], axis=0)
        total = jnp.zeros((3, inner), jnp.float32)
        for part in reversed(split_in(rows, 3)):
            total += jnp.dot(part, spread, preferred_element_type=jnp.float32)
        params_ref[...] = total

    return local_kernel(
        body,
        "spread_heads",
        [shaped((3, inner)), shaped((heads, inner), jnp.bfloat16)],
        [(step_bias, IN_VMEM), (decay_log, IN_VMEM), (skip_gain, IN_VMEM)],
    )


def mix(parts, head_params, spread, convs, windows, norm_gain, ssm_state, steps):
    own_rows, heads, head_dim, state_size = ssm_state.shape
    block, columns = parts[0].shape
    inner, width = convs[0].shape[1], convs[1].shape[1]
    groups = width // state_size
    heads_group = heads // groups
    channels = heads_group * head_dim
    taps = convs[0].shape[0]
    count = len(parts)
    edges = (0, inner, 2 * inner, 2 * inner + width, 2 * inner + 2 * width, columns)
    terms = 1 + steps

    def body(*refs):
        part_refs = refs[:count]
        params_ref, spread_ref, *rest = refs[count:]
        conv_refs, window_refs = rest[:3], rest[3:6]
        gain_ref, state_ref, normed_ref, pre_ref, coef_ref, write_ref = rest[6:]
        total = part_refs[0][...]
        for ref in part_refs[1:]:
            total = total + ref[...]
        rounded = total.astype(jnp.bfloat16).astype(jnp.float32)
        pre_ref[...] = rounded[:, edges[1] : edges[4]]
        gate, *newest = [rounded[:, edges[i] : edges[i + 1]] for i in range(4)]
        bias, rate, skip = [params_ref[i : i + 1] for i in range(3)]
        step_pre = jnp.dot(
            rounded[:, edges[4] :].astype(jnp.bfloat16),
            spread_ref[...],
            preferred_element_type=jnp.float32,
        )
        step_size = jax.nn.softplus(step_pre + bias)
        decay = jnp.exp(-step_size * rate)
        gate = silu_float(gate)
        for own in range(own_rows):
            first = own * steps
            acts = []
            for which in range(3):
                taps_in = conv_refs[which][...]
                earlier = window_refs[which][own].astype(jnp.float32)
                line = [earlier[k : k + 1] for k in range(taps - 1)]
                line += [newest[which][first + s : first + s + 1] for s in range(steps)]
                acts.append(
                    [
                        silu_float(added([line[s + k] * taps_in[k : k + 1] for k in range(taps)]))
                        for s in range(steps)
                    ]
                )
            input_act, write_act, read_act = acts
            for s in range(steps):
                write_ref[pl.ds(first + s, 1), :] = write_act[s]
            sizes = [step_size[first + s : first + s + 1] for s in range(steps)]
            decays = [decay[first + s : first + s + 1] for s in range(steps)]
            fresh = [sizes[s] * input_act[s] for s in range(steps)]
            coefs = list(fresh)
            kept = jnp.ones_like(decays[0])
            for s in reversed(range(steps)):
                coefs[s] = coefs[s] * kept
                kept = kept * decays[s]
            for i, row in enumerate([kept] + coefs):
                coef_ref[own, i : i + 1, :] = row
            for g in range(groups):
                span = slice(g * channels, (g + 1) * channels)
                lanes = slice(g * state_size, (g + 1) * state_size)
                state = state_ref[own, g * heads_group : (g + 1) * heads_group]
                state = state.reshape(channels, state_size)
                reads = jnp.concatenate([read_act[s][:, lanes] for s in range(steps)], axis=0)
                high, low = [p.astype(jnp.float32) for p in split_in(reads, 2)]
                reads = jnp.concatenate([high, low], axis=0).astype(jnp.bfloat16)
                by_high, by_low = [
                    lax.dot_general(
                        reads, p, (((1,), (1,)), ((), ())), preferred_element_type=jnp.float32
                    )
                    for p in split_in(state, 2)
                ]
                product = by_high[:steps] + by_high[steps:] + by_low[:steps]
                for s in range(steps):
                    value = product[s : s + 1]
                    for j in range(s + 1):
                        overlap = jnp.sum(
                            write_act[j][:, lanes] * read_act[s][:, lanes], axis=1, keepdims=True
                        )
                        value = decays[j][:, span] * value + fresh[j][:, span] * overlap
                    value = value + skip[:, span] * input_act[s][:, span]
                    value = value * gate[first + s : first + s + 1, span]
                    mean = jnp.mean(value * value, axis=1, keepdims=True)
                    value = value * lax.rsqrt(mean + 1e-05) * gain_ref[:, span]
                    normed_ref[pl.ds(first + s, 1), span] = value.astype(jnp.bfloat16)

    return local_kernel(
        body,
        "mix",
        [
            shaped((block, inner), jnp.bfloat16),
            shaped((block, inner + 2 * width)),
            shaped((own_rows, terms, inner)),
            shaped((block, width)),
        ],
        [(a, IN_VMEM) for a in (*parts, head_params, spread, *convs, *windows, norm_gain, ssm_state)],
        bytes_accessed=4 << 20,
    )


def renew(pre, coefs, writes, windows, ssm_state, steps):
    own_rows, heads, head_dim, state_size = ssm_state.shape
    groups = writes.shape[1] // state_size
    heads_group = heads // groups
    inner = coefs.shape[2]
    widths = [w.shape[2] for w in windows]
    kept = windows[0].shape[1]

    def body(pre_ref, coef_ref, write_ref, *rest):
        window_refs, (state_ref, final_ref), out_refs = rest[:3], rest[3:5], rest[5:]
        for own in range(own_rows):
            first = own * steps
            base = 0
            for window_ref, out_ref, width in zip(window_refs, out_refs, widths):
                line = jnp.concatenate(
                    [
                        window_ref[own].astype(jnp.float32),
                        pre_ref[pl.ds(first, steps), pl.ds(base, width)],
                    ],
                    axis=0,
                )
                out_ref[own] = line[steps:].astype(jnp.bfloat16)
                base += width
            rows = jnp.concatenate(
                [coef_ref[own], jnp.zeros((8 - 1 - steps, inner), jnp.float32)], axis=0
            )
            for h in range(heads):
                lanes = slice((h // heads_group) * state_size, (h // heads_group + 1) * state_size)
                if h % 2 == 0:
                    pair = rows[:, h * head_dim : (h + 2) * head_dim].T
                columns = pair[(h % 2) * head_dim : (h % 2 + 1) * head_dim]
                value = columns[:, 0:1] * state_ref[own, h]
                for s in range(steps):
                    value = value + columns[:, 1 + s : 2 + s] * write_ref[pl.ds(first + s, 1), lanes]
                final_ref[own, h] = value

    return local_kernel(
        body,
        "renew",
        [shaped(ssm_state.shape)] + [shaped(w.shape, jnp.bfloat16) for w in windows],
        [(a, IN_VMEM) for a in (pre, coefs, writes, *windows, ssm_state)],
        bytes_accessed=2 << 20,
    )


def project_out(normed, out_proj, steps):
    owners = len(normed)
    block, inner = normed[0].shape
    own_rows = block // steps
    rows = own_rows * owners

    def body(*refs):
        weights_ref, out_ref, lhs = refs[owners:]
        for slot in range(owners):
            owner = owner_of(slot, "expert")
            values = refs[slot][...].astype(jnp.float32)
            for own in range(own_rows):
                for s in range(steps):
                    row = s * rows + owner * own_rows + own
                    lhs[pl.ds(row, 1), :] = values[own * steps + s : own * steps + s + 1]
        out_ref[...] = jnp.dot(
            lhs[...].astype(jnp.bfloat16), weights_ref[...], preferred_element_type=jnp.float32
        )

    return local_kernel(
        body,
        "project_out",
        shaped((rows * steps, out_proj.shape[1])),
        [(a, IN_VMEM) for a in (*normed, resident(out_proj))],
        [pltpu.VMEM((rows * steps, inner), jnp.float32)],
        bytes_accessed=4 << 20,
    )


def experts(moe_in, chosen, gates, expert_up, expert_down):
    owners = len(moe_in)
    many, width = moe_in[0].shape
    steps, rows, _ = chosen.shape
    local_experts, _, hidden_width = expert_up.shape

    def body(*refs):
        chosen_ref, gates_ref, up_ref, down_ref = refs[owners : owners + 4]
        outs, hidden_ref = refs[owners + 4 : -1], refs[-1]
        first = lax.axis_index("expert") * local_experts

        def span(slot):
            start = owner_of(slot, "expert") * width
            return pl.ds(pl.multiple_of(start, width) if pairwise("expert") else start, width)

        row_weights = []
        for e in range(local_experts):
            total = jnp.zeros((many, hidden_width), jnp.float32)
            for slot in range(owners):
                total += jnp.dot(
                    refs[slot][...], up_ref[e, span(slot), :], preferred_element_type=jnp.float32
                )
            total = jnp.maximum(total, 0.0)
            hidden_ref[e] = (total * total).astype(jnp.bfloat16)
            row_weights.append(
                jnp.concatenate(
                    [
                        jnp.sum(
                            jnp.where(chosen_ref[s] == first + e, gates_ref[s], 0.0),
                            axis=1,
                            keepdims=True,
                        )
                        for s in range(steps)
                    ],
                    axis=0,
                )
            )
        for slot in range(owners):
            total = jnp.zeros((many, width), jnp.float32)
            for e in range(local_experts):
                total += row_weights[e] * jnp.dot(
                    hidden_ref[e], down_ref[e, :, span(slot)], preferred_element_type=jnp.float32
                )
            outs[slot][...] = total

    return local_kernel(
        body,
        "experts",
        [shaped((many, width))] * owners,
        [
            (a, IN_VMEM)
            for a in (*moe_in, chosen, gates, resident(expert_up), resident(expert_down))
        ],
        [pltpu.VMEM((local_experts, many, hidden_width), jnp.bfloat16)],
        bytes_accessed=16 << 20,
    )


def finish(parts, shape):
    steps, rows, _ = shape

    def body(*refs):
        total = added([ref[...] for ref in refs[:-1]])
        for s in range(steps):
            refs[-1][s] = total[s * rows : (s + 1) * rows].astype(jnp.bfloat16)

    return local_kernel(body, "finish", shaped(shape, jnp.bfloat16), [(p, IN_VMEM) for p in parts])


def per_device(
    tokens,
    proj_gate,
    proj_input,
    proj_write,
    proj_read,
    proj_step,
    conv_input,
    conv_write,
    conv_read,
    window_input,
    window_write,
    window_read,
    step_bias,
    decay_log,
    skip_gain,
    norm_gain,
    ssm_state,
    out_proj,
    expert_up,
    expert_down,
    expert_ids,
    route_gates,
):
    steps = tokens.shape[0]
    inner = conv_input.shape[1]
    convs = (conv_input, conv_write, conv_read)
    windows = (window_input, window_write, window_read)
    head_params, spread = spread_heads(
        *[p.reshape(1, -1) for p in (step_bias, decay_log, skip_gain)], inner
    )
    projected, current = project(
        lax.axis_size("expert"),
        tokens,
        (proj_gate, proj_input, proj_write, proj_read),
        proj_step.T,
    )
    normed, pre, coefs, writes = mix(
        scatter_parts(projected, "expert"),
        head_params,
        spread,
        convs,
        windows,
        norm_gain.reshape(1, -1),
        ssm_state,
        steps,
    )
    partial = project_out(gather(normed, "expert"), out_proj, steps)
    ssm_final, *finals = renew(pre, coefs, writes, windows, ssm_state, steps)
    residual = added([current] + sum_parts(partial, "tensor"))
    moe_in = gather(residual.astype(jnp.bfloat16), "expert")
    moe_sum = experts(moe_in, expert_ids, route_gates, expert_up, expert_down)
    moe_sum = added(scatter_parts(moe_sum, "expert"))
    mixed_out = finish([residual] + sum_parts(moe_sum, "tensor"), tokens.shape)
    return (mixed_out, ssm_final, *finals)


def solution(mesh):
    placed = (
        P(None, "groups", "expert"),
        P("expert", "tensor"),
        P("expert", "tensor"),
        P("expert", "tensor"),
        P("expert", "tensor"),
        P("expert", "tensor"),
        P(None, "tensor"),
        P(None, "tensor"),
        P(None, "tensor"),
        P(("groups", "expert"), None, "tensor"),
        P(("groups", "expert"), None, "tensor"),
        P(("groups", "expert"), None, "tensor"),
        P("tensor"),
        P("tensor"),
        P("tensor"),
        P("tensor"),
        P(("groups", "expert"), "tensor", None, None),
        P("tensor", "expert"),
        P("expert", None, "tensor"),
        P("expert", "tensor", None),
        P(None, "groups", None),
        P(None, "groups", None),
    )
    return jax.shard_map(
        per_device,
        mesh=mesh,
        in_specs=placed,
        out_specs=(
            P(None, "groups", "expert"),
            P(("groups", "expert"), "tensor", None, None),
            P(("groups", "expert"), None, "tensor"),
            P(("groups", "expert"), None, "tensor"),
            P(("groups", "expert"), None, "tensor"),
        ),
        check_vma=False,
    )
```

time: 67.2 us -> 54.5 us (0.81)
  local copies, waits for them, and re-layouts: 18.7 us -> 11.5 us
  waiting for transfers between devices: 17.4 us -> 12.6 us
  other arithmetic: 4.42 us -> 0.03 us
  Pallas kernels: 7.11 us -> 11.3 us
    unnamed x46 -> x42, local copies, waits for them, and re-layouts: 17 us -> 11.5 us
    ppermute x18, waiting for transfers between devices: 17.4 us -> 12.6 us  [swap(): return lax.ppermute(values, axis, [(i, i ^ distance) for i in range(size)])]
    pallas_call x3 -> x7, Pallas kernels: 7.11 us -> 11.3 us  [local_kernel(): pl.pallas_call(body, out_shape=out_shape, in_specs=[spec for _, spec in i...]
    reduce_sum x7 -> x0, other arithmetic: 2.68 us -> none  [the longest x1 2.17 us: per_device(): jnp.sum(state * read_grouped, axis=-1)]
    concatenate x2 -> x0, other arithmetic: 1.22 us -> none  [convolve(): window = jnp.concatenate([window_state, newest], axis=1)]
  transfers between devices with their start and end apart: 18 -> 18, of which waited for: 11 -> 9; matrix products, arithmetic and copies ran while one was open for 2% -> 0% of each run, Pallas kernels for 0% -> 5%
where the time goes in v3:
time: 54.5 us; the launch traced here: 54 us
  starting transfers between devices  17.7 us (32%)
  waiting for transfers between devices  12.6 us (23%)
  local copies, waits for them, and re-layouts  11.5 us (21%)
  Pallas kernels  11.3 us (21%)
  between operations  0.8 us (1%)
    ppermute x18, starting transfers between devices, swap(): return lax.ppermute(values, axis, [(i, i ^ distance) for i in range(size)])  17.7 us
    ppermute x18, waiting for transfers between devices, swap(): return lax.ppermute(values, axis, [(i, i ^ distance) for i in range(size)])  12.6 us
    unnamed x42, local copies, waits for them, and re-layouts  11.5 us
    pallas_call x7, Pallas kernels, local_kernel(): pl.pallas_call(body, out_shape=out_shape, in_specs=[spec for _, spec in i...  11.3 us
  transfers between devices with their start and end apart: 18, of which 9 were waited for; matrix products, arithmetic and copies ran while one was open for 0% of the time, Pallas kernels for 5%

profile of v3, /device:TPU:0, one launch (start us, length us, event | category | flops | bytes accessed | tf_op | source)
XLA Modules:
  0.0 54.0 jit_solution(15501660758031949874)
XLA Ops:
  0.7 4.5 %project.1 = (f32[2,4640]{1,0:T(2,128)S(1)}, f32[2,4640]{1,0:T(2,128)S(1)}, f32[2,4640]{1,0:T(2,128)S(1)}, f32[2,4640]{1,0:T(2,128)S(1)}, f32[8,1024]{1,0:T(8,128)S(1)}) custom-call(bf16[2,4,1024]{2,1,0:T(4,128)(2,1)} %refs_0_.1, bf16[32,1024]{1,0:T(8,128)(2,1)} %bitcast.11, bf16[1024,2048]{1,0:T(8,128)(2,1)} %refs_2_.1, bf16[1024,2048]{1,0:T(8,128)(2,1)} %refs_3_.1, ...), custom_call_target="tpu_custom_call" | custom-call | flops 10485760 | bytes 10485760 | tf_op jit(solution)/shard_map/project/pallas_call | solution.py:59
  5.7 2.6 %collective-permute-start.1 = (f32[2,4640]{1,0:T(2,128)S(1)}, f32[2,4640]{1,0:T(2,128)S(1)}, u32[]{:S(2)}, u32[]{:S(2)}) collective-permute-start(f32[2,4640]{1,0:T(2,128)S(1)} %get-tuple-element.27), channel_id=1, source_target_pairs={{0,8},{4,12},{8,0},{12,4},{1,9},{5,13},{9,1},{13,5},{2,10},{6,14},... | collective-permute-start | bytes 111368 | tf_op jit(solution)/shard_map/ppermute | solution.py:20
  8.3 0.7 %copy-done.16 = f32[32]{0:T(128)S(1)} copy-done((f32[32]{0:T(128)S(1)}, f32[32]{0:T(128)}, u32[]{:S(2)}) %copy-start.16) | copy-done | bytes 152
  10.6 1.2 %collective-permute-done.2.refs_3_ = f32[2,4640]{1,0:T(2,128)S(1)} collective-permute-done((f32[2,4640]{1,0:T(2,128)S(1)}, f32[2,4640]{1,0:T(2,128)S(1)}, u32[]{:S(2)}, u32[]{:S(2)}) %collective-permute-start.2) | collective-permute-done | bytes 37152 | tf_op jit(solution)/shard_map/ppermute | solution.py:20
  11.7 1.2 %copy-done.2 = f32[1,32,64,128]{3,2,1,0:T(8,128)S(1)} copy-done((f32[1,32,64,128]{3,2,1,0:T(8,128)S(1)}, f32[1,32,64,128]{3,2,1,0:T(8,128)}, u32[]{:S(2)}) %copy-start.2) | copy-done | bytes 1048600
  13.0 0.7 %copy-done.4 = bf16[1,3,2048]{2,1,0:T(4,128)(2,1)S(1)} copy-done((bf16[1,3,2048]{2,1,0:T(4,128)(2,1)S(1)}, bf16[1,3,2048]{2,1,0:T(4,128)(2,1)}, u32[]{:S(2)}) %copy-start.4) | copy-done | bytes 12312
  13.7 0.8 %copy-done.6 = f32[4,2048]{1,0:T(4,128)S(1)} copy-done((f32[4,2048]{1,0:T(4,128)S(1)}, f32[4,2048]{1,0:T(4,128)}, u32[]{:S(2)}) %copy-start.6) | copy-done | bytes 32792
  14.4 0.7 %copy-done.7 = f32[2048]{0:T(1024)S(1)} copy-done((f32[2048]{0:T(1024)S(1)}, f32[2048]{0:T(1024)}, u32[]{:S(2)}) %copy-start.7) | copy-done | bytes 8216
  15.1 0.7 %copy-done.8 = bf16[1,3,256]{2,1,0:T(4,128)(2,1)S(1)} copy-done((bf16[1,3,256]{2,1,0:T(4,128)(2,1)S(1)}, bf16[1,3,256]{2,1,0:T(4,128)(2,1)}, u32[]{:S(2)}) %copy-start.8) | copy-done | bytes 1560
  15.8 0.7 %copy-done.10 = bf16[1,3,256]{2,1,0:T(4,128)(2,1)S(1)} copy-done((bf16[1,3,256]{2,1,0:T(4,128)(2,1)S(1)}, bf16[1,3,256]{2,1,0:T(4,128)(2,1)}, u32[]{:S(2)}) %copy-start.10) | copy-done | bytes 1560
  16.5 0.7 %copy-done.12 = f32[4,256]{1,0:T(4,128)S(1)} copy-done((f32[4,256]{1,0:T(4,128)S(1)}, f32[4,256]{1,0:T(4,128)}, u32[]{:S(2)}) %copy-start.12) | copy-done | bytes 4120
  17.2 0.7 %copy-done.13 = f32[4,256]{1,0:T(4,128)S(1)} copy-done((f32[4,256]{1,0:T(4,128)S(1)}, f32[4,256]{1,0:T(4,128)}, u32[]{:S(2)}) %copy-start.13) | copy-done | bytes 4120
  18.5 0.7 %collective-permute-start.5 = (bf16[2,2048]{1,0:T(2,128)(2,1)S(1)}, bf16[2,2048]{1,0:T(2,128)(2,1)S(1)}, u32[]{:S(2)}, u32[]{:S(2)}) collective-permute-start(bf16[2,2048]{1,0:T(2,128)(2,1)S(1)} %get-tuple-element.31.refs_0_), channel_id=1, source_target_pairs={{0,12},{4,8},{8,4},{12,0},{1,13},{5,9},{9,5},{13,1},{2,14},{6,10},... | collective-permute-start | bytes 24584 | tf_op jit(solution)/shard_map/ppermute | solution.py:20
  19.2 1.2 %collective-permute-start.4 = (bf16[2,2048]{1,0:T(2,128)(2,1)S(1)}, bf16[2,2048]{1,0:T(2,128)(2,1)S(1)}, u32[]{:S(2)}, u32[]{:S(2)}) collective-permute-start(bf16[2,2048]{1,0:T(2,128)(2,1)S(1)} %get-tuple-element.31.refs_0_), channel_id=1, source_target_pairs={{0,8},{4,12},{8,0},{12,4},{1,9},{5,13},{9,1},{13,5},{2,10},{6,14},... | collective-permute-start | bytes 24584 | tf_op jit(solution)/shard_map/ppermute | solution.py:20
  20.4 1.2 %collective-permute-done.5.refs_3_ = bf16[2,2048]{1,0:T(2,128)(2,1)S(1)} collective-permute-done((bf16[2,2048]{1,0:T(2,128)(2,1)S(1)}, bf16[2,2048]{1,0:T(2,128)(2,1)S(1)}, u32[]{:S(2)}, u32[]{:S(2)}) %collective-permute-start.5) | collective-permute-done | bytes 8224 | tf_op jit(solution)/shard_map/ppermute | solution.py:20
  21.6 1.2 %collective-permute-done.4.refs_2_ = bf16[2,2048]{1,0:T(2,128)(2,1)S(1)} collective-permute-done((bf16[2,2048]{1,0:T(2,128)(2,1)S(1)}, bf16[2,2048]{1,0:T(2,128)(2,1)S(1)}, u32[]{:S(2)}, u32[]{:S(2)}) %collective-permute-start.4) | collective-permute-done | bytes 8224 | tf_op jit(solution)/shard_map/ppermute | solution.py:20
  23.5 3.7 %collective-permute-start.8 = (f32[8,1024]{1,0:T(8,128)S(1)}, f32[8,1024]{1,0:T(8,128)S(1)}, u32[]{:S(2)}, u32[]{:S(2)}) collective-permute-start(f32[8,1024]{1,0:T(8,128)S(1)} %project_out.1), channel_id=1, source_target_pairs={{0,3},{1,2},{2,1},{3,0},{4,7},{5,6},{6,5},{7,4},{8,11},{9,10},{10,... | collective-permute-start | bytes 98312 | tf_op jit(solution)/shard_map/ppermute | solution.py:20
  27.2 0.7 %collective-permute-start.6 = (f32[8,1024]{1,0:T(8,128)S(1)}, f32[8,1024]{1,0:T(8,128)S(1)}, u32[]{:S(2)}, u32[]{:S(2)}) collective-permute-start(f32[8,1024]{1,0:T(8,128)S(1)} %project_out.1), channel_id=1, source_target_pairs={{0,1},{1,0},{2,3},{3,2},{4,5},{5,4},{6,7},{7,6},{8,9},{9,8},{10,11... | collective-permute-start | bytes 98312 | tf_op jit(solution)/shard_map/ppermute | solution.py:20
  27.9 1.4 %collective-permute-done.8 = f32[8,1024]{1,0:T(8,128)S(1)} collective-permute-done((f32[8,1024]{1,0:T(8,128)S(1)}, f32[8,1024]{1,0:T(8,128)S(1)}, u32[]{:S(2)}, u32[]{:S(2)}) %collective-permute-start.8) | collective-permute-done | bytes 32800 | tf_op jit(solution)/shard_map/ppermute | solution.py:20
  29.3 2.7 %collective-permute-done.7 = f32[8,1024]{1,0:T(8,128)S(1)} collective-permute-done((f32[8,1024]{1,0:T(8,128)S(1)}, f32[8,1024]{1,0:T(8,128)S(1)}, u32[]{:S(2)}, u32[]{:S(2)}) %collective-permute-start.7) | collective-permute-done | bytes 32800 | tf_op jit(solution)/shard_map/ppermute | solution.py:20
  32.1 1.2 %collective-permute-start.10 = (bf16[8,1024]{1,0:T(8,128)(2,1)S(1)}, bf16[8,1024]{1,0:T(8,128)(2,1)S(1)}, u32[]{:S(2)}, u32[]{:S(2)}) collective-permute-start(bf16[8,1024]{1,0:T(8,128)(2,1)S(1)} %get-tuple-element.43.refs_0_), channel_id=1, source_target_pairs={{0,8},{4,12},{8,0},{12,4},{1,9},{5,13},{9,1},{13,5},{2,10},{6,14},... | collective-permute-start | bytes 49160 | tf_op jit(solution)/shard_map/ppermute | solution.py:20
  33.3 0.7 %collective-permute-start.9 = (bf16[8,1024]{1,0:T(8,128)(2,1)S(1)}, bf16[8,1024]{1,0:T(8,128)(2,1)S(1)}, u32[]{:S(2)}, u32[]{:S(2)}) collective-permute-start(bf16[8,1024]{1,0:T(8,128)(2,1)S(1)} %get-tuple-element.43.refs_0_), channel_id=1, source_target_pairs={{0,4},{4,0},{8,12},{12,8},{1,5},{5,1},{9,13},{13,9},{2,6},{6,2},{1... | collective-permute-start | bytes 49160 | tf_op jit(solution)/shard_map/ppermute | solution.py:20
  34.0 1.3 %collective-permute-done.11.refs_3_ = bf16[8,1024]{1,0:T(8,128)(2,1)S(1)} collective-permute-done((bf16[8,1024]{1,0:T(8,128)(2,1)S(1)}, bf16[8,1024]{1,0:T(8,128)(2,1)S(1)}, u32[]{:S(2)}, u32[]{:S(2)}) %collective-permute-start.11) | collective-permute-done | bytes 16416 | tf_op jit(solution)/shard_map/ppermute | solution.py:20
  35.3 0.7 %collective-permute-done.10.refs_2_ = bf16[8,1024]{1,0:T(8,128)(2,1)S(1)} collective-permute-done((bf16[8,1024]{1,0:T(8,128)(2,1)S(1)}, bf16[8,1024]{1,0:T(8,128)(2,1)S(1)}, u32[]{:S(2)}, u32[]{:S(2)}) %collective-permute-start.10) | collective-permute-done | bytes 16416 | tf_op jit(solution)/shard_map/ppermute | solution.py:20
  36.0 3.4 %copy-done = bf16[4,256,4096]{2,1,0:T(8,128)(2,1)S(1)} copy-done((bf16[4,256,4096]{2,1,0:T(8,128)(2,1)S(1)}, bf16[4,256,4096]{2,1,0:T(8,128)(2,1)}, u32[]{:S(2)}) %copy-start) | copy-done | bytes 8388632
  39.4 2.3 %experts.1 = (f32[8,1024]{1,0:T(8,128)S(1)}, f32[8,1024]{1,0:T(8,128)S(1)}, f32[8,1024]{1,0:T(8,128)S(1)}, f32[8,1024]{1,0:T(8,128)S(1)}) custom-call(bf16[8,1024]{1,0:T(8,128)(2,1)S(1)} %get-tuple-element.43.refs_0_, bf16[8,1024]{1,0:T(8,128)(2,1)S(1)} %collective-permute-done.9.refs_1_, bf16[8,1024]{1,0:T(8,128)(2,1)S(1)} %collective-permute-done.10.refs_2_, ...), custom_call_target="tpu_custom_call" | custom-call | flops 16777216 | bytes 16777216 | tf_op jit(solution)/shard_map/experts/pallas_call | solution.py:59
  41.8 1.3 %collective-permute-start.13 = (f32[8,1024]{1,0:T(8,128)S(1)}, f32[8,1024]{1,0:T(8,128)S(1)}, u32[]{:S(2)}, u32[]{:S(2)}) collective-permute-start(f32[8,1024]{1,0:T(8,128)S(1)} %get-tuple-element.34), channel_id=1, source_target_pairs={{0,8},{4,12},{8,0},{12,4},{1,9},{5,13},{9,1},{13,5},{2,10},{6,14},... | collective-permute-start | bytes 98312 | tf_op jit(solution)/shard_map/ppermute | solution.py:20
  43.6 2.2 %collective-permute-done.13 = f32[8,1024]{1,0:T(8,128)S(1)} collective-permute-done((f32[8,1024]{1,0:T(8,128)S(1)}, f32[8,1024]{1,0:T(8,128)S(1)}, u32[]{:S(2)}, u32[]{:S(2)}) %collective-permute-start.13) | collective-permute-done | bytes 32800 | tf_op jit(solution)/shard_map/ppermute | solution.py:20
  45.8 0.7 %collective-permute-done.14 = f32[8,1024]{1,0:T(8,128)S(1)} collective-permute-done((f32[8,1024]{1,0:T(8,128)S(1)}, f32[8,1024]{1,0:T(8,128)S(1)}, u32[]{:S(2)}, u32[]{:S(2)}) %collective-permute-start.14) | collective-permute-done | bytes 32800 | tf_op jit(solution)/shard_map/ppermute | solution.py:20
  46.5 1.5 %collective-permute-start.17 = (f32[8,1024]{1,0:T(8,128)S(1)}, f32[8,1024]{1,0:T(8,128)S(1)}, u32[]{:S(2)}, u32[]{:S(2)}) collective-permute-start(f32[8,1024]{1,0:T(8,128)S(1)} %add_add_fusion.refs_1_), channel_id=1, source_target_pairs={{0,3},{1,2},{2,1},{3,0},{4,7},{5,6},{6,5},{7,4},{8,11},{9,10},{10,... | collective-permute-start | bytes 98312 | tf_op jit(solution)/shard_map/ppermute | solution.py:20
  48.7 2.3 %collective-permute-start.15 = (f32[8,1024]{1,0:T(8,128)S(1)}, f32[8,1024]{1,0:T(8,128)S(1)}, u32[]{:S(2)}, u32[]{:S(2)}) collective-permute-start(f32[8,1024]{1,0:T(8,128)S(1)} %add_add_fusion.refs_1_), channel_id=1, source_target_pairs={{0,1},{1,0},{2,3},{3,2},{4,5},{5,4},{6,7},{7,6},{8,9},{9,8},{10,11... | collective-permute-start | bytes 98312 | tf_op jit(solution)/shard_map/ppermute | solution.py:20
  51.0 2.3 %renew.1 = (f32[1,32,64,128]{3,2,1,0:T(8,128)}, bf16[1,3,2048]{2,1,0:T(4,128)(2,1)}, bf16[1,3,256]{2,1,0:T(4,128)(2,1)}, bf16[1,3,256]{2,1,0:T(4,128)(2,1)}) custom-call(f32[2,2560]{1,0:T(2,128)S(1)} %get-tuple-element.36.pre_ref, f32[1,3,2048]{2,1,0:T(4,128)S(1)} %get-tuple-element.37.coef_ref, f32[2,256]{1,0:T(2,128)S(1)} %get-tuple-element.38.write_ref, ...), custom_call_target="tpu_custom_call" | custom-call | flops 2097152 | bytes 2097152 | tf_op jit(solution)/shard_map/renew/pallas_call | solution.py:59
  (56 shorter events, 5.5 us)
Async XLA Ops:
  0.6 22.2 %copy-start.1 = (bf16[2048,1024]{1,0:T(8,128)(2,1)S(1)}, bf16[2048,1024]{1,0:T(8,128)(2,1)}, u32[]{:S(2)}) copy-start(bf16[2048,1024]{1,0:T(8,128)(2,1)} %refs_4_.4) | copy-start | bytes 12582916
  0.6 35.3 %slice-start = ((s8[8388608]{0:T(1024)(128)(4,1)}), s8[4194304]{0:T(1024)(128)(4,1)S(1)}, s32[]{:S(2)}) async-start(s8[8388608]{0:T(1024)(128)(4,1)} %bitcast.5), calls=%async_computation | async-start | bytes 8388608
  0.7 35.3 %slice-start.1 = ((s8[8388608]{0:T(1024)(128)(4,1)}), s8[4194304]{0:T(1024)(128)(4,1)S(1)}, s32[]{:S(2)}) async-start(s8[8388608]{0:T(1024)(128)(4,1)} %bitcast.5), calls=%async_computation.1 | async-start | bytes 8388608
  5.2 5.4 %collective-permute-start = (f32[2,4640]{1,0:T(2,128)S(1)}, f32[2,4640]{1,0:T(2,128)S(1)}, u32[]{:S(2)}, u32[]{:S(2)}) collective-permute-start(f32[2,4640]{1,0:T(2,128)S(1)} %get-tuple-element.26), channel_id=1, source_target_pairs={{0,4},{4,0},{8,12},{12,8},{1,5},{5,1},{9,13},{13,9},{2,6},{6,2},{1... | collective-permute-start | bytes 111368 | tf_op jit(solution)/shard_map/ppermute | solution.py:20
  5.7 4.9 %collective-permute-start.1 = (f32[2,4640]{1,0:T(2,128)S(1)}, f32[2,4640]{1,0:T(2,128)S(1)}, u32[]{:S(2)}, u32[]{:S(2)}) collective-permute-start(f32[2,4640]{1,0:T(2,128)S(1)} %get-tuple-element.27), channel_id=1, source_target_pairs={{0,8},{4,12},{8,0},{12,4},{1,9},{5,13},{9,1},{13,5},{2,10},{6,14},... | collective-permute-start | bytes 111368 | tf_op jit(solution)/shard_map/ppermute | solution.py:20
  8.3 3.5 %collective-permute-start.2 = (f32[2,4640]{1,0:T(2,128)S(1)}, f32[2,4640]{1,0:T(2,128)S(1)}, u32[]{:S(2)}, u32[]{:S(2)}) collective-permute-start(f32[2,4640]{1,0:T(2,128)S(1)} %get-tuple-element.28), channel_id=1, source_target_pairs={{0,12},{4,8},{8,4},{12,0},{1,13},{5,9},{9,5},{13,1},{2,14},{6,10},... | collective-permute-start | bytes 111368 | tf_op jit(solution)/shard_map/ppermute | solution.py:20
  11.7 1.2 %copy-start.2 = (f32[1,32,64,128]{3,2,1,0:T(8,128)S(1)}, f32[1,32,64,128]{3,2,1,0:T(8,128)}, u32[]{:S(2)}) copy-start(f32[1,32,64,128]{3,2,1,0:T(8,128)} %rest_3_.1) | copy-start | bytes 3145732
  13.0 0.7 %copy-start.4 = (bf16[1,3,2048]{2,1,0:T(4,128)(2,1)S(1)}, bf16[1,3,2048]{2,1,0:T(4,128)(2,1)}, u32[]{:S(2)}) copy-start(bf16[1,3,2048]{2,1,0:T(4,128)(2,1)} %rest_0_.1) | copy-start | bytes 36868
  13.7 0.8 %copy-start.6 = (f32[4,2048]{1,0:T(4,128)S(1)}, f32[4,2048]{1,0:T(4,128)}, u32[]{:S(2)}) copy-start(f32[4,2048]{1,0:T(4,128)} %refs_6_.2) | copy-start | bytes 98308
  14.4 0.7 %copy-start.7 = (f32[2048]{0:T(1024)S(1)}, f32[2048]{0:T(1024)}, u32[]{:S(2)}) copy-start(f32[2048]{0:T(1024)} %param.37) | copy-start | bytes 24580
  17.9 18.1 %copy-start.14 = (s32[2,4,8]{2,1,0:T(4,128)S(1)}, s32[2,4,8]{2,1,0:T(4,128)}, u32[]{:S(2)}) copy-start(s32[2,4,8]{2,1,0:T(4,128)} %refs_4_.5) | copy-start | bytes 772
  17.9 18.1 %copy-start.15 = (f32[2,4,8]{2,1,0:T(4,128)S(1)}, f32[2,4,8]{2,1,0:T(4,128)}, u32[]{:S(2)}) copy-start(f32[2,4,8]{2,1,0:T(4,128)} %refs_5_.3) | copy-start | bytes 772
  18.5 3.1 %collective-permute-start.5 = (bf16[2,2048]{1,0:T(2,128)(2,1)S(1)}, bf16[2,2048]{1,0:T(2,128)(2,1)S(1)}, u32[]{:S(2)}, u32[]{:S(2)}) collective-permute-start(bf16[2,2048]{1,0:T(2,128)(2,1)S(1)} %get-tuple-element.31.refs_0_), channel_id=1, source_target_pairs={{0,12},{4,8},{8,4},{12,0},{1,13},{5,9},{9,5},{13,1},{2,14},{6,10},... | collective-permute-start | bytes 24584 | tf_op jit(solution)/shard_map/ppermute | solution.py:20
  19.2 3.7 %collective-permute-start.4 = (bf16[2,2048]{1,0:T(2,128)(2,1)S(1)}, bf16[2,2048]{1,0:T(2,128)(2,1)S(1)}, u32[]{:S(2)}, u32[]{:S(2)}) collective-permute-start(bf16[2,2048]{1,0:T(2,128)(2,1)S(1)} %get-tuple-element.31.refs_0_), channel_id=1, source_target_pairs={{0,8},{4,12},{8,0},{12,4},{1,9},{5,13},{9,1},{13,5},{2,10},{6,14},... | collective-permute-start | bytes 24584 | tf_op jit(solution)/shard_map/ppermute | solution.py:20
  20.3 2.5 %collective-permute-start.3 = (bf16[2,2048]{1,0:T(2,128)(2,1)S(1)}, bf16[2,2048]{1,0:T(2,128)(2,1)S(1)}, u32[]{:S(2)}, u32[]{:S(2)}) collective-permute-start(bf16[2,2048]{1,0:T(2,128)(2,1)S(1)} %get-tuple-element.31.refs_0_), channel_id=1, source_target_pairs={{0,4},{4,0},{8,12},{12,8},{1,5},{5,1},{9,13},{13,9},{2,6},{6,2},{1... | collective-permute-start | bytes 24584 | tf_op jit(solution)/shard_map/ppermute | solution.py:20
  23.5 5.8 %collective-permute-start.8 = (f32[8,1024]{1,0:T(8,128)S(1)}, f32[8,1024]{1,0:T(8,128)S(1)}, u32[]{:S(2)}, u32[]{:S(2)}) collective-permute-start(f32[8,1024]{1,0:T(8,128)S(1)} %project_out.1), channel_id=1, source_target_pairs={{0,3},{1,2},{2,1},{3,0},{4,7},{5,6},{6,5},{7,4},{8,11},{9,10},{10,... | collective-permute-start | bytes 98312 | tf_op jit(solution)/shard_map/ppermute | solution.py:20
  27.2 4.8 %collective-permute-start.7 = (f32[8,1024]{1,0:T(8,128)S(1)}, f32[8,1024]{1,0:T(8,128)S(1)}, u32[]{:S(2)}, u32[]{:S(2)}) collective-permute-start(f32[8,1024]{1,0:T(8,128)S(1)} %project_out.1), channel_id=1, source_target_pairs={{0,2},{1,3},{2,0},{3,1},{4,6},{5,7},{6,4},{7,5},{8,10},{9,11},{10,... | collective-permute-start | bytes 98312 | tf_op jit(solution)/shard_map/ppermute | solution.py:20
  27.2 4.8 %collective-permute-start.6 = (f32[8,1024]{1,0:T(8,128)S(1)}, f32[8,1024]{1,0:T(8,128)S(1)}, u32[]{:S(2)}, u32[]{:S(2)}) collective-permute-start(f32[8,1024]{1,0:T(8,128)S(1)} %project_out.1), channel_id=1, source_target_pairs={{0,1},{1,0},{2,3},{3,2},{4,5},{5,4},{6,7},{7,6},{8,9},{9,8},{10,11... | collective-permute-start | bytes 98312 | tf_op jit(solution)/shard_map/ppermute | solution.py:20
  32.0 19.0 %copy-start.5 = (bf16[1,3,2048]{2,1,0:T(4,128)(2,1)S(1)}, bf16[1,3,2048]{2,1,0:T(4,128)(2,1)}, u32[]{:S(2)}) copy-start(bf16[1,3,2048]{2,1,0:T(4,128)(2,1)} %rest_0_.1) | copy-start | bytes 36868
  32.0 19.0 %copy-start.9 = (bf16[1,3,256]{2,1,0:T(4,128)(2,1)S(1)}, bf16[1,3,256]{2,1,0:T(4,128)(2,1)}, u32[]{:S(2)}) copy-start(bf16[1,3,256]{2,1,0:T(4,128)(2,1)} %rest_1_.1) | copy-start | bytes 4612
  32.0 19.0 %copy-start.11 = (bf16[1,3,256]{2,1,0:T(4,128)(2,1)S(1)}, bf16[1,3,256]{2,1,0:T(4,128)(2,1)}, u32[]{:S(2)}) copy-start(bf16[1,3,256]{2,1,0:T(4,128)(2,1)} %rest_2_.1) | copy-start | bytes 4612
  32.0 3.2 %collective-permute-start.11 = (bf16[8,1024]{1,0:T(8,128)(2,1)S(1)}, bf16[8,1024]{1,0:T(8,128)(2,1)S(1)}, u32[]{:S(2)}, u32[]{:S(2)}) collective-permute-start(bf16[8,1024]{1,0:T(8,128)(2,1)S(1)} %get-tuple-element.43.refs_0_), channel_id=1, source_target_pairs={{0,12},{4,8},{8,4},{12,0},{1,13},{5,9},{9,5},{13,1},{2,14},{6,10},... | collective-permute-start | bytes 49160 | tf_op jit(solution)/shard_map/ppermute | solution.py:20
  32.1 3.8 %collective-permute-start.10 = (bf16[8,1024]{1,0:T(8,128)(2,1)S(1)}, bf16[8,1024]{1,0:T(8,128)(2,1)S(1)}, u32[]{:S(2)}, u32[]{:S(2)}) collective-permute-start(bf16[8,1024]{1,0:T(8,128)(2,1)S(1)} %get-tuple-element.43.refs_0_), channel_id=1, source_target_pairs={{0,8},{4,12},{8,0},{12,4},{1,9},{5,13},{9,1},{13,5},{2,10},{6,14},... | collective-permute-start | bytes 49160 | tf_op jit(solution)/shard_map/ppermute | solution.py:20
  33.3 2.7 %collective-permute-start.9 = (bf16[8,1024]{1,0:T(8,128)(2,1)S(1)}, bf16[8,1024]{1,0:T(8,128)(2,1)S(1)}, u32[]{:S(2)}, u32[]{:S(2)}) collective-permute-start(bf16[8,1024]{1,0:T(8,128)(2,1)S(1)} %get-tuple-element.43.refs_0_), channel_id=1, source_target_pairs={{0,4},{4,0},{8,12},{12,8},{1,5},{5,1},{9,13},{13,9},{2,6},{6,2},{1... | collective-permute-start | bytes 49160 | tf_op jit(solution)/shard_map/ppermute | solution.py:20
  36.0 3.4 %copy-start = (bf16[4,256,4096]{2,1,0:T(8,128)(2,1)S(1)}, bf16[4,256,4096]{2,1,0:T(8,128)(2,1)}, u32[]{:S(2)}) copy-start(bf16[4,256,4096]{2,1,0:T(8,128)(2,1)} %refs_7_.3) | copy-start | bytes 25165828
  39.4 11.6 %copy-start.3 = (f32[1,32,64,128]{3,2,1,0:T(8,128)S(1)}, f32[1,32,64,128]{3,2,1,0:T(8,128)}, u32[]{:S(2)}) copy-start(f32[1,32,64,128]{3,2,1,0:T(8,128)} %rest_3_.1) | copy-start | bytes 3145732
  41.7 1.9 %collective-permute-start.12 = (f32[8,1024]{1,0:T(8,128)S(1)}, f32[8,1024]{1,0:T(8,128)S(1)}, u32[]{:S(2)}, u32[]{:S(2)}) collective-permute-start(f32[8,1024]{1,0:T(8,128)S(1)} %get-tuple-element.33), channel_id=1, source_target_pairs={{0,4},{4,0},{8,12},{12,8},{1,5},{5,1},{9,13},{13,9},{2,6},{6,2},{1... | collective-permute-start | bytes 98312 | tf_op jit(solution)/shard_map/ppermute | solution.py:20
  41.8 3.9 %collective-permute-start.13 = (f32[8,1024]{1,0:T(8,128)S(1)}, f32[8,1024]{1,0:T(8,128)S(1)}, u32[]{:S(2)}, u32[]{:S(2)}) collective-permute-start(f32[8,1024]{1,0:T(8,128)S(1)} %get-tuple-element.34), channel_id=1, source_target_pairs={{0,8},{4,12},{8,0},{12,4},{1,9},{5,13},{9,1},{13,5},{2,10},{6,14},... | collective-permute-start | bytes 98312 | tf_op jit(solution)/shard_map/ppermute | solution.py:20
  43.1 3.4 %collective-permute-start.14 = (f32[8,1024]{1,0:T(8,128)S(1)}, f32[8,1024]{1,0:T(8,128)S(1)}, u32[]{:S(2)}, u32[]{:S(2)}) collective-permute-start(f32[8,1024]{1,0:T(8,128)S(1)} %get-tuple-element.35), channel_id=1, source_target_pairs={{0,12},{4,8},{8,4},{12,0},{1,13},{5,9},{9,5},{13,1},{2,14},{6,10},... | collective-permute-start | bytes 98312 | tf_op jit(solution)/shard_map/ppermute | solution.py:20
  46.5 6.8 %collective-permute-start.17 = (f32[8,1024]{1,0:T(8,128)S(1)}, f32[8,1024]{1,0:T(8,128)S(1)}, u32[]{:S(2)}, u32[]{:S(2)}) collective-permute-start(f32[8,1024]{1,0:T(8,128)S(1)} %add_add_fusion.refs_1_), channel_id=1, source_target_pairs={{0,3},{1,2},{2,1},{3,0},{4,7},{5,6},{6,5},{7,4},{8,11},{9,10},{10,... | collective-permute-start | bytes 98312 | tf_op jit(solution)/shard_map/ppermute | solution.py:20
  48.0 5.3 %collective-permute-start.16 = (f32[8,1024]{1,0:T(8,128)S(1)}, f32[8,1024]{1,0:T(8,128)S(1)}, u32[]{:S(2)}, u32[]{:S(2)}) collective-permute-start(f32[8,1024]{1,0:T(8,128)S(1)} %add_add_fusion.refs_1_), channel_id=1, source_target_pairs={{0,2},{1,3},{2,0},{3,1},{4,6},{5,7},{6,4},{7,5},{8,10},{9,11},{10,... | collective-permute-start | bytes 98312 | tf_op jit(solution)/shard_map/ppermute | solution.py:20
  48.7 4.7 %collective-permute-start.15 = (f32[8,1024]{1,0:T(8,128)S(1)}, f32[8,1024]{1,0:T(8,128)S(1)}, u32[]{:S(2)}, u32[]{:S(2)}) collective-permute-start(f32[8,1024]{1,0:T(8,128)S(1)} %add_add_fusion.refs_1_), channel_id=1, source_target_pairs={{0,1},{1,0},{2,3},{3,2},{4,5},{5,4},{6,7},{7,6},{8,9},{9,8},{10,11... | collective-permute-start | bytes 98312 | tf_op jit(solution)/shard_map/ppermute | solution.py:20
  (7 other events, 4.7 us)

commit v4 on v3

--- a/solution.py
+++ b/solution.py
@@ -28,20 +28,24 @@
     return [values] + [swap(values, axis, d) for d in range(1, size)]
 
 
-def sum_parts(values, axis):
-    return gather(values, axis) if pairwise(axis) else [lax.psum(values, axis)]
+def sum_parts(values, axis, sent=None):
+    if not pairwise(axis):
+        return [lax.psum(values, axis)]
+    sent = values if sent is None else sent
+    return [values] + [swap(sent, axis, d) for d in range(1, lax.axis_size(axis))]
 
 
 def scatter_parts(blocks, axis):
     if not pairwise(axis):
-        return [lax.psum_scatter(jnp.stack(blocks), axis, scatter_dimension=0, tiled=False)]
-    return [blocks[0]] + [swap(blocks[d], axis, d) for d in range(1, len(blocks))]
+        blocks = jnp.stack([block.astype(jnp.float32) for block in blocks])
+        return [lax.psum_scatter(blocks, axis, scatter_dimension=0, tiled=False)]
+    return [blocks[0]] + [swap(blocks[d], axis, d) for d in reversed(range(1, len(blocks)))]
 
 
 def added(parts):
     total = parts[0]
     for part in parts[1:]:
-        total = total + part
+        total = total + part.astype(total.dtype)
     return total
 
 
@@ -52,7 +56,8 @@
 VMEM_LIMIT = 16 * 1024 * 1024
 IN_VMEM = pl.BlockSpec(memory_space=pltpu.VMEM)
 IN_HBM = pl.BlockSpec(memory_space=pltpu.HBM)
-CHUNK = 512
+CHUNK = 512 * 1024
+MIX_COST = 64 << 20
 
 
 def local_kernel(body, name, out_shape, ins, scratch=(), bytes_accessed=1 << 20):
@@ -84,6 +89,10 @@
     return jax.ShapeDtypeStruct(tuple(shape), dtype)
 
 
+def sent_narrow(shape, slots):
+    return [shaped(shape)] + [shaped(shape, jnp.bfloat16)] * (slots - 1)
+
+
 def project(owners, tokens, weights, step_weights):
     steps, rows, depth = tokens.shape
     own_rows = rows // owners
@@ -92,37 +101,33 @@
     columns = sum(widths) + heads
     block = own_rows * steps
     pieces = []
-    base = 0
     for index, width in enumerate(widths):
-        for start in range(0, width, CHUNK):
-            size = min(CHUNK, width - start)
-            pieces.append((index, start, base + start, size))
-        base += width
+        size = max(16, min(depth, CHUNK // width))
+        pieces += [(index, start, min(size, depth - start)) for start in range(0, depth, size)]
+    bases = [sum(widths[:index]) for index in range(len(widths))]
     count = len(weights)
 
     def body(*refs):
         tokens_ref, step_ref = refs[:2]
         weight_refs = refs[2 : 2 + count]
         outs = refs[2 + count : 2 + count + owners]
-        current_ref, tokens_in, step_in, weights_in, wide, lhs, sems = refs[2 + count + owners :]
+        tokens_in, step_in, wide, lhs, sems, *weights_in = refs[2 + count + owners :]
         first = [
             pltpu.make_async_copy(tokens_ref, tokens_in, sems.at[0]),
             pltpu.make_async_copy(step_ref, step_in, sems.at[1]),
         ]
         copies = [
             pltpu.make_async_copy(
-                weight_refs[index].at[:, pl.ds(start, size)],
-                weights_in.at[:, pl.ds(place, size)],
+                weight_refs[index].at[pl.ds(start, size)],
+                weights_in[index].at[pl.ds(start, size)],
                 sems.at[2 + i],
             )
-            for i, (index, start, place, size) in enumerate(pieces)
+            for i, (index, start, size) in enumerate(pieces)
         ]
         for copy in first + copies:
             copy.start()
         first[0].wait()
-        for s in range(steps):
-            wide[s] = tokens_in[s].astype(jnp.float32)
-            current_ref[pl.ds(s * rows, rows), :] = wide[s]
+        wide[...] = tokens_in[...].astype(jnp.float32)
         for slot in range(owners):
             owner = owner_of(slot, "expert")
             for own in range(own_rows):
@@ -133,7 +138,8 @@
 
         def put(place, size, result):
             for slot in range(owners):
-                outs[slot][:, pl.ds(place, size)] = result[slot * block : (slot + 1) * block]
+                part = result[slot * block : (slot + 1) * block]
+                outs[slot][:, pl.ds(place, size)] = part.astype(outs[slot].dtype)
 
         first[1].wait()
         put(
@@ -146,32 +152,33 @@
                 preferred_element_type=jnp.float32,
             ),
         )
-        for copy, (_, _, place, size) in zip(copies, pieces):
+        total = None
+        for copy, (index, start, size) in zip(copies, pieces):
             copy.wait()
-            put(
-                place,
-                size,
-                jnp.dot(
-                    rows_in, weights_in[:, pl.ds(place, size)], preferred_element_type=jnp.float32
-                ),
+            product = jnp.dot(
+                rows_in[:, start : start + size],
+                weights_in[index][pl.ds(start, size)],
+                preferred_element_type=jnp.float32,
             )
-
-    *blocks, current = local_kernel(
+            total = product if start == 0 else total + product
+            if start + size == depth:
+                put(bases[index], widths[index], total)
+
+    return local_kernel(
         body,
         "project",
-        [shaped((block, columns))] * owners + [shaped((steps * rows, depth))],
+        sent_narrow((block, columns), owners),
         [(tokens, IN_HBM), (step_weights, IN_HBM)] + [(w, IN_HBM) for w in weights],
         [
             pltpu.VMEM(tokens.shape, jnp.bfloat16),
             pltpu.VMEM(step_weights.shape, jnp.bfloat16),
-            pltpu.VMEM((depth, sum(widths)), jnp.bfloat16),
             pltpu.VMEM(tokens.shape, jnp.float32),
             pltpu.VMEM((owners * block, depth), jnp.float32),
             pltpu.SemaphoreType.DMA((2 + len(pieces),)),
-        ],
+        ]
+        + [pltpu.VMEM(w.shape, jnp.bfloat16) for w in weights],
         bytes_accessed=10 << 20,
     )
-    return blocks, current
 
 
 def split_in(values, terms):
@@ -183,28 +190,55 @@
     return parts
 
 
-def spread_heads(step_bias, decay_log, skip_gain, inner):
+def stacked(*parts):
+    rows = sum(part.shape[0] for part in parts)
+    parts = [part.astype(jnp.float32) for part in parts]
+    parts.append(jnp.zeros((-rows % 8, parts[0].shape[1]), jnp.float32))
+    return jnp.concatenate(parts, axis=0).astype(jnp.bfloat16)
+
+
+def prepare(step_bias, decay_log, skip_gain, inner, arrays):
     heads = step_bias.shape[1]
     head_dim = inner // heads
-
-    def body(bias_ref, decay_ref, skip_ref, params_ref, spread_ref):
+    count = 3 + len(arrays)
+
+    def body(*refs):
+        sources, (params_ref, spread_ref), outs = refs[:count], refs[count : count + 2], refs[count + 2 :]
+        loaded, sems = outs[:-2], outs[-1]
+        rows_ref = outs[-2]
+        targets = [rows_ref.at[pl.ds(i, 1)] for i in range(3)] + list(loaded)
+        copies = [
+            pltpu.make_async_copy(source, target, sems.at[i])
+            for i, (source, target) in enumerate(zip(sources, targets))
+        ]
+        for copy in copies:
+            copy.start()
         head = lax.broadcasted_iota(jnp.int32, (heads, inner), 0) * head_dim
         channel = lax.broadcasted_iota(jnp.int32, (heads, inner), 1)
         inside = (channel >= head) & (channel < head + head_dim)
         spread = jnp.where(inside, 1.0, 0.0).astype(jnp.bfloat16)
         spread_ref[...] = spread
-        rows = jnp.concatenate([bias_ref[...], jnp.exp(decay_ref[...]), skip_ref[...]], axis=0)
+        for copy in copies[:3]:
+            copy.wait()
+        rows = rows_ref[...]
+        rows = jnp.concatenate([rows[0:1], jnp.exp(rows[1:2]), rows[2:3]], axis=0)
         total = jnp.zeros((3, inner), jnp.float32)
         for part in reversed(split_in(rows, 3)):
             total += jnp.dot(part, spread, preferred_element_type=jnp.float32)
         params_ref[...] = total
-
-    return local_kernel(
-        body,
-        "spread_heads",
-        [shaped((3, inner)), shaped((heads, inner), jnp.bfloat16)],
-        [(step_bias, IN_VMEM), (decay_log, IN_VMEM), (skip_gain, IN_VMEM)],
-    )
+        for copy in copies[3:]:
+            copy.wait()
+
+    params, spread, *loaded = local_kernel(
+        body,
+        "prepare",
+        [shaped((3, inner)), shaped((heads, inner), jnp.bfloat16)]
+        + [shaped(a.shape, a.dtype) for a in arrays],
+        [(a, IN_HBM) for a in (step_bias, decay_log, skip_gain, *arrays)],
+        [pltpu.VMEM((3, heads), jnp.float32), pltpu.SemaphoreType.DMA((count,))],
+        bytes_accessed=4 << 20,
+    )
+    return params, spread, loaded
 
 
 def mix(parts, head_params, spread, convs, windows, norm_gain, ssm_state, steps):
@@ -226,7 +260,7 @@
         gain_ref, state_ref, normed_ref, pre_ref, coef_ref, write_ref = rest[6:]
         total = part_refs[0][...]
         for ref in part_refs[1:]:
-            total = total + ref[...]
+            total = total + ref[...].astype(jnp.float32)
         rounded = total.astype(jnp.bfloat16).astype(jnp.float32)
         pre_ref[...] = rounded[:, edges[1] : edges[4]]
         gate, *newest = [rounded[:, edges[i] : edges[i + 1]] for i in range(4)]
@@ -304,11 +338,12 @@
             shaped((block, width)),
         ],
         [(a, IN_VMEM) for a in (*parts, head_params, spread, *convs, *windows, norm_gain, ssm_state)],
-        bytes_accessed=4 << 20,
-    )
-
-
-def renew(pre, coefs, writes, windows, ssm_state, steps):
+        bytes_accessed=MIX_COST,
+    )
+
+
+def renew(pre, coefs, writes, windows, ssm_state, tokens):
+    steps, rows_all, depth = tokens.shape
     own_rows, heads, head_dim, state_size = ssm_state.shape
     groups = writes.shape[1] // state_size
     heads_group = heads // groups
@@ -317,7 +352,10 @@
     kept = windows[0].shape[1]
 
     def body(pre_ref, coef_ref, write_ref, *rest):
-        window_refs, (state_ref, final_ref), out_refs = rest[:3], rest[3:5], rest[5:]
+        window_refs, (state_ref, tokens_ref, final_ref, current_ref) = rest[:3], rest[3:7]
+        out_refs = rest[7:]
+        for s in range(steps):
+            current_ref[pl.ds(s * rows_all, rows_all), :] = tokens_ref[s].astype(jnp.float32)
         for own in range(own_rows):
             first = own * steps
             base = 0
@@ -331,25 +369,47 @@
                 )
                 out_ref[own] = line[steps:].astype(jnp.bfloat16)
                 base += width
-            rows = jnp.concatenate(
-                [coef_ref[own], jnp.zeros((8 - 1 - steps, inner), jnp.float32)], axis=0
-            )
-            for h in range(heads):
-                lanes = slice((h // heads_group) * state_size, (h // heads_group + 1) * state_size)
-                if h % 2 == 0:
-                    pair = rows[:, h * head_dim : (h + 2) * head_dim].T
-                columns = pair[(h % 2) * head_dim : (h % 2 + 1) * head_dim]
-                value = columns[:, 0:1] * state_ref[own, h]
-                for s in range(steps):
-                    value = value + columns[:, 1 + s : 2 + s] * write_ref[pl.ds(first + s, 1), lanes]
-                final_ref[own, h] = value
+            coefs_high, coefs_low = split_in(coef_ref[own, 1 : 1 + steps, :], 2)
+            writes_high, writes_low = split_in(write_ref[pl.ds(first, steps), :], 2)
+            left = stacked(coefs_high, coefs_high, coefs_low)
+            right = stacked(writes_high, writes_low, writes_high)
+            for g in range(groups):
+                fresh = lax.dot_general(
+                    left[:, g * heads_group * head_dim : (g + 1) * heads_group * head_dim],
+                    right[:, g * state_size : (g + 1) * state_size],
+                    (((0,), (0,)), ((), ())),
+                    preferred_element_type=jnp.float32,
+                )
+                for i in range(heads_group):
+                    h = g * heads_group + i
+                    kept = coef_ref[own, 0:1, pl.ds(h * head_dim, 1)]
+                    final_ref[own, h] = (
+                        kept * state_ref[own, h] + fresh[i * head_dim : (i + 1) * head_dim]
+                    )
 
     return local_kernel(
         body,
         "renew",
-        [shaped(ssm_state.shape)] + [shaped(w.shape, jnp.bfloat16) for w in windows],
-        [(a, IN_VMEM) for a in (pre, coefs, writes, *windows, ssm_state)],
-        bytes_accessed=2 << 20,
+        [shaped(ssm_state.shape), shaped((steps * rows_all, depth))]
+        + [shaped(w.shape, jnp.bfloat16) for w in windows],
+        [(a, IN_VMEM) for a in (pre, coefs, writes, *windows, ssm_state, tokens)],
+        bytes_accessed=4 << 20,
+    )
+
+
+def fetch(array, after):
+    def body(source, _, target, sem):
+        copy = pltpu.make_async_copy(source, target, sem)
+        copy.start()
+        copy.wait()
+
+    return local_kernel(
+        body,
+        "fetch",
+        shaped(array.shape, array.dtype),
+        [(array, IN_HBM), (after, IN_VMEM)],
+        [pltpu.SemaphoreType.DMA],
+        bytes_accessed=8 << 20,
     )
 
 
@@ -360,7 +420,7 @@
     rows = own_rows * owners
 
     def body(*refs):
-        weights_ref, out_ref, lhs = refs[owners:]
+        weights_ref, out_ref, sent_ref, lhs = refs[owners:]
         for slot in range(owners):
             owner = owner_of(slot, "expert")
             values = refs[slot][...].astype(jnp.float32)
@@ -368,15 +428,17 @@
                 for s in range(steps):
                     row = s * rows + owner * own_rows + own
                     lhs[pl.ds(row, 1), :] = values[own * steps + s : own * steps + s + 1]
-        out_ref[...] = jnp.dot(
+        total = jnp.dot(
             lhs[...].astype(jnp.bfloat16), weights_ref[...], preferred_element_type=jnp.float32
         )
+        out_ref[...] = total
+        sent_ref[...] = total.astype(jnp.bfloat16)
 
     return local_kernel(
         body,
         "project_out",
-        shaped((rows * steps, out_proj.shape[1])),
-        [(a, IN_VMEM) for a in (*normed, resident(out_proj))],
+        sent_narrow((rows * steps, out_proj.shape[1]), 2),
+        [(a, IN_VMEM) for a in (*normed, out_proj)],
         [pltpu.VMEM((rows * steps, inner), jnp.float32)],
         bytes_accessed=4 << 20,
     )
@@ -425,12 +487,12 @@
                 total += row_weights[e] * jnp.dot(
                     hidden_ref[e], down_ref[e, :, span(slot)], preferred_element_type=jnp.float32
                 )
-            outs[slot][...] = total
+            outs[slot][...] = total.astype(outs[slot].dtype)
 
     return local_kernel(
         body,
         "experts",
-        [shaped((many, width))] * owners,
+        sent_narrow((many, width), owners),
         [
             (a, IN_VMEM)
             for a in (*moe_in, chosen, gates, resident(expert_up), resident(expert_down))
@@ -477,34 +539,38 @@
 ):
     steps = tokens.shape[0]
     inner = conv_input.shape[1]
-    convs = (conv_input, conv_write, conv_read)
     windows = (window_input, window_write, window_read)
-    head_params, spread = spread_heads(
-        *[p.reshape(1, -1) for p in (step_bias, decay_log, skip_gain)], inner
-    )
-    projected, current = project(
+    projected = project(
         lax.axis_size("expert"),
         tokens,
         (proj_gate, proj_input, proj_write, proj_read),
         proj_step.T,
     )
+    head_params, spread, loaded = prepare(
+        *[p.reshape(1, -1) for p in (step_bias, decay_log, skip_gain)],
+        inner,
+        (conv_input, conv_write, conv_read, *windows, norm_gain.reshape(1, -1), ssm_state)
+        + (tokens, expert_ids, route_gates),
+    )
+    convs, windows = loaded[:3], loaded[3:6]
+    norm_gain, ssm_state, tokens, expert_ids, route_gates = loaded[6:]
     normed, pre, coefs, writes = mix(
         scatter_parts(projected, "expert"),
         head_params,
         spread,
         convs,
         windows,
-        norm_gain.reshape(1, -1),
+        norm_gain,
         ssm_state,
         steps,
     )
-    partial = project_out(gather(normed, "expert"), out_proj, steps)
-    ssm_final, *finals = renew(pre, coefs, writes, windows, ssm_state, steps)
-    residual = added([current] + sum_parts(partial, "tensor"))
+    partial, sent = project_out(gather(normed, "expert"), fetch(out_proj, writes), steps)
+    ssm_final, current, *finals = renew(pre, coefs, writes, windows, ssm_state, tokens)
+    residual = added([current] + sum_parts(partial, "tensor", sent))
     moe_in = gather(residual.astype(jnp.bfloat16), "expert")
     moe_sum = experts(moe_in, expert_ids, route_gates, expert_up, expert_down)
     moe_sum = added(scatter_parts(moe_sum, "expert"))
-    mixed_out = finish([residual] + sum_parts(moe_sum, "tensor"), tokens.shape)
+    mixed_out = finish([residual] + sum_parts(moe_sum, "tensor", moe_sum.astype(jnp.bfloat16)), tokens.shape)
     return (mixed_out, ssm_final, *finals)
 
 

time: 54.5 us -> 42.9 us (0.79)
  local copies, waits for them, and re-layouts: 11.5 us -> 0.01 us
  Pallas kernels: 11.3 us -> 13.8 us
  waiting for transfers between devices: 12.6 us -> 10.3 us
    unnamed x42 -> x6, local copies, waits for them, and re-layouts: 11.5 us -> 0.01 us
    pallas_call x7 -> x8, Pallas kernels: 11.3 us -> 13.8 us  [local_kernel(): pl.pallas_call(body, out_shape=out_shape, in_specs=[spec for _, spec in i...]
    ppermute x18, waiting for transfers between devices: 12.6 us -> 10.3 us  [swap(): return lax.ppermute(values, axis, [(i, i ^ distance) for i in range(size)])]
  transfers between devices with their start and end apart: 18 -> 18, of which waited for: 9 -> 9; matrix products, arithmetic and copies ran while one was open for 0% -> 0% of each run, Pallas kernels for 5% -> 12%
where the time goes in v4:
time: 42.9 us; the launch traced here: 42.7 us
  starting transfers between devices  17.7 us (41%)
  Pallas kernels  13.8 us (32%)
  waiting for transfers between devices  10.3 us (24%)
  between operations  0.76 us (2%)
    ppermute x18, starting transfers between devices, swap(): return lax.ppermute(values, axis, [(i, i ^ distance) for i in range(size)])  17.7 us
    pallas_call x8, Pallas kernels, local_kernel(): pl.pallas_call(body, out_shape=out_shape, in_specs=[spec for _, spec in i...  13.8 us
    ppermute x18, waiting for transfers between devices, swap(): return lax.ppermute(values, axis, [(i, i ^ distance) for i in range(size)])  10.3 us
  transfers between devices with their start and end apart: 18, of which 9 were waited for; matrix products, arithmetic and copies ran while one was open for 0% of the time, Pallas kernels for 12%

profile of v4, /device:TPU:0, one launch (start us, length us, event | category | flops | bytes accessed | tf_op | source)
XLA Modules:
  0.0 42.7 jit_solution(4035918800736569453)
XLA Ops:
  0.6 4.5 %project.1 = (f32[2,4640]{1,0:T(2,128)S(1)}, bf16[2,4640]{1,0:T(2,128)(2,1)S(1)}, bf16[2,4640]{1,0:T(2,128)(2,1)S(1)}, bf16[2,4640]{1,0:T(2,128)(2,1)S(1)}) custom-call(bf16[2,4,1024]{2,1,0:T(4,128)(2,1)} %refs_11_.1, bf16[32,1024]{1,0:T(8,128)(2,1)} %bitcast.7, bf16[1024,2048]{1,0:T(8,128)(2,1)} %refs_2_.1, bf16[1024,2048]{1,0:T(8,128)(2,1)} %refs_3_.2, ...), custom_call_target="tpu_custom_call" | custom-call | flops 10485760 | bytes 10485760 | tf_op jit(solution)/shard_map/project/pallas_call | solution.py:64
  5.1 2.4 %collective-permute-start = (bf16[2,4640]{1,0:T(2,128)(2,1)S(1)}, bf16[2,4640]{1,0:T(2,128)(2,1)S(1)}, u32[]{:S(2)}, u32[]{:S(2)}) collective-permute-start(bf16[2,4640]{1,0:T(2,128)(2,1)S(1)} %get-tuple-element.38), channel_id=1, source_target_pairs={{0,12},{4,8},{8,4},{12,0},{1,13},{5,9},{9,5},{13,1},{2,14},{6,10},... | collective-permute-start | bytes 55688 | tf_op jit(solution)/shard_map/ppermute | solution.py:20
  7.6 0.6 %collective-permute-start.1 = (bf16[2,4640]{1,0:T(2,128)(2,1)S(1)}, bf16[2,4640]{1,0:T(2,128)(2,1)S(1)}, u32[]{:S(2)}, u32[]{:S(2)}) collective-permute-start(bf16[2,4640]{1,0:T(2,128)(2,1)S(1)} %get-tuple-element.39), channel_id=1, source_target_pairs={{0,8},{4,12},{8,0},{12,4},{1,9},{5,13},{9,1},{13,5},{2,10},{6,14},... | collective-permute-start | bytes 55688 | tf_op jit(solution)/shard_map/ppermute | solution.py:20
  8.2 1.5 %prepare.1 = (f32[3,2048]{1,0:T(4,128)S(1)}, bf16[32,2048]{1,0:T(8,128)(2,1)S(1)}, f32[4,2048]{1,0:T(4,128)S(1)}, f32[4,256]{1,0:T(4,128)S(1)}, f32[4,256]{1,0:T...) custom-call(f32[1,32]{1,0:T(1,128)} %bitcast.9, ...), custom_call_target="tpu_custom_call" | custom-call | flops 4194304 | bytes 4194304 | tf_op jit(solution)/shard_map/prepare/pallas_call | solution.py:64
  9.8 1.6 %collective-permute-done.1.refs_2_ = bf16[2,4640]{1,0:T(2,128)(2,1)S(1)} collective-permute-done((bf16[2,4640]{1,0:T(2,128)(2,1)S(1)}, bf16[2,4640]{1,0:T(2,128)(2,1)S(1)}, u32[]{:S(2)}, u32[]{:S(2)}) %collective-permute-start.1) | collective-permute-done | bytes 18592 | tf_op jit(solution)/shard_map/ppermute | solution.py:20
  11.3 0.6 %mix.1 = (bf16[2,2048]{1,0:T(2,128)(2,1)S(1)}, f32[2,2560]{1,0:T(2,128)S(1)}, f32[1,3,2048]{2,1,0:T(4,128)S(1)}, f32[2,256]{1,0:T(2,128)S(1)}) custom-call(f32[2,4640]{1,0:T(2,128)S(1)} %get-tuple-element.37.refs_0_, bf16[2,4640]{1,0:T(2,128)(2,1)S(1)} %collective-permute-done.refs_1_, bf16[2,4640]{1,0:T(2,128)(2,1)S(1)} %collective-permute-done.1.refs_2_, ...), custom_call_target="tpu_custom_call" | custom-call | flops 67108864 | bytes 67108864 | tf_op jit(solution)/shard_map/mix/pallas_call | solution.py:64
  11.9 0.1 collective-permute-start.5
  12.0 1.1 %collective-permute-start.4 = (bf16[2,2048]{1,0:T(2,128)(2,1)S(1)}, bf16[2,2048]{1,0:T(2,128)(2,1)S(1)}, u32[]{:S(2)}, u32[]{:S(2)}) collective-permute-start(bf16[2,2048]{1,0:T(2,128)(2,1)S(1)} %get-tuple-element.56.refs_0_), channel_id=1, source_target_pairs={{0,8},{4,12},{8,0},{12,4},{1,9},{5,13},{9,1},{13,5},{2,10},{6,14},... | collective-permute-start | bytes 24584 | tf_op jit(solution)/shard_map/ppermute | solution.py:20
  13.2 0.7 %collective-permute-start.3 = (bf16[2,2048]{1,0:T(2,128)(2,1)S(1)}, bf16[2,2048]{1,0:T(2,128)(2,1)S(1)}, u32[]{:S(2)}, u32[]{:S(2)}) collective-permute-start(bf16[2,2048]{1,0:T(2,128)(2,1)S(1)} %get-tuple-element.56.refs_0_), channel_id=1, source_target_pairs={{0,4},{4,0},{8,12},{12,8},{1,5},{5,1},{9,13},{13,9},{2,6},{6,2},{1... | collective-permute-start | bytes 24584 | tf_op jit(solution)/shard_map/ppermute | solution.py:20
  13.9 2.3 %fetch.1.refs_4_ = bf16[2048,1024]{1,0:T(8,128)(2,1)S(1)} custom-call(bf16[2048,1024]{1,0:T(8,128)(2,1)} %source.1, f32[2,256]{1,0:T(2,128)S(1)} %get-tuple-element.53.write_ref._), custom_call_target="tpu_custom_call" | custom-call | flops 8388608 | bytes 8388608 | tf_op jit(solution)/shard_map/fetch/pallas_call | solution.py:64
  16.3 0.6 %project_out.1 = (f32[8,1024]{1,0:T(8,128)S(1)}, bf16[8,1024]{1,0:T(8,128)(2,1)S(1)}) custom-call(bf16[2,2048]{1,0:T(2,128)(2,1)S(1)} %get-tuple-element.56.refs_0_, bf16[2,2048]{1,0:T(2,128)(2,1)S(1)} %collective-permute-done.3.refs_1_, bf16[2,2048]{1,0:T(2,128)(2,1)S(1)} %collective-permute-done.4.refs_2_, ...), custom_call_target="tpu_custom_call" | custom-call | flops 4194304 | bytes 4194304 | tf_op jit(solution)/shard_map/project_out/pallas_call | solution.py:64
  16.9 3.6 %collective-permute-start.8 = (bf16[8,1024]{1,0:T(8,128)(2,1)S(1)}, bf16[8,1024]{1,0:T(8,128)(2,1)S(1)}, u32[]{:S(2)}, u32[]{:S(2)}) collective-permute-start(bf16[8,1024]{1,0:T(8,128)(2,1)S(1)} %get-tuple-element.58), channel_id=1, source_target_pairs={{0,3},{1,2},{2,1},{3,0},{4,7},{5,6},{6,5},{7,4},{8,11},{9,10},{10,... | collective-permute-start | bytes 49160 | tf_op jit(solution)/shard_map/ppermute | solution.py:20
  20.5 0.8 %collective-permute-start.6 = (bf16[8,1024]{1,0:T(8,128)(2,1)S(1)}, bf16[8,1024]{1,0:T(8,128)(2,1)S(1)}, u32[]{:S(2)}, u32[]{:S(2)}) collective-permute-start(bf16[8,1024]{1,0:T(8,128)(2,1)S(1)} %get-tuple-element.58), channel_id=1, source_target_pairs={{0,1},{1,0},{2,3},{3,2},{4,5},{5,4},{6,7},{7,6},{8,9},{9,8},{10,11... | collective-permute-start | bytes 49160 | tf_op jit(solution)/shard_map/ppermute | solution.py:20
  21.3 1.3 %renew.1 = (f32[1,32,64,128]{3,2,1,0:T(8,128)}, f32[8,1024]{1,0:T(8,128)S(1)}, bf16[1,3,2048]{2,1,0:T(4,128)(2,1)}, bf16[1,3,256]{2,1,0:T(4,128)(2,1)}, bf16[1,3,256]{2,1,0:T(4,128)(2,1)}) custom-call(f32[2,2560]{1,0:T(2,128)S(1)} %get-tuple-element.51.pre_ref, f32[1,3,2048]{2,1,0:T(4,128)S(1)} %get-tuple-element.52.coef_ref, ...), custom_call_target="tpu_custom_call" | custom-call | flops 4194304 | bytes 4194304 | tf_op jit(solution)/shard_map/renew/pallas_call | solution.py:64
  22.6 2.5 %collective-permute-done.7 = bf16[8,1024]{1,0:T(8,128)(2,1)S(1)} collective-permute-done((bf16[8,1024]{1,0:T(8,128)(2,1)S(1)}, bf16[8,1024]{1,0:T(8,128)(2,1)S(1)}, u32[]{:S(2)}, u32[]{:S(2)}) %collective-permute-start.7) | collective-permute-done | bytes 16416 | tf_op jit(solution)/shard_map/ppermute | solution.py:20
  25.3 0.7 %collective-permute-start.10 = (bf16[8,1024]{1,0:T(8,128)(2,1)S(1)}, bf16[8,1024]{1,0:T(8,128)(2,1)S(1)}, u32[]{:S(2)}, u32[]{:S(2)}) collective-permute-start(bf16[8,1024]{1,0:T(8,128)(2,1)S(1)} %get-tuple-element.71.refs_0_), channel_id=1, source_target_pairs={{0,8},{4,12},{8,0},{12,4},{1,9},{5,13},{9,1},{13,5},{2,10},{6,14},... | collective-permute-start | bytes 49160 | tf_op jit(solution)/shard_map/ppermute | solution.py:20
  26.0 1.1 %collective-permute-start.9 = (bf16[8,1024]{1,0:T(8,128)(2,1)S(1)}, bf16[8,1024]{1,0:T(8,128)(2,1)S(1)}, u32[]{:S(2)}, u32[]{:S(2)}) collective-permute-start(bf16[8,1024]{1,0:T(8,128)(2,1)S(1)} %get-tuple-element.71.refs_0_), channel_id=1, source_target_pairs={{0,4},{4,0},{8,12},{12,8},{1,5},{5,1},{9,13},{13,9},{2,6},{6,2},{1... | collective-permute-start | bytes 49160 | tf_op jit(solution)/shard_map/ppermute | solution.py:20
  27.1 1.3 %collective-permute-done.11.refs_3_ = bf16[8,1024]{1,0:T(8,128)(2,1)S(1)} collective-permute-done((bf16[8,1024]{1,0:T(8,128)(2,1)S(1)}, bf16[8,1024]{1,0:T(8,128)(2,1)S(1)}, u32[]{:S(2)}, u32[]{:S(2)}) %collective-permute-start.11) | collective-permute-done | bytes 16416 | tf_op jit(solution)/shard_map/ppermute | solution.py:20
  28.4 0.7 %collective-permute-done.10.refs_2_ = bf16[8,1024]{1,0:T(8,128)(2,1)S(1)} collective-permute-done((bf16[8,1024]{1,0:T(8,128)(2,1)S(1)}, bf16[8,1024]{1,0:T(8,128)(2,1)S(1)}, u32[]{:S(2)}, u32[]{:S(2)}) %collective-permute-start.10) | collective-permute-done | bytes 16416 | tf_op jit(solution)/shard_map/ppermute | solution.py:20
  29.1 2.3 %experts.1 = (f32[8,1024]{1,0:T(8,128)S(1)}, bf16[8,1024]{1,0:T(8,128)(2,1)S(1)}, bf16[8,1024]{1,0:T(8,128)(2,1)S(1)}, bf16[8,1024]{1,0:T(8,128)(2,1)S(1)}) custom-call(bf16[8,1024]{1,0:T(8,128)(2,1)S(1)} %get-tuple-element.71.refs_0_, bf16[8,1024]{1,0:T(8,128)(2,1)S(1)} %collective-permute-done.9.refs_1_, ...), custom_call_target="tpu_custom_call" | custom-call | flops 16777216 | bytes 16777216 | tf_op jit(solution)/shard_map/experts/pallas_call | solution.py:64
  31.4 0.6 %collective-permute-start.12 = (bf16[8,1024]{1,0:T(8,128)(2,1)S(1)}, bf16[8,1024]{1,0:T(8,128)(2,1)S(1)}, u32[]{:S(2)}, u32[]{:S(2)}) collective-permute-start(bf16[8,1024]{1,0:T(8,128)(2,1)S(1)} %get-tuple-element.62), channel_id=1, source_target_pairs={{0,12},{4,8},{8,4},{12,0},{1,13},{5,9},{9,5},{13,1},{2,14},{6,10},... | collective-permute-start | bytes 49160 | tf_op jit(solution)/shard_map/ppermute | solution.py:20
  32.0 0.6 %collective-permute-start.13 = (bf16[8,1024]{1,0:T(8,128)(2,1)S(1)}, bf16[8,1024]{1,0:T(8,128)(2,1)S(1)}, u32[]{:S(2)}, u32[]{:S(2)}) collective-permute-start(bf16[8,1024]{1,0:T(8,128)(2,1)S(1)} %get-tuple-element.63), channel_id=1, source_target_pairs={{0,8},{4,12},{8,0},{12,4},{1,9},{5,13},{9,1},{13,5},{2,10},{6,14},... | collective-permute-start | bytes 49160 | tf_op jit(solution)/shard_map/ppermute | solution.py:20
  32.6 0.7 %collective-permute-start.14 = (bf16[8,1024]{1,0:T(8,128)(2,1)S(1)}, bf16[8,1024]{1,0:T(8,128)(2,1)S(1)}, u32[]{:S(2)}, u32[]{:S(2)}) collective-permute-start(bf16[8,1024]{1,0:T(8,128)(2,1)S(1)} %get-tuple-element.64), channel_id=1, source_target_pairs={{0,4},{4,0},{8,12},{12,8},{1,5},{5,1},{9,13},{13,9},{2,6},{6,2},{1... | collective-permute-start | bytes 49160 | tf_op jit(solution)/shard_map/ppermute | solution.py:20
  33.3 1.3 %collective-permute-done.12 = bf16[8,1024]{1,0:T(8,128)(2,1)S(1)} collective-permute-done((bf16[8,1024]{1,0:T(8,128)(2,1)S(1)}, bf16[8,1024]{1,0:T(8,128)(2,1)S(1)}, u32[]{:S(2)}, u32[]{:S(2)}) %collective-permute-start.12) | collective-permute-done | bytes 16416 | tf_op jit(solution)/shard_map/ppermute | solution.py:20
  34.6 1.1 %collective-permute-done.13 = bf16[8,1024]{1,0:T(8,128)(2,1)S(1)} collective-permute-done((bf16[8,1024]{1,0:T(8,128)(2,1)S(1)}, bf16[8,1024]{1,0:T(8,128)(2,1)S(1)}, u32[]{:S(2)}, u32[]{:S(2)}) %collective-permute-start.13) | collective-permute-done | bytes 16416 | tf_op jit(solution)/shard_map/ppermute | solution.py:20
  35.7 1.5 %collective-permute-start.17 = (bf16[8,1024]{1,0:T(8,128)(2,1)S(1)}, bf16[8,1024]{1,0:T(8,128)(2,1)S(1)}, u32[]{:S(2)}, u32[]{:S(2)}) collective-permute-start(bf16[8,1024]{1,0:T(8,128)(2,1)S(1)} %get-tuple-element.69), channel_id=1, source_target_pairs={{0,3},{1,2},{2,1},{3,0},{4,7},{5,6},{6,5},{7,4},{8,11},{9,10},{10,... | collective-permute-start | bytes 49160 | tf_op jit(solution)/shard_map/ppermute | solution.py:20
  37.3 0.6 %collective-permute-start.16 = (bf16[8,1024]{1,0:T(8,128)(2,1)S(1)}, bf16[8,1024]{1,0:T(8,128)(2,1)S(1)}, u32[]{:S(2)}, u32[]{:S(2)}) collective-permute-start(bf16[8,1024]{1,0:T(8,128)(2,1)S(1)} %get-tuple-element.69), channel_id=1, source_target_pairs={{0,2},{1,3},{2,0},{3,1},{4,6},{5,7},{6,4},{7,5},{8,10},{9,11},{10,... | collective-permute-start | bytes 49160 | tf_op jit(solution)/shard_map/ppermute | solution.py:20
  37.9 2.3 %collective-permute-start.15 = (bf16[8,1024]{1,0:T(8,128)(2,1)S(1)}, bf16[8,1024]{1,0:T(8,128)(2,1)S(1)}, u32[]{:S(2)}, u32[]{:S(2)}) collective-permute-start(bf16[8,1024]{1,0:T(8,128)(2,1)S(1)} %get-tuple-element.69), channel_id=1, source_target_pairs={{0,1},{1,0},{2,3},{3,2},{4,5},{5,4},{6,7},{7,6},{8,9},{9,8},{10,11... | collective-permute-start | bytes 49160 | tf_op jit(solution)/shard_map/ppermute | solution.py:20
  40.2 1.1 %collective-permute-done.17.refs_4_ = bf16[8,1024]{1,0:T(8,128)(2,1)S(1)} collective-permute-done((bf16[8,1024]{1,0:T(8,128)(2,1)S(1)}, bf16[8,1024]{1,0:T(8,128)(2,1)S(1)}, u32[]{:S(2)}, u32[]{:S(2)}) %collective-permute-start.17) | collective-permute-done | bytes 16416 | tf_op jit(solution)/shard_map/ppermute | solution.py:20
  41.3 0.6 %collective-permute-done.16.refs_3_ = bf16[8,1024]{1,0:T(8,128)(2,1)S(1)} collective-permute-done((bf16[8,1024]{1,0:T(8,128)(2,1)S(1)}, bf16[8,1024]{1,0:T(8,128)(2,1)S(1)}, u32[]{:S(2)}, u32[]{:S(2)}) %collective-permute-start.16) | collective-permute-done | bytes 16416 | tf_op jit(solution)/shard_map/ppermute | solution.py:20
  41.9 0.2 collective-permute-done.15.refs_2_
  42.1 0.6 %finish.1 = bf16[2,4,1024]{2,1,0:T(4,128)(2,1)} custom-call(f32[8,1024]{1,0:T(8,128)S(1)} %get-tuple-element.72.refs_0_, f32[8,1024]{1,0:T(8,128)S(1)} %get-tuple-element.70.refs_1_, bf16[8,1024]{1,0:T(8,128)(2,1)S(1)} %collective-permute-done.15.refs_2_, bf16[8,1024]{1,0:T(8,128)(2,1)S(1)} %collective-permute-done.16.refs_3_, ...), custom_call_target="tpu_custom_call" | custom-call | flops 1048576 | bytes 1048576 | tf_op jit(solution)/shard_map/finish/pallas_call | solution.py:64
  (21 shorter events, 0.2 us)
Async XLA Ops:
  0.6 28.4 %copy-start = (bf16[4,256,4096]{2,1,0:T(8,128)(2,1)S(1)}, bf16[4,256,4096]{2,1,0:T(8,128)(2,1)}, u32[]{:S(2)}) copy-start(bf16[4,256,4096]{2,1,0:T(8,128)(2,1)} %refs_7_.3) | copy-start | bytes 25165828
  5.1 4.6 %collective-permute-start = (bf16[2,4640]{1,0:T(2,128)(2,1)S(1)}, bf16[2,4640]{1,0:T(2,128)(2,1)S(1)}, u32[]{:S(2)}, u32[]{:S(2)}) collective-permute-start(bf16[2,4640]{1,0:T(2,128)(2,1)S(1)} %get-tuple-element.38), channel_id=1, source_target_pairs={{0,12},{4,8},{8,4},{12,0},{1,13},{5,9},{9,5},{13,1},{2,14},{6,10},... | collective-permute-start | bytes 55688 | tf_op jit(solution)/shard_map/ppermute | solution.py:20
  7.6 3.8 %collective-permute-start.1 = (bf16[2,4640]{1,0:T(2,128)(2,1)S(1)}, bf16[2,4640]{1,0:T(2,128)(2,1)S(1)}, u32[]{:S(2)}, u32[]{:S(2)}) collective-permute-start(bf16[2,4640]{1,0:T(2,128)(2,1)S(1)} %get-tuple-element.39), channel_id=1, source_target_pairs={{0,8},{4,12},{8,0},{12,4},{1,9},{5,13},{9,1},{13,5},{2,10},{6,14},... | collective-permute-start | bytes 55688 | tf_op jit(solution)/shard_map/ppermute | solution.py:20
  8.2 3.1 %collective-permute-start.2 = (bf16[2,4640]{1,0:T(2,128)(2,1)S(1)}, bf16[2,4640]{1,0:T(2,128)(2,1)S(1)}, u32[]{:S(2)}, u32[]{:S(2)}) collective-permute-start(bf16[2,4640]{1,0:T(2,128)(2,1)S(1)} %get-tuple-element.40), channel_id=1, source_target_pairs={{0,4},{4,0},{8,12},{12,8},{1,5},{5,1},{9,13},{13,9},{2,6},{6,2},{1... | collective-permute-start | bytes 55688 | tf_op jit(solution)/shard_map/ppermute | solution.py:20
  11.3 17.7 %slice-start = ((s8[8388608]{0:T(1024)(128)(4,1)}), s8[4194304]{0:T(1024)(128)(4,1)S(1)}, s32[]{:S(2)}) async-start(s8[8388608]{0:T(1024)(128)(4,1)} %bitcast.5), calls=%async_computation | async-start | bytes 8388608
  11.9 4.3 %collective-permute-start.5 = (bf16[2,2048]{1,0:T(2,128)(2,1)S(1)}, bf16[2,2048]{1,0:T(2,128)(2,1)S(1)}, u32[]{:S(2)}, u32[]{:S(2)}) collective-permute-start(bf16[2,2048]{1,0:T(2,128)(2,1)S(1)} %get-tuple-element.56.refs_0_), channel_id=1, source_target_pairs={{0,12},{4,8},{8,4},{12,0},{1,13},{5,9},{9,5},{13,1},{2,14},{6,10},... | collective-permute-start | bytes 24584 | tf_op jit(solution)/shard_map/ppermute | solution.py:20
  12.0 4.2 %collective-permute-start.4 = (bf16[2,2048]{1,0:T(2,128)(2,1)S(1)}, bf16[2,2048]{1,0:T(2,128)(2,1)S(1)}, u32[]{:S(2)}, u32[]{:S(2)}) collective-permute-start(bf16[2,2048]{1,0:T(2,128)(2,1)S(1)} %get-tuple-element.56.refs_0_), channel_id=1, source_target_pairs={{0,8},{4,12},{8,0},{12,4},{1,9},{5,13},{9,1},{13,5},{2,10},{6,14},... | collective-permute-start | bytes 24584 | tf_op jit(solution)/shard_map/ppermute | solution.py:20
  13.2 3.1 %collective-permute-start.3 = (bf16[2,2048]{1,0:T(2,128)(2,1)S(1)}, bf16[2,2048]{1,0:T(2,128)(2,1)S(1)}, u32[]{:S(2)}, u32[]{:S(2)}) collective-permute-start(bf16[2,2048]{1,0:T(2,128)(2,1)S(1)} %get-tuple-element.56.refs_0_), channel_id=1, source_target_pairs={{0,4},{4,0},{8,12},{12,8},{1,5},{5,1},{9,13},{13,9},{2,6},{6,2},{1... | collective-permute-start | bytes 24584 | tf_op jit(solution)/shard_map/ppermute | solution.py:20
  13.9 15.2 %slice-start.1 = ((s8[8388608]{0:T(1024)(128)(4,1)}), s8[4194304]{0:T(1024)(128)(4,1)S(1)}, s32[]{:S(2)}) async-start(s8[8388608]{0:T(1024)(128)(4,1)} %bitcast.5), calls=%async_computation.1 | async-start | bytes 8388608
  16.9 5.7 %collective-permute-start.8 = (bf16[8,1024]{1,0:T(8,128)(2,1)S(1)}, bf16[8,1024]{1,0:T(8,128)(2,1)S(1)}, u32[]{:S(2)}, u32[]{:S(2)}) collective-permute-start(bf16[8,1024]{1,0:T(8,128)(2,1)S(1)} %get-tuple-element.58), channel_id=1, source_target_pairs={{0,3},{1,2},{2,1},{3,0},{4,7},{5,6},{6,5},{7,4},{8,11},{9,10},{10,... | collective-permute-start | bytes 49160 | tf_op jit(solution)/shard_map/ppermute | solution.py:20
  20.5 4.6 %collective-permute-start.7 = (bf16[8,1024]{1,0:T(8,128)(2,1)S(1)}, bf16[8,1024]{1,0:T(8,128)(2,1)S(1)}, u32[]{:S(2)}, u32[]{:S(2)}) collective-permute-start(bf16[8,1024]{1,0:T(8,128)(2,1)S(1)} %get-tuple-element.58), channel_id=1, source_target_pairs={{0,2},{1,3},{2,0},{3,1},{4,6},{5,7},{6,4},{7,5},{8,10},{9,11},{10,... | collective-permute-start | bytes 49160 | tf_op jit(solution)/shard_map/ppermute | solution.py:20
  20.5 4.6 %collective-permute-start.6 = (bf16[8,1024]{1,0:T(8,128)(2,1)S(1)}, bf16[8,1024]{1,0:T(8,128)(2,1)S(1)}, u32[]{:S(2)}, u32[]{:S(2)}) collective-permute-start(bf16[8,1024]{1,0:T(8,128)(2,1)S(1)} %get-tuple-element.58), channel_id=1, source_target_pairs={{0,1},{1,0},{2,3},{3,2},{4,5},{5,4},{6,7},{7,6},{8,9},{9,8},{10,11... | collective-permute-start | bytes 49160 | tf_op jit(solution)/shard_map/ppermute | solution.py:20
  25.2 3.2 %collective-permute-start.11 = (bf16[8,1024]{1,0:T(8,128)(2,1)S(1)}, bf16[8,1024]{1,0:T(8,128)(2,1)S(1)}, u32[]{:S(2)}, u32[]{:S(2)}) collective-permute-start(bf16[8,1024]{1,0:T(8,128)(2,1)S(1)} %get-tuple-element.71.refs_0_), channel_id=1, source_target_pairs={{0,12},{4,8},{8,4},{12,0},{1,13},{5,9},{9,5},{13,1},{2,14},{6,10},... | collective-permute-start | bytes 49160 | tf_op jit(solution)/shard_map/ppermute | solution.py:20
  25.3 3.8 %collective-permute-start.10 = (bf16[8,1024]{1,0:T(8,128)(2,1)S(1)}, bf16[8,1024]{1,0:T(8,128)(2,1)S(1)}, u32[]{:S(2)}, u32[]{:S(2)}) collective-permute-start(bf16[8,1024]{1,0:T(8,128)(2,1)S(1)} %get-tuple-element.71.refs_0_), channel_id=1, source_target_pairs={{0,8},{4,12},{8,0},{12,4},{1,9},{5,13},{9,1},{13,5},{2,10},{6,14},... | collective-permute-start | bytes 49160 | tf_op jit(solution)/shard_map/ppermute | solution.py:20
  26.0 3.1 %collective-permute-start.9 = (bf16[8,1024]{1,0:T(8,128)(2,1)S(1)}, bf16[8,1024]{1,0:T(8,128)(2,1)S(1)}, u32[]{:S(2)}, u32[]{:S(2)}) collective-permute-start(bf16[8,1024]{1,0:T(8,128)(2,1)S(1)} %get-tuple-element.71.refs_0_), channel_id=1, source_target_pairs={{0,4},{4,0},{8,12},{12,8},{1,5},{5,1},{9,13},{13,9},{2,6},{6,2},{1... | collective-permute-start | bytes 49160 | tf_op jit(solution)/shard_map/ppermute | solution.py:20
  31.4 3.2 %collective-permute-start.12 = (bf16[8,1024]{1,0:T(8,128)(2,1)S(1)}, bf16[8,1024]{1,0:T(8,128)(2,1)S(1)}, u32[]{:S(2)}, u32[]{:S(2)}) collective-permute-start(bf16[8,1024]{1,0:T(8,128)(2,1)S(1)} %get-tuple-element.62), channel_id=1, source_target_pairs={{0,12},{4,8},{8,4},{12,0},{1,13},{5,9},{9,5},{13,1},{2,14},{6,10},... | collective-permute-start | bytes 49160 | tf_op jit(solution)/shard_map/ppermute | solution.py:20
  32.0 3.7 %collective-permute-start.13 = (bf16[8,1024]{1,0:T(8,128)(2,1)S(1)}, bf16[8,1024]{1,0:T(8,128)(2,1)S(1)}, u32[]{:S(2)}, u32[]{:S(2)}) collective-permute-start(bf16[8,1024]{1,0:T(8,128)(2,1)S(1)} %get-tuple-element.63), channel_id=1, source_target_pairs={{0,8},{4,12},{8,0},{12,4},{1,9},{5,13},{9,1},{13,5},{2,10},{6,14},... | collective-permute-start | bytes 49160 | tf_op jit(solution)/shard_map/ppermute | solution.py:20
  32.6 3.1 %collective-permute-start.14 = (bf16[8,1024]{1,0:T(8,128)(2,1)S(1)}, bf16[8,1024]{1,0:T(8,128)(2,1)S(1)}, u32[]{:S(2)}, u32[]{:S(2)}) collective-permute-start(bf16[8,1024]{1,0:T(8,128)(2,1)S(1)} %get-tuple-element.64), channel_id=1, source_target_pairs={{0,4},{4,0},{8,12},{12,8},{1,5},{5,1},{9,13},{13,9},{2,6},{6,2},{1... | collective-permute-start | bytes 49160 | tf_op jit(solution)/shard_map/ppermute | solution.py:20
  35.7 5.6 %collective-permute-start.17 = (bf16[8,1024]{1,0:T(8,128)(2,1)S(1)}, bf16[8,1024]{1,0:T(8,128)(2,1)S(1)}, u32[]{:S(2)}, u32[]{:S(2)}) collective-permute-start(bf16[8,1024]{1,0:T(8,128)(2,1)S(1)} %get-tuple-element.69), channel_id=1, source_target_pairs={{0,3},{1,2},{2,1},{3,0},{4,7},{5,6},{6,5},{7,4},{8,11},{9,10},{10,... | collective-permute-start | bytes 49160 | tf_op jit(solution)/shard_map/ppermute | solution.py:20
  37.3 4.7 %collective-permute-start.16 = (bf16[8,1024]{1,0:T(8,128)(2,1)S(1)}, bf16[8,1024]{1,0:T(8,128)(2,1)S(1)}, u32[]{:S(2)}, u32[]{:S(2)}) collective-permute-start(bf16[8,1024]{1,0:T(8,128)(2,1)S(1)} %get-tuple-element.69), channel_id=1, source_target_pairs={{0,2},{1,3},{2,0},{3,1},{4,6},{5,7},{6,4},{7,5},{8,10},{9,11},{10,... | collective-permute-start | bytes 49160 | tf_op jit(solution)/shard_map/ppermute | solution.py:20
  37.9 4.2 %collective-permute-start.15 = (bf16[8,1024]{1,0:T(8,128)(2,1)S(1)}, bf16[8,1024]{1,0:T(8,128)(2,1)S(1)}, u32[]{:S(2)}, u32[]{:S(2)}) collective-permute-start(bf16[8,1024]{1,0:T(8,128)(2,1)S(1)} %get-tuple-element.69), channel_id=1, source_target_pairs={{0,1},{1,0},{2,3},{3,2},{4,5},{5,4},{6,7},{7,6},{8,9},{9,8},{10,11... | collective-permute-start | bytes 49160 | tf_op jit(solution)/shard_map/ppermute | solution.py:20

commit v5 on v4

--- a/solution.py
+++ b/solution.py
@@ -28,11 +28,12 @@
     return [values] + [swap(values, axis, d) for d in range(1, size)]
 
 
-def sum_parts(values, axis, sent=None):
+def sum_parts(values, axis, sent, order):
     if not pairwise(axis):
         return [lax.psum(values, axis)]
-    sent = values if sent is None else sent
-    return [values] + [swap(sent, axis, d) for d in range(1, lax.axis_size(axis))]
+    if lax.axis_size(axis) != 4:
+        return [values] + [swap(sent, axis, d) for d in range(1, lax.axis_size(axis))]
+    return [values] + [lax.ppermute(sent, axis, list(enumerate(p))) for p in order]
 
 
 def scatter_parts(blocks, axis):
@@ -57,7 +58,9 @@
 IN_VMEM = pl.BlockSpec(memory_space=pltpu.VMEM)
 IN_HBM = pl.BlockSpec(memory_space=pltpu.HBM)
 CHUNK = 512 * 1024
-MIX_COST = 64 << 20
+MIX_COST = 4 << 20
+FIRST = 4
+NEAR = 1
 
 
 def local_kernel(body, name, out_shape, ins, scratch=(), bytes_accessed=1 << 20):
@@ -197,15 +200,18 @@
     return jnp.concatenate(parts, axis=0).astype(jnp.bfloat16)
 
 
-def prepare(step_bias, decay_log, skip_gain, inner, arrays):
+def prepare(step_bias, decay_log, skip_gain, inner, arrays, weights, rows_first):
     heads = step_bias.shape[1]
     head_dim = inner // heads
-    count = 3 + len(arrays)
+    count = 4 + len(arrays)
+    wanted = [shaped(a.shape, a.dtype) for a in arrays]
+    wanted.append(shaped((rows_first, weights.shape[1]), weights.dtype))
 
     def body(*refs):
         sources, (params_ref, spread_ref), outs = refs[:count], refs[count : count + 2], refs[count + 2 :]
         loaded, sems = outs[:-2], outs[-1]
         rows_ref = outs[-2]
+        sources = [*sources[:-1], sources[-1].at[pl.ds(0, rows_first)]]
         targets = [rows_ref.at[pl.ds(i, 1)] for i in range(3)] + list(loaded)
         copies = [
             pltpu.make_async_copy(source, target, sems.at[i])
@@ -233,8 +239,8 @@
         body,
         "prepare",
         [shaped((3, inner)), shaped((heads, inner), jnp.bfloat16)]
-        + [shaped(a.shape, a.dtype) for a in arrays],
-        [(a, IN_HBM) for a in (step_bias, decay_log, skip_gain, *arrays)],
+        + wanted,
+        [(a, IN_HBM) for a in (step_bias, decay_log, skip_gain, *arrays, weights)],
         [pltpu.VMEM((3, heads), jnp.float32), pltpu.SemaphoreType.DMA((count,))],
         bytes_accessed=4 << 20,
     )
@@ -397,30 +403,32 @@
     )
 
 
-def fetch(array, after):
+def fetch(array, start, after):
+    rows = array.shape[0] - start
+
     def body(source, _, target, sem):
-        copy = pltpu.make_async_copy(source, target, sem)
+        copy = pltpu.make_async_copy(source.at[pl.ds(start, rows)], target, sem)
         copy.start()
         copy.wait()
 
     return local_kernel(
         body,
         "fetch",
-        shaped(array.shape, array.dtype),
+        shaped((rows, array.shape[1]), array.dtype),
         [(array, IN_HBM), (after, IN_VMEM)],
         [pltpu.SemaphoreType.DMA],
         bytes_accessed=8 << 20,
     )
 
 
-def project_out(normed, out_proj, steps):
+def project_out(normed, parts, steps):
     owners = len(normed)
     block, inner = normed[0].shape
     own_rows = block // steps
     rows = own_rows * owners
 
     def body(*refs):
-        weights_ref, out_ref, sent_ref, lhs = refs[owners:]
+        out_ref, sent_ref, lhs = refs[owners + len(parts) :]
         for slot in range(owners):
             owner = owner_of(slot, "expert")
             values = refs[slot][...].astype(jnp.float32)
@@ -428,77 +436,140 @@
                 for s in range(steps):
                     row = s * rows + owner * own_rows + own
                     lhs[pl.ds(row, 1), :] = values[own * steps + s : own * steps + s + 1]
-        total = jnp.dot(
-            lhs[...].astype(jnp.bfloat16), weights_ref[...], preferred_element_type=jnp.float32
-        )
+        products = []
+        base = 0
+        for ref in refs[owners : owners + len(parts)]:
+            values = lhs[:, pl.ds(base, ref.shape[0])].astype(jnp.bfloat16)
+            products.append(jnp.dot(values, ref[...], preferred_element_type=jnp.float32))
+            base += ref.shape[0]
+        total = added(products)
         out_ref[...] = total
         sent_ref[...] = total.astype(jnp.bfloat16)
 
     return local_kernel(
         body,
         "project_out",
-        sent_narrow((rows * steps, out_proj.shape[1]), 2),
-        [(a, IN_VMEM) for a in (*normed, out_proj)],
+        sent_narrow((rows * steps, parts[0].shape[1]), 2),
+        [(a, IN_VMEM) for a in (*normed, *parts)],
         [pltpu.VMEM((rows * steps, inner), jnp.float32)],
         bytes_accessed=4 << 20,
     )
 
 
-def experts(moe_in, chosen, gates, expert_up, expert_down):
-    owners = len(moe_in)
+def slot_rows(slot, width):
+    start = owner_of(slot, "expert") * width
+    return pl.ds(pl.multiple_of(start, width) if pairwise("expert") else start, width)
+
+
+def expert_near(moe_in, expert_up):
+    count = len(moe_in)
     many, width = moe_in[0].shape
-    steps, rows, _ = chosen.shape
     local_experts, _, hidden_width = expert_up.shape
 
     def body(*refs):
-        chosen_ref, gates_ref, up_ref, down_ref = refs[owners : owners + 4]
-        outs, hidden_ref = refs[owners + 4 : -1], refs[-1]
-        first = lax.axis_index("expert") * local_experts
-
-        def span(slot):
-            start = owner_of(slot, "expert") * width
-            return pl.ds(pl.multiple_of(start, width) if pairwise("expert") else start, width)
-
-        row_weights = []
+        up_ref, out_ref = refs[count:]
         for e in range(local_experts):
-            total = jnp.zeros((many, hidden_width), jnp.float32)
-            for slot in range(owners):
+            out_ref[e] = added(
+                [
+                    jnp.dot(
+                        refs[slot][...],
+                        up_ref[e, slot_rows(slot, width), :],
+                        preferred_element_type=jnp.float32,
+                    )
+                    for slot in range(count)
+                ]
+            )
+
+    return local_kernel(
+        body,
+        "expert_near",
+        shaped((local_experts, many, hidden_width)),
+        [(a, IN_VMEM) for a in (*moe_in, expert_up)],
+        bytes_accessed=4 << 20,
+    )
+
+
+def row_weights(chosen_ref, gates_ref, local_experts):
+    first = lax.axis_index("expert") * local_experts
+    steps = chosen_ref.shape[0]
+    return [
+        jnp.concatenate(
+            [
+                jnp.sum(
+                    jnp.where(chosen_ref[s] == first + e, gates_ref[s], 0.0),
+                    axis=1,
+                    keepdims=True,
+                )
+                for s in range(steps)
+            ],
+            axis=0,
+        )
+        for e in range(local_experts)
+    ]
+
+
+def gated_sum(hidden_ref, weights, down_ref, columns):
+    return added(
+        [
+            weights[e]
+            * jnp.dot(
+                hidden_ref[e], down_ref[e, :, columns], preferred_element_type=jnp.float32
+            )
+            for e in range(len(weights))
+        ]
+    )
+
+
+def experts_far(near, moe_in, chosen, gates, expert_up, expert_down, owners):
+    count = len(moe_in)
+    many, width = moe_in[0].shape
+    local_experts, _, hidden_width = expert_up.shape
+    far = range(1, owners)
+
+    def body(*refs):
+        near_ref, chosen_ref, gates_ref, up_ref, down_ref, hidden_ref, *outs = refs[count:]
+        for e in range(local_experts):
+            total = near_ref[e]
+            for i in range(count):
                 total += jnp.dot(
-                    refs[slot][...], up_ref[e, span(slot), :], preferred_element_type=jnp.float32
+                    refs[i][...],
+                    up_ref[e, slot_rows(owners - count + i, width), :],
+                    preferred_element_type=jnp.float32,
                 )
             total = jnp.maximum(total, 0.0)
             hidden_ref[e] = (total * total).astype(jnp.bfloat16)
-            row_weights.append(
-                jnp.concatenate(
-                    [
-                        jnp.sum(
-                            jnp.where(chosen_ref[s] == first + e, gates_ref[s], 0.0),
-                            axis=1,
-                            keepdims=True,
-                        )
-                        for s in range(steps)
-                    ],
-                    axis=0,
-                )
-            )
-        for slot in range(owners):
-            total = jnp.zeros((many, width), jnp.float32)
-            for e in range(local_experts):
-                total += row_weights[e] * jnp.dot(
-                    hidden_ref[e], down_ref[e, :, span(slot)], preferred_element_type=jnp.float32
-                )
-            outs[slot][...] = total.astype(outs[slot].dtype)
+        weights = row_weights(chosen_ref, gates_ref, local_experts)
+        for slot, out in zip(far, outs):
+            total = gated_sum(hidden_ref, weights, down_ref, slot_rows(slot, width))
+            out[...] = total.astype(out.dtype)
+
+    hidden, *outs = local_kernel(
+        body,
+        "experts_far",
+        [shaped((local_experts, many, hidden_width), jnp.bfloat16)]
+        + sent_narrow((many, width), 1 + len(far))[1:],
+        [(a, IN_VMEM) for a in (*moe_in, near, chosen, gates, expert_up, expert_down)],
+        bytes_accessed=16 << 20,
+    )
+    return hidden, outs
+
+
+def experts_close(hidden, chosen, gates, expert_down, owners):
+    local_experts, many, _ = hidden.shape
+    width = expert_down.shape[2] // owners
+
+    def body(hidden_ref, chosen_ref, gates_ref, down_ref, *outs):
+        weights = row_weights(chosen_ref, gates_ref, local_experts)
+        for slot, out in enumerate(outs):
+            total = gated_sum(hidden_ref, weights, down_ref, slot_rows(slot, width))
+            out[...] = total.astype(out.dtype)
 
     return local_kernel(
         body,
-        "experts",
-        sent_narrow((many, width), owners),
-        [
-            (a, IN_VMEM)
-            for a in (*moe_in, chosen, gates, resident(expert_up), resident(expert_down))
-        ],
-        [pltpu.VMEM((local_experts, many, hidden_width), jnp.bfloat16)],
-        bytes_accessed=16 << 20,
+        "experts_close",
+        sent_narrow((many, width), 1),
+        [(a, IN_VMEM) for a in (hidden, chosen, gates, expert_down)],
+        bytes_accessed=4 << 20,
     )
 
 
@@ -551,9 +622,11 @@
         inner,
         (conv_input, conv_write, conv_read, *windows, norm_gain.reshape(1, -1), ssm_state)
         + (tokens, expert_ids, route_gates),
+        out_proj,
+        inner // FIRST,
     )
     convs, windows = loaded[:3], loaded[3:6]
-    norm_gain, ssm_state, tokens, expert_ids, route_gates = loaded[6:]
+    norm_gain, ssm_state, tokens, expert_ids, route_gates, out_first = loaded[6:]
     normed, pre, coefs, writes = mix(
         scatter_parts(projected, "expert"),
         head_params,
@@ -564,13 +637,19 @@
         ssm_state,
         steps,
     )
-    partial, sent = project_out(gather(normed, "expert"), fetch(out_proj, writes), steps)
+    partial, sent = project_out(gather(normed, "expert"), (out_first, fetch(out_proj, inner // FIRST, writes)), steps)
     ssm_final, current, *finals = renew(pre, coefs, writes, windows, ssm_state, tokens)
-    residual = added([current] + sum_parts(partial, "tensor", sent))
+    residual = added([current] + sum_parts(partial, "tensor", sent, ((2, 0, 3, 1), (3, 2, 1, 0), (1, 3, 0, 2))))
     moe_in = gather(residual.astype(jnp.bfloat16), "expert")
-    moe_sum = experts(moe_in, expert_ids, route_gates, expert_up, expert_down)
+    expert_up, expert_down = resident(expert_up), resident(expert_down)
+    near = expert_near(moe_in[:NEAR], expert_up)
+    owners = len(moe_in)
+    hidden, far = experts_far(
+        near, moe_in[NEAR:], expert_ids, route_gates, expert_up, expert_down, owners
+    )
+    moe_sum = [*experts_close(hidden, expert_ids, route_gates, expert_down, owners), *far]
     moe_sum = added(scatter_parts(moe_sum, "expert"))
-    mixed_out = finish([residual] + sum_parts(moe_sum, "tensor", moe_sum.astype(jnp.bfloat16)), tokens.shape)
+    mixed_out = finish([residual] + sum_parts(moe_sum, "tensor", moe_sum.astype(jnp.bfloat16), ((1, 0, 3, 2), (2, 3, 0, 1), (3, 2, 1, 0))), tokens.shape)
     return (mixed_out, ssm_final, *finals)
 
 

time: 42.9 us -> 41.9 us (0.977)
  waiting for transfers between devices: 10.3 us -> 7.81 us
  starting transfers between devices: 17.7 us -> 19 us
    ppermute x0 -> x6, starting transfers between devices: none -> 10.1 us  [sum_parts(): lax.ppermute(sent, axis, list(enumerate(p)))]
    ppermute x18 -> x12, starting transfers between devices: 17.7 us -> 8.87 us  [swap(): return lax.ppermute(values, axis, [(i, i ^ distance) for i in range(size)])]
    ppermute x18 -> x12, waiting for transfers between devices: 10.3 us -> 4.82 us  [swap(): return lax.ppermute(values, axis, [(i, i ^ distance) for i in range(size)])]
    ppermute x0 -> x6, waiting for transfers between devices: none -> 2.99 us  [sum_parts(): lax.ppermute(sent, axis, list(enumerate(p)))]
    pallas_call x8 -> x10, Pallas kernels: 13.8 us -> 14.1 us  [local_kernel(): pl.pallas_call(body, out_shape=out_shape, in_specs=[spec for _, spec in i...]
  transfers between devices with their start and end apart: 18 -> 18, of which waited for: 9 -> 10; matrix products, arithmetic and copies ran while one was open for 0% -> 0% of each run, Pallas kernels for 12% -> 15%
where the time goes in v5:
time: 41.9 us; the launch traced here: 41.6 us
  starting transfers between devices  19 us (45%)
  Pallas kernels  14.1 us (34%)
  waiting for transfers between devices  7.81 us (19%)
  between operations  0.73 us (2%)
    pallas_call x10, Pallas kernels, local_kernel(): pl.pallas_call(body, out_shape=out_shape, in_specs=[spec for _, spec in i...  14.1 us
    ppermute x6, starting transfers between devices, sum_parts(): lax.ppermute(sent, axis, list(enumerate(p)))  10.1 us
    ppermute x12, starting transfers between devices, swap(): return lax.ppermute(values, axis, [(i, i ^ distance) for i in range(size)])  8.87 us
    ppermute x12, waiting for transfers between devices, swap(): return lax.ppermute(values, axis, [(i, i ^ distance) for i in range(size)])  4.82 us
    ppermute x6, waiting for transfers between devices, sum_parts(): lax.ppermute(sent, axis, list(enumerate(p)))  2.99 us
  transfers between devices with their start and end apart: 18, of which 10 were waited for; matrix products, arithmetic and copies ran while one was open for 0% of the time, Pallas kernels for 15%

profile of v5, /device:TPU:0, one launch (start us, length us, event | category | flops | bytes accessed | tf_op | source)
XLA Modules:
  0.0 41.6 jit_solution(3924190393873285365)
XLA Ops:
  0.6 4.3 %project.1 = (f32[2,4640]{1,0:T(2,128)S(1)}, bf16[2,4640]{1,0:T(2,128)(2,1)S(1)}, bf16[2,4640]{1,0:T(2,128)(2,1)S(1)}, bf16[2,4640]{1,0:T(2,128)(2,1)S(1)}) custom-call(bf16[2,4,1024]{2,1,0:T(4,128)(2,1)} %refs_11_.1, bf16[32,1024]{1,0:T(8,128)(2,1)} %bitcast.9, bf16[1024,2048]{1,0:T(8,128)(2,1)} %refs_2_.1, bf16[1024,2048]{1,0:T(8,128)(2,1)} %refs_3_.2, ...), custom_call_target="tpu_custom_call" | custom-call | flops 10485760 | bytes 10485760 | tf_op jit(solution)/shard_map/project/pallas_call | solution.py:67
  5.0 2.4 %collective-permute-start = (bf16[2,4640]{1,0:T(2,128)(2,1)S(1)}, bf16[2,4640]{1,0:T(2,128)(2,1)S(1)}, u32[]{:S(2)}, u32[]{:S(2)}) collective-permute-start(bf16[2,4640]{1,0:T(2,128)(2,1)S(1)} %get-tuple-element.39), channel_id=1, source_target_pairs={{0,12},{4,8},{8,4},{12,0},{1,13},{5,9},{9,5},{13,1},{2,14},{6,10},... | collective-permute-start | bytes 55688 | tf_op jit(solution)/shard_map/ppermute | solution.py:20
  7.4 0.6 %collective-permute-start.1 = (bf16[2,4640]{1,0:T(2,128)(2,1)S(1)}, bf16[2,4640]{1,0:T(2,128)(2,1)S(1)}, u32[]{:S(2)}, u32[]{:S(2)}) collective-permute-start(bf16[2,4640]{1,0:T(2,128)(2,1)S(1)} %get-tuple-element.40), channel_id=1, source_target_pairs={{0,8},{4,12},{8,0},{12,4},{1,9},{5,13},{9,1},{13,5},{2,10},{6,14},... | collective-permute-start | bytes 55688 | tf_op jit(solution)/shard_map/ppermute | solution.py:20
  8.1 2.0 %prepare.1 = (f32[3,2048]{1,0:T(4,128)S(1)}, bf16[32,2048]{1,0:T(8,128)(2,1)S(1)}, f32[4,2048]{1,0:T(4,128)S(1)}, f32[4,256]{1,0:T(4,128)S(1)}, f32[4,256]{1,0:T...) custom-call(f32[1,32]{1,0:T(1,128)} %bitcast.11, ...), custom_call_target="tpu_custom_call" | custom-call | flops 4194304 | bytes 4194304 | tf_op jit(solution)/shard_map/prepare/pallas_call | solution.py:67
  10.1 1.1 %collective-permute-done.1.refs_2_ = bf16[2,4640]{1,0:T(2,128)(2,1)S(1)} collective-permute-done((bf16[2,4640]{1,0:T(2,128)(2,1)S(1)}, bf16[2,4640]{1,0:T(2,128)(2,1)S(1)}, u32[]{:S(2)}, u32[]{:S(2)}) %collective-permute-start.1) | collective-permute-done | bytes 18592 | tf_op jit(solution)/shard_map/ppermute | solution.py:20
  11.2 0.6 %mix.1 = (bf16[2,2048]{1,0:T(2,128)(2,1)S(1)}, f32[2,2560]{1,0:T(2,128)S(1)}, f32[1,3,2048]{2,1,0:T(4,128)S(1)}, f32[2,256]{1,0:T(2,128)S(1)}) custom-call(f32[2,4640]{1,0:T(2,128)S(1)} %get-tuple-element.38.refs_0_, bf16[2,4640]{1,0:T(2,128)(2,1)S(1)} %collective-permute-done.refs_1_, bf16[2,4640]{1,0:T(2,128)(2,1)S(1)} %collective-permute-done.1.refs_2_, ...), custom_call_target="tpu_custom_call" | custom-call | flops 4194304 | bytes 4194304 | tf_op jit(solution)/shard_map/mix/pallas_call | solution.py:67
  11.8 0.4 %collective-permute-start.5 = (bf16[2,2048]{1,0:T(2,128)(2,1)S(1)}, bf16[2,2048]{1,0:T(2,128)(2,1)S(1)}, u32[]{:S(2)}, u32[]{:S(2)}) collective-permute-start(bf16[2,2048]{1,0:T(2,128)(2,1)S(1)} %get-tuple-element.57.refs_0_), channel_id=1, source_target_pairs={{0,12},{4,8},{8,4},{12,0},{1,13},{5,9},{9,5},{13,1},{2,14},{6,10},... | collective-permute-start | bytes 24584 | tf_op jit(solution)/shard_map/ppermute | solution.py:20
  12.2 0.8 %collective-permute-start.4 = (bf16[2,2048]{1,0:T(2,128)(2,1)S(1)}, bf16[2,2048]{1,0:T(2,128)(2,1)S(1)}, u32[]{:S(2)}, u32[]{:S(2)}) collective-permute-start(bf16[2,2048]{1,0:T(2,128)(2,1)S(1)} %get-tuple-element.57.refs_0_), channel_id=1, source_target_pairs={{0,8},{4,12},{8,0},{12,4},{1,9},{5,13},{9,1},{13,5},{2,10},{6,14},... | collective-permute-start | bytes 24584 | tf_op jit(solution)/shard_map/ppermute | solution.py:20
  13.0 0.7 %collective-permute-start.3 = (bf16[2,2048]{1,0:T(2,128)(2,1)S(1)}, bf16[2,2048]{1,0:T(2,128)(2,1)S(1)}, u32[]{:S(2)}, u32[]{:S(2)}) collective-permute-start(bf16[2,2048]{1,0:T(2,128)(2,1)S(1)} %get-tuple-element.57.refs_0_), channel_id=1, source_target_pairs={{0,4},{4,0},{8,12},{12,8},{1,5},{5,1},{9,13},{13,9},{2,6},{6,2},{1... | collective-permute-start | bytes 24584 | tf_op jit(solution)/shard_map/ppermute | solution.py:20
  13.7 2.0 %fetch.1.refs_5_ = bf16[1536,1024]{1,0:T(8,128)(2,1)S(1)} custom-call(bf16[2048,1024]{1,0:T(8,128)(2,1)} %source.1, f32[2,256]{1,0:T(2,128)S(1)} %get-tuple-element.54.write_ref._), custom_call_target="tpu_custom_call" | custom-call | flops 8388608 | bytes 8388608 | tf_op jit(solution)/shard_map/fetch/pallas_call | solution.py:67
  15.9 0.6 %project_out.1 = (f32[8,1024]{1,0:T(8,128)S(1)}, bf16[8,1024]{1,0:T(8,128)(2,1)S(1)}) custom-call(bf16[2,2048]{1,0:T(2,128)(2,1)S(1)} %get-tuple-element.57.refs_0_, bf16[2,2048]{1,0:T(2,128)(2,1)S(1)} %collective-permute-done.3.refs_1_, bf16[2,2048]{1,0:T(2,128)(2,1)S(1)} %collective-permute-done.4.refs_2_, ...), custom_call_target="tpu_custom_call" | custom-call | flops 4194304 | bytes 4194304 | tf_op jit(solution)/shard_map/project_out/pallas_call | solution.py:67
  16.5 1.6 %collective-permute-start.8 = (bf16[8,1024]{1,0:T(8,128)(2,1)S(1)}, bf16[8,1024]{1,0:T(8,128)(2,1)S(1)}, u32[]{:S(2)}, u32[]{:S(2)}) collective-permute-start(bf16[8,1024]{1,0:T(8,128)(2,1)S(1)} %get-tuple-element.60), channel_id=1, source_target_pairs={{0,1},{1,3},{2,0},{3,2},{4,5},{5,7},{6,4},{7,6},{8,9},{9,11},{10,8... | collective-permute-start | bytes 49160 | tf_op jit(solution)/shard_map/ppermute | solution.py:36
  18.1 2.5 %collective-permute-start.7 = (bf16[8,1024]{1,0:T(8,128)(2,1)S(1)}, bf16[8,1024]{1,0:T(8,128)(2,1)S(1)}, u32[]{:S(2)}, u32[]{:S(2)}) collective-permute-start(bf16[8,1024]{1,0:T(8,128)(2,1)S(1)} %get-tuple-element.60), channel_id=1, source_target_pairs={{0,3},{1,2},{2,1},{3,0},{4,7},{5,6},{6,5},{7,4},{8,11},{9,10},{10,... | collective-permute-start | bytes 49160 | tf_op jit(solution)/shard_map/ppermute | solution.py:36
  20.6 1.6 %collective-permute-start.6 = (bf16[8,1024]{1,0:T(8,128)(2,1)S(1)}, bf16[8,1024]{1,0:T(8,128)(2,1)S(1)}, u32[]{:S(2)}, u32[]{:S(2)}) collective-permute-start(bf16[8,1024]{1,0:T(8,128)(2,1)S(1)} %get-tuple-element.60), channel_id=1, source_target_pairs={{0,2},{1,0},{2,3},{3,1},{4,6},{5,4},{6,7},{7,5},{8,10},{9,8},{10,1... | collective-permute-start | bytes 49160 | tf_op jit(solution)/shard_map/ppermute | solution.py:36
  22.2 1.3 %renew.1 = (f32[1,32,64,128]{3,2,1,0:T(8,128)}, f32[8,1024]{1,0:T(8,128)S(1)}, bf16[1,3,2048]{2,1,0:T(4,128)(2,1)}, bf16[1,3,256]{2,1,0:T(4,128)(2,1)}, bf16[1,3,256]{2,1,0:T(4,128)(2,1)}) custom-call(f32[2,2560]{1,0:T(2,128)S(1)} %get-tuple-element.52.pre_ref, f32[1,3,2048]{2,1,0:T(4,128)S(1)} %get-tuple-element.53.coef_ref, ...), custom_call_target="tpu_custom_call" | custom-call | flops 4194304 | bytes 4194304 | tf_op jit(solution)/shard_map/renew/pallas_call | solution.py:67
  23.7 0.7 %collective-permute-done.6 = bf16[8,1024]{1,0:T(8,128)(2,1)S(1)} collective-permute-done((bf16[8,1024]{1,0:T(8,128)(2,1)S(1)}, bf16[8,1024]{1,0:T(8,128)(2,1)S(1)}, u32[]{:S(2)}, u32[]{:S(2)}) %collective-permute-start.6) | collective-permute-done | bytes 16416 | tf_op jit(solution)/shard_map/ppermute | solution.py:36
  24.4 0.9 %collective-permute-start.10 = (bf16[8,1024]{1,0:T(8,128)(2,1)S(1)}, bf16[8,1024]{1,0:T(8,128)(2,1)S(1)}, u32[]{:S(2)}, u32[]{:S(2)}) collective-permute-start(bf16[8,1024]{1,0:T(8,128)(2,1)S(1)} %get-tuple-element.73.refs_0_), channel_id=1, source_target_pairs={{0,8},{4,12},{8,0},{12,4},{1,9},{5,13},{9,1},{13,5},{2,10},{6,14},... | collective-permute-start | bytes 49160 | tf_op jit(solution)/shard_map/ppermute | solution.py:20
  25.3 0.9 %collective-permute-start.9 = (bf16[8,1024]{1,0:T(8,128)(2,1)S(1)}, bf16[8,1024]{1,0:T(8,128)(2,1)S(1)}, u32[]{:S(2)}, u32[]{:S(2)}) collective-permute-start(bf16[8,1024]{1,0:T(8,128)(2,1)S(1)} %get-tuple-element.73.refs_0_), channel_id=1, source_target_pairs={{0,4},{4,0},{8,12},{12,8},{1,5},{5,1},{9,13},{13,9},{2,6},{6,2},{1... | collective-permute-start | bytes 49160 | tf_op jit(solution)/shard_map/ppermute | solution.py:20
  26.7 0.9 %collective-permute-done.11.refs_2_ = bf16[8,1024]{1,0:T(8,128)(2,1)S(1)} collective-permute-done((bf16[8,1024]{1,0:T(8,128)(2,1)S(1)}, bf16[8,1024]{1,0:T(8,128)(2,1)S(1)}, u32[]{:S(2)}, u32[]{:S(2)}) %collective-permute-start.11) | collective-permute-done | bytes 16416 | tf_op jit(solution)/shard_map/ppermute | solution.py:20
  27.6 0.7 %collective-permute-done.10.refs_1_ = bf16[8,1024]{1,0:T(8,128)(2,1)S(1)} collective-permute-done((bf16[8,1024]{1,0:T(8,128)(2,1)S(1)}, bf16[8,1024]{1,0:T(8,128)(2,1)S(1)}, u32[]{:S(2)}, u32[]{:S(2)}) %collective-permute-start.10) | collective-permute-done | bytes 16416 | tf_op jit(solution)/shard_map/ppermute | solution.py:20
  28.3 1.8 %experts_far.1 = (bf16[4,8,256]{2,1,0:T(8,128)(2,1)S(1)}, bf16[8,1024]{1,0:T(8,128)(2,1)S(1)}, bf16[8,1024]{1,0:T(8,128)(2,1)S(1)}, bf16[8,1024]{1,0:T(8,128)(2,1)S(1)}) custom-call(bf16[8,1024]{1,0:T(8,128)(2,1)S(1)} %collective-permute-done.9.refs_0_, bf16[8,1024]{1,0:T(8,128)(2,1)S(1)} %collective-permute-done.10.refs_1_, ...), custom_call_target="tpu_custom_call" | custom-call | flops 16777216 | bytes 16777216 | tf_op jit(solution)/shard_map/experts_far/pallas_call | solution.py:67
  30.1 0.5 %collective-permute-start.12 = (bf16[8,1024]{1,0:T(8,128)(2,1)S(1)}, bf16[8,1024]{1,0:T(8,128)(2,1)S(1)}, u32[]{:S(2)}, u32[]{:S(2)}) collective-permute-start(bf16[8,1024]{1,0:T(8,128)(2,1)S(1)} %get-tuple-element.64), channel_id=1, source_target_pairs={{0,12},{4,8},{8,4},{12,0},{1,13},{5,9},{9,5},{13,1},{2,14},{6,10},... | collective-permute-start | bytes 49160 | tf_op jit(solution)/shard_map/ppermute | solution.py:20
  30.6 1.2 %collective-permute-start.13 = (bf16[8,1024]{1,0:T(8,128)(2,1)S(1)}, bf16[8,1024]{1,0:T(8,128)(2,1)S(1)}, u32[]{:S(2)}, u32[]{:S(2)}) collective-permute-start(bf16[8,1024]{1,0:T(8,128)(2,1)S(1)} %get-tuple-element.65), channel_id=1, source_target_pairs={{0,8},{4,12},{8,0},{12,4},{1,9},{5,13},{9,1},{13,5},{2,10},{6,14},... | collective-permute-start | bytes 49160 | tf_op jit(solution)/shard_map/ppermute | solution.py:20
  32.0 0.4 experts_close.1
  32.4 0.9 %collective-permute-done.12 = bf16[8,1024]{1,0:T(8,128)(2,1)S(1)} collective-permute-done((bf16[8,1024]{1,0:T(8,128)(2,1)S(1)}, bf16[8,1024]{1,0:T(8,128)(2,1)S(1)}, u32[]{:S(2)}, u32[]{:S(2)}) %collective-permute-start.12) | collective-permute-done | bytes 16416 | tf_op jit(solution)/shard_map/ppermute | solution.py:20
  33.3 1.1 %collective-permute-done.13 = bf16[8,1024]{1,0:T(8,128)(2,1)S(1)} collective-permute-done((bf16[8,1024]{1,0:T(8,128)(2,1)S(1)}, bf16[8,1024]{1,0:T(8,128)(2,1)S(1)}, u32[]{:S(2)}, u32[]{:S(2)}) %collective-permute-start.13) | collective-permute-done | bytes 16416 | tf_op jit(solution)/shard_map/ppermute | solution.py:20
  34.4 2.0 %collective-permute-start.17 = (bf16[8,1024]{1,0:T(8,128)(2,1)S(1)}, bf16[8,1024]{1,0:T(8,128)(2,1)S(1)}, u32[]{:S(2)}, u32[]{:S(2)}) collective-permute-start(bf16[8,1024]{1,0:T(8,128)(2,1)S(1)} %get-tuple-element.71), channel_id=1, source_target_pairs={{0,3},{1,2},{2,1},{3,0},{4,7},{5,6},{6,5},{7,4},{8,11},{9,10},{10,... | collective-permute-start | bytes 49160 | tf_op jit(solution)/shard_map/ppermute | solution.py:36
  36.4 0.6 %collective-permute-start.16 = (bf16[8,1024]{1,0:T(8,128)(2,1)S(1)}, bf16[8,1024]{1,0:T(8,128)(2,1)S(1)}, u32[]{:S(2)}, u32[]{:S(2)}) collective-permute-start(bf16[8,1024]{1,0:T(8,128)(2,1)S(1)} %get-tuple-element.71), channel_id=1, source_target_pairs={{0,2},{1,3},{2,0},{3,1},{4,6},{5,7},{6,4},{7,5},{8,10},{9,11},{10,... | collective-permute-start | bytes 49160 | tf_op jit(solution)/shard_map/ppermute | solution.py:36
  37.0 1.8 %collective-permute-start.15 = (bf16[8,1024]{1,0:T(8,128)(2,1)S(1)}, bf16[8,1024]{1,0:T(8,128)(2,1)S(1)}, u32[]{:S(2)}, u32[]{:S(2)}) collective-permute-start(bf16[8,1024]{1,0:T(8,128)(2,1)S(1)} %get-tuple-element.71), channel_id=1, source_target_pairs={{0,1},{1,0},{2,3},{3,2},{4,5},{5,4},{6,7},{7,6},{8,9},{9,8},{10,11... | collective-permute-start | bytes 49160 | tf_op jit(solution)/shard_map/ppermute | solution.py:36
  38.8 1.2 %collective-permute-done.17.refs_4_ = bf16[8,1024]{1,0:T(8,128)(2,1)S(1)} collective-permute-done((bf16[8,1024]{1,0:T(8,128)(2,1)S(1)}, bf16[8,1024]{1,0:T(8,128)(2,1)S(1)}, u32[]{:S(2)}, u32[]{:S(2)}) %collective-permute-start.17) | collective-permute-done | bytes 16416 | tf_op jit(solution)/shard_map/ppermute | solution.py:36
  40.1 0.9 %collective-permute-done.16.refs_3_ = bf16[8,1024]{1,0:T(8,128)(2,1)S(1)} collective-permute-done((bf16[8,1024]{1,0:T(8,128)(2,1)S(1)}, bf16[8,1024]{1,0:T(8,128)(2,1)S(1)}, u32[]{:S(2)}, u32[]{:S(2)}) %collective-permute-start.16) | collective-permute-done | bytes 16416 | tf_op jit(solution)/shard_map/ppermute | solution.py:36
  41.0 0.6 %finish.1 = bf16[2,4,1024]{2,1,0:T(4,128)(2,1)} custom-call(f32[8,1024]{1,0:T(8,128)S(1)} %get-tuple-element.74.refs_0_, f32[8,1024]{1,0:T(8,128)S(1)} %get-tuple-element.72.refs_1_, bf16[8,1024]{1,0:T(8,128)(2,1)S(1)} %collective-permute-done.15.refs_2_, bf16[8,1024]{1,0:T(8,128)(2,1)S(1)} %collective-permute-done.16.refs_3_, ...), custom_call_target="tpu_custom_call" | custom-call | flops 1048576 | bytes 1048576 | tf_op jit(solution)/shard_map/finish/pallas_call | solution.py:67
  (26 shorter events, 1.0 us)
Async XLA Ops:
  5.0 5.1 %collective-permute-start = (bf16[2,4640]{1,0:T(2,128)(2,1)S(1)}, bf16[2,4640]{1,0:T(2,128)(2,1)S(1)}, u32[]{:S(2)}, u32[]{:S(2)}) collective-permute-start(bf16[2,4640]{1,0:T(2,128)(2,1)S(1)} %get-tuple-element.39), channel_id=1, source_target_pairs={{0,12},{4,8},{8,4},{12,0},{1,13},{5,9},{9,5},{13,1},{2,14},{6,10},... | collective-permute-start | bytes 55688 | tf_op jit(solution)/shard_map/ppermute | solution.py:20
  7.4 3.8 %collective-permute-start.1 = (bf16[2,4640]{1,0:T(2,128)(2,1)S(1)}, bf16[2,4640]{1,0:T(2,128)(2,1)S(1)}, u32[]{:S(2)}, u32[]{:S(2)}) collective-permute-start(bf16[2,4640]{1,0:T(2,128)(2,1)S(1)} %get-tuple-element.40), channel_id=1, source_target_pairs={{0,8},{4,12},{8,0},{12,4},{1,9},{5,13},{9,1},{13,5},{2,10},{6,14},... | collective-permute-start | bytes 55688 | tf_op jit(solution)/shard_map/ppermute | solution.py:20
  8.1 3.1 %collective-permute-start.2 = (bf16[2,4640]{1,0:T(2,128)(2,1)S(1)}, bf16[2,4640]{1,0:T(2,128)(2,1)S(1)}, u32[]{:S(2)}, u32[]{:S(2)}) collective-permute-start(bf16[2,4640]{1,0:T(2,128)(2,1)S(1)} %get-tuple-element.41), channel_id=1, source_target_pairs={{0,4},{4,0},{8,12},{12,8},{1,5},{5,1},{9,13},{13,9},{2,6},{6,2},{1... | collective-permute-start | bytes 55688 | tf_op jit(solution)/shard_map/ppermute | solution.py:20
  8.1 18.2 %slice-start = ((s8[8388608]{0:T(1024)(128)(4,1)}), s8[4194304]{0:T(1024)(128)(4,1)S(1)}, s32[]{:S(2)}) async-start(s8[8388608]{0:T(1024)(128)(4,1)} %bitcast.5), calls=%async_computation | async-start | bytes 8388608
  11.8 4.0 %collective-permute-start.5 = (bf16[2,2048]{1,0:T(2,128)(2,1)S(1)}, bf16[2,2048]{1,0:T(2,128)(2,1)S(1)}, u32[]{:S(2)}, u32[]{:S(2)}) collective-permute-start(bf16[2,2048]{1,0:T(2,128)(2,1)S(1)} %get-tuple-element.57.refs_0_), channel_id=1, source_target_pairs={{0,12},{4,8},{8,4},{12,0},{1,13},{5,9},{9,5},{13,1},{2,14},{6,10},... | collective-permute-start | bytes 24584 | tf_op jit(solution)/shard_map/ppermute | solution.py:20
  12.2 3.7 %collective-permute-start.4 = (bf16[2,2048]{1,0:T(2,128)(2,1)S(1)}, bf16[2,2048]{1,0:T(2,128)(2,1)S(1)}, u32[]{:S(2)}, u32[]{:S(2)}) collective-permute-start(bf16[2,2048]{1,0:T(2,128)(2,1)S(1)} %get-tuple-element.57.refs_0_), channel_id=1, source_target_pairs={{0,8},{4,12},{8,0},{12,4},{1,9},{5,13},{9,1},{13,5},{2,10},{6,14},... | collective-permute-start | bytes 24584 | tf_op jit(solution)/shard_map/ppermute | solution.py:20
  13.0 2.9 %collective-permute-start.3 = (bf16[2,2048]{1,0:T(2,128)(2,1)S(1)}, bf16[2,2048]{1,0:T(2,128)(2,1)S(1)}, u32[]{:S(2)}, u32[]{:S(2)}) collective-permute-start(bf16[2,2048]{1,0:T(2,128)(2,1)S(1)} %get-tuple-element.57.refs_0_), channel_id=1, source_target_pairs={{0,4},{4,0},{8,12},{12,8},{1,5},{5,1},{9,13},{13,9},{2,6},{6,2},{1... | collective-permute-start | bytes 24584 | tf_op jit(solution)/shard_map/ppermute | solution.py:20
  13.7 12.6 %slice-start.1 = ((s8[8388608]{0:T(1024)(128)(4,1)}), s8[4194304]{0:T(1024)(128)(4,1)S(1)}, s32[]{:S(2)}) async-start(s8[8388608]{0:T(1024)(128)(4,1)} %bitcast.5), calls=%async_computation.1 | async-start | bytes 8388608
  13.7 14.6 %slice-start.2 = ((s8[8388608]{0:T(1024)(128)(4,1)}), s8[4194304]{0:T(1024)(128)(4,1)S(1)}, s32[]{:S(2)}) async-start(s8[8388608]{0:T(1024)(128)(4,1)} %bitcast.7), calls=%async_computation.2 | async-start | bytes 8388608
  15.9 12.5 %slice-start.3 = ((s8[8388608]{0:T(1024)(128)(4,1)}), s8[4194304]{0:T(1024)(128)(4,1)S(1)}, s32[]{:S(2)}) async-start(s8[8388608]{0:T(1024)(128)(4,1)} %bitcast.7), calls=%async_computation.3 | async-start | bytes 8388608
  16.5 7.0 %collective-permute-start.8 = (bf16[8,1024]{1,0:T(8,128)(2,1)S(1)}, bf16[8,1024]{1,0:T(8,128)(2,1)S(1)}, u32[]{:S(2)}, u32[]{:S(2)}) collective-permute-start(bf16[8,1024]{1,0:T(8,128)(2,1)S(1)} %get-tuple-element.60), channel_id=1, source_target_pairs={{0,1},{1,3},{2,0},{3,2},{4,5},{5,7},{6,4},{7,6},{8,9},{9,11},{10,8... | collective-permute-start | bytes 49160 | tf_op jit(solution)/shard_map/ppermute | solution.py:36
  18.1 5.5 %collective-permute-start.7 = (bf16[8,1024]{1,0:T(8,128)(2,1)S(1)}, bf16[8,1024]{1,0:T(8,128)(2,1)S(1)}, u32[]{:S(2)}, u32[]{:S(2)}) collective-permute-start(bf16[8,1024]{1,0:T(8,128)(2,1)S(1)} %get-tuple-element.60), channel_id=1, source_target_pairs={{0,3},{1,2},{2,1},{3,0},{4,7},{5,6},{6,5},{7,4},{8,11},{9,10},{10,... | collective-permute-start | bytes 49160 | tf_op jit(solution)/shard_map/ppermute | solution.py:36
  20.6 3.7 %collective-permute-start.6 = (bf16[8,1024]{1,0:T(8,128)(2,1)S(1)}, bf16[8,1024]{1,0:T(8,128)(2,1)S(1)}, u32[]{:S(2)}, u32[]{:S(2)}) collective-permute-start(bf16[8,1024]{1,0:T(8,128)(2,1)S(1)} %get-tuple-element.60), channel_id=1, source_target_pairs={{0,2},{1,0},{2,3},{3,1},{4,6},{5,4},{6,7},{7,5},{8,10},{9,8},{10,1... | collective-permute-start | bytes 49160 | tf_op jit(solution)/shard_map/ppermute | solution.py:36
  24.4 3.2 %collective-permute-start.11 = (bf16[8,1024]{1,0:T(8,128)(2,1)S(1)}, bf16[8,1024]{1,0:T(8,128)(2,1)S(1)}, u32[]{:S(2)}, u32[]{:S(2)}) collective-permute-start(bf16[8,1024]{1,0:T(8,128)(2,1)S(1)} %get-tuple-element.73.refs_0_), channel_id=1, source_target_pairs={{0,12},{4,8},{8,4},{12,0},{1,13},{5,9},{9,5},{13,1},{2,14},{6,10},... | collective-permute-start | bytes 49160 | tf_op jit(solution)/shard_map/ppermute | solution.py:20
  24.4 3.9 %collective-permute-start.10 = (bf16[8,1024]{1,0:T(8,128)(2,1)S(1)}, bf16[8,1024]{1,0:T(8,128)(2,1)S(1)}, u32[]{:S(2)}, u32[]{:S(2)}) collective-permute-start(bf16[8,1024]{1,0:T(8,128)(2,1)S(1)} %get-tuple-element.73.refs_0_), channel_id=1, source_target_pairs={{0,8},{4,12},{8,0},{12,4},{1,9},{5,13},{9,1},{13,5},{2,10},{6,14},... | collective-permute-start | bytes 49160 | tf_op jit(solution)/shard_map/ppermute | solution.py:20
  25.3 3.0 %collective-permute-start.9 = (bf16[8,1024]{1,0:T(8,128)(2,1)S(1)}, bf16[8,1024]{1,0:T(8,128)(2,1)S(1)}, u32[]{:S(2)}, u32[]{:S(2)}) collective-permute-start(bf16[8,1024]{1,0:T(8,128)(2,1)S(1)} %get-tuple-element.73.refs_0_), channel_id=1, source_target_pairs={{0,4},{4,0},{8,12},{12,8},{1,5},{5,1},{9,13},{13,9},{2,6},{6,2},{1... | collective-permute-start | bytes 49160 | tf_op jit(solution)/shard_map/ppermute | solution.py:20
  30.1 3.2 %collective-permute-start.12 = (bf16[8,1024]{1,0:T(8,128)(2,1)S(1)}, bf16[8,1024]{1,0:T(8,128)(2,1)S(1)}, u32[]{:S(2)}, u32[]{:S(2)}) collective-permute-start(bf16[8,1024]{1,0:T(8,128)(2,1)S(1)} %get-tuple-element.64), channel_id=1, source_target_pairs={{0,12},{4,8},{8,4},{12,0},{1,13},{5,9},{9,5},{13,1},{2,14},{6,10},... | collective-permute-start | bytes 49160 | tf_op jit(solution)/shard_map/ppermute | solution.py:20
  30.6 3.7 %collective-permute-start.13 = (bf16[8,1024]{1,0:T(8,128)(2,1)S(1)}, bf16[8,1024]{1,0:T(8,128)(2,1)S(1)}, u32[]{:S(2)}, u32[]{:S(2)}) collective-permute-start(bf16[8,1024]{1,0:T(8,128)(2,1)S(1)} %get-tuple-element.65), channel_id=1, source_target_pairs={{0,8},{4,12},{8,0},{12,4},{1,9},{5,13},{9,1},{13,5},{2,10},{6,14},... | collective-permute-start | bytes 49160 | tf_op jit(solution)/shard_map/ppermute | solution.py:20
  31.8 2.6 %collective-permute-start.14 = (bf16[8,1024]{1,0:T(8,128)(2,1)S(1)}, bf16[8,1024]{1,0:T(8,128)(2,1)S(1)}, u32[]{:S(2)}, u32[]{:S(2)}) collective-permute-start(bf16[8,1024]{1,0:T(8,128)(2,1)S(1)} %get-tuple-element.66), channel_id=1, source_target_pairs={{0,4},{4,0},{8,12},{12,8},{1,5},{5,1},{9,13},{13,9},{2,6},{6,2},{1... | collective-permute-start | bytes 49160 | tf_op jit(solution)/shard_map/ppermute | solution.py:20
  34.4 5.7 %collective-permute-start.17 = (bf16[8,1024]{1,0:T(8,128)(2,1)S(1)}, bf16[8,1024]{1,0:T(8,128)(2,1)S(1)}, u32[]{:S(2)}, u32[]{:S(2)}) collective-permute-start(bf16[8,1024]{1,0:T(8,128)(2,1)S(1)} %get-tuple-element.71), channel_id=1, source_target_pairs={{0,3},{1,2},{2,1},{3,0},{4,7},{5,6},{6,5},{7,4},{8,11},{9,10},{10,... | collective-permute-start | bytes 49160 | tf_op jit(solution)/shard_map/ppermute | solution.py:36
  36.4 4.6 %collective-permute-start.16 = (bf16[8,1024]{1,0:T(8,128)(2,1)S(1)}, bf16[8,1024]{1,0:T(8,128)(2,1)S(1)}, u32[]{:S(2)}, u32[]{:S(2)}) collective-permute-start(bf16[8,1024]{1,0:T(8,128)(2,1)S(1)} %get-tuple-element.71), channel_id=1, source_target_pairs={{0,2},{1,3},{2,0},{3,1},{4,6},{5,7},{6,4},{7,5},{8,10},{9,11},{10,... | collective-permute-start | bytes 49160 | tf_op jit(solution)/shard_map/ppermute | solution.py:36
  37.0 4.0 %collective-permute-start.15 = (bf16[8,1024]{1,0:T(8,128)(2,1)S(1)}, bf16[8,1024]{1,0:T(8,128)(2,1)S(1)}, u32[]{:S(2)}, u32[]{:S(2)}) collective-permute-start(bf16[8,1024]{1,0:T(8,128)(2,1)S(1)} %get-tuple-element.71), channel_id=1, source_target_pairs={{0,1},{1,0},{2,3},{3,2},{4,5},{5,4},{6,7},{7,6},{8,9},{9,8},{10,11... | collective-permute-start | bytes 49160 | tf_op jit(solution)/shard_map/ppermute | solution.py:36

commit v6 on v5

--- a/solution.py
+++ b/solution.py
@@ -40,7 +40,7 @@
     if not pairwise(axis):
         blocks = jnp.stack([block.astype(jnp.float32) for block in blocks])
         return [lax.psum_scatter(blocks, axis, scatter_dimension=0, tiled=False)]
-    return [blocks[0]] + [swap(blocks[d], axis, d) for d in reversed(range(1, len(blocks)))]
+    return [blocks[0]] + [swap(blocks[d], axis, d) for d in (2, 3, 1) if d < len(blocks)]
 
 
 def added(parts):
@@ -58,7 +58,6 @@
 IN_VMEM = pl.BlockSpec(memory_space=pltpu.VMEM)
 IN_HBM = pl.BlockSpec(memory_space=pltpu.HBM)
 CHUNK = 512 * 1024
-MIX_COST = 4 << 20
 FIRST = 4
 NEAR = 1
 
@@ -279,40 +278,36 @@
         step_size = jax.nn.softplus(step_pre + bias)
         decay = jnp.exp(-step_size * rate)
         gate = silu_float(gate)
+        normed = []
         for own in range(own_rows):
-            first = own * steps
+            mine = slice(own * steps, (own + 1) * steps)
             acts = []
             for which in range(3):
                 taps_in = conv_refs[which][...]
                 earlier = window_refs[which][own].astype(jnp.float32)
-                line = [earlier[k : k + 1] for k in range(taps - 1)]
-                line += [newest[which][first + s : first + s + 1] for s in range(steps)]
+                line = jnp.concatenate([earlier, newest[which][mine]], axis=0)
                 acts.append(
-                    [
-                        silu_float(added([line[s + k] * taps_in[k : k + 1] for k in range(taps)]))
-                        for s in range(steps)
-                    ]
+                    silu_float(
+                        added([line[k : k + steps] * taps_in[k : k + 1] for k in range(taps)])
+                    )
                 )
             input_act, write_act, read_act = acts
-            for s in range(steps):
-                write_ref[pl.ds(first + s, 1), :] = write_act[s]
-            sizes = [step_size[first + s : first + s + 1] for s in range(steps)]
-            decays = [decay[first + s : first + s + 1] for s in range(steps)]
-            fresh = [sizes[s] * input_act[s] for s in range(steps)]
-            coefs = list(fresh)
-            kept = jnp.ones_like(decays[0])
+            write_ref[pl.ds(own * steps, steps), :] = write_act
+            decays = decay[mine]
+            fresh = step_size[mine] * input_act
+            coefs = [fresh[s : s + 1] for s in range(steps)]
+            kept = jnp.ones_like(decays[0:1])
             for s in reversed(range(steps)):
                 coefs[s] = coefs[s] * kept
-                kept = kept * decays[s]
-            for i, row in enumerate([kept] + coefs):
-                coef_ref[own, i : i + 1, :] = row
+                kept = kept * decays[s : s + 1]
+            coef_ref[own] = jnp.concatenate([kept] + coefs, axis=0)
+            normed.append([])
             for g in range(groups):
                 span = slice(g * channels, (g + 1) * channels)
                 lanes = slice(g * state_size, (g + 1) * state_size)
                 state = state_ref[own, g * heads_group : (g + 1) * heads_group]
                 state = state.reshape(channels, state_size)
-                reads = jnp.concatenate([read_act[s][:, lanes] for s in range(steps)], axis=0)
-                high, low = [p.astype(jnp.float32) for p in split_in(reads, 2)]
+                high, low = [p.astype(jnp.float32) for p in split_in(read_act[:, lanes], 2)]
                 reads = jnp.concatenate([high, low], axis=0).astype(jnp.bfloat16)
                 by_high, by_low = [
                     lax.dot_general(
@@ -321,18 +316,23 @@
                     for p in split_in(state, 2)
                 ]
                 product = by_high[:steps] + by_high[steps:] + by_low[:steps]
+                values = []
                 for s in range(steps):
                     value = product[s : s + 1]
                     for j in range(s + 1):
                         overlap = jnp.sum(
-                            write_act[j][:, lanes] * read_act[s][:, lanes], axis=1, keepdims=True
+                            write_act[j : j + 1, lanes] * read_act[s : s + 1, lanes],
+                            axis=1,
+                            keepdims=True,
                         )
-                        value = decays[j][:, span] * value + fresh[j][:, span] * overlap
-                    value = value + skip[:, span] * input_act[s][:, span]
-                    value = value * gate[first + s : first + s + 1, span]
-                    mean = jnp.mean(value * value, axis=1, keepdims=True)
-                    value = value * lax.rsqrt(mean + 1e-05) * gain_ref[:, span]
-                    normed_ref[pl.ds(first + s, 1), span] = value.astype(jnp.bfloat16)
+                        value = decays[j : j + 1, span] * value + fresh[j : j + 1, span] * overlap
+                    values.append(value)
+                value = jnp.concatenate(values, axis=0) + skip[:, span] * input_act[:, span]
+                value = value * gate[mine, span]
+                mean = jnp.mean(value * value, axis=1, keepdims=True)
+                normed[own].append(value * lax.rsqrt(mean + 1e-05) * gain_ref[:, span])
+        normed = [jnp.concatenate(row, axis=1) for row in normed]
+        normed_ref[...] = jnp.concatenate(normed, axis=0).astype(jnp.bfloat16)
 
     return local_kernel(
         body,
@@ -344,7 +344,7 @@
             shaped((block, width)),
         ],
         [(a, IN_VMEM) for a in (*parts, head_params, spread, *convs, *windows, norm_gain, ssm_state)],
-        bytes_accessed=MIX_COST,
+        bytes_accessed=4 << 20,
     )
 
 
@@ -355,7 +355,6 @@
     heads_group = heads // groups
     inner = coefs.shape[2]
     widths = [w.shape[2] for w in windows]
-    kept = windows[0].shape[1]
 
     def body(pre_ref, coef_ref, write_ref, *rest):
         window_refs, (state_ref, tokens_ref, final_ref, current_ref) = rest[:3], rest[3:7]

time: 41.9 us -> 41.7 us (level)
  waiting for transfers between devices: 7.81 us -> 7.27 us
    ppermute x12, waiting for transfers between devices: 4.82 us -> 4.35 us  [swap(): return lax.ppermute(values, axis, [(i, i ^ distance) for i in range(size)])]
where the time goes in v6:
time: 41.7 us; the launch traced here: 41.4 us
  starting transfers between devices  19.3 us (46%)
  Pallas kernels  14.1 us (34%)
  waiting for transfers between devices  7.27 us (17%)
  between operations  0.73 us (2%)
    pallas_call x10, Pallas kernels, local_kernel(): pl.pallas_call(body, out_shape=out_shape, in_specs=[spec for _, spec in i...  14.1 us
    ppermute x6, starting transfers between devices, sum_parts(): lax.ppermute(sent, axis, list(enumerate(p)))  10.1 us
    ppermute x12, starting transfers between devices, swap(): return lax.ppermute(values, axis, [(i, i ^ distance) for i in range(size)])  9.23 us
    ppermute x12, waiting for transfers between devices, swap(): return lax.ppermute(values, axis, [(i, i ^ distance) for i in range(size)])  4.35 us
    ppermute x6, waiting for transfers between devices, sum_parts(): lax.ppermute(sent, axis, list(enumerate(p)))  2.91 us
  transfers between devices with their start and end apart: 18, of which 10 were waited for; matrix products, arithmetic and copies ran while one was open for 0% of the time, Pallas kernels for 15%

profile of v6, /device:TPU:0, one launch (start us, length us, event | category | flops | bytes accessed | tf_op | source)
XLA Modules:
  0.0 41.4 jit_solution(15202456834787011527)
XLA Ops:
  0.6 4.3 %project.1 = (f32[2,4640]{1,0:T(2,128)S(1)}, bf16[2,4640]{1,0:T(2,128)(2,1)S(1)}, bf16[2,4640]{1,0:T(2,128)(2,1)S(1)}, bf16[2,4640]{1,0:T(2,128)(2,1)S(1)}) custom-call(bf16[2,4,1024]{2,1,0:T(4,128)(2,1)} %refs_11_.1, bf16[32,1024]{1,0:T(8,128)(2,1)} %bitcast.9, bf16[1024,2048]{1,0:T(8,128)(2,1)} %refs_2_.1, bf16[1024,2048]{1,0:T(8,128)(2,1)} %refs_3_.2, ...), custom_call_target="tpu_custom_call" | custom-call | flops 10485760 | bytes 10485760 | tf_op jit(solution)/shard_map/project/pallas_call | solution.py:66
  5.0 3.0 %collective-permute-start = (bf16[2,4640]{1,0:T(2,128)(2,1)S(1)}, bf16[2,4640]{1,0:T(2,128)(2,1)S(1)}, u32[]{:S(2)}, u32[]{:S(2)}) collective-permute-start(bf16[2,4640]{1,0:T(2,128)(2,1)S(1)} %get-tuple-element.39), channel_id=1, source_target_pairs={{0,8},{4,12},{8,0},{12,4},{1,9},{5,13},{9,1},{13,5},{2,10},{6,14},... | collective-permute-start | bytes 55688 | tf_op jit(solution)/shard_map/ppermute | solution.py:20
  8.2 2.0 %prepare.1 = (f32[3,2048]{1,0:T(4,128)S(1)}, bf16[32,2048]{1,0:T(8,128)(2,1)S(1)}, f32[4,2048]{1,0:T(4,128)S(1)}, f32[4,256]{1,0:T(4,128)S(1)}, f32[4,256]{1,0:T...) custom-call(f32[1,32]{1,0:T(1,128)} %bitcast.11, ...), custom_call_target="tpu_custom_call" | custom-call | flops 4194304 | bytes 4194304 | tf_op jit(solution)/shard_map/prepare/pallas_call | solution.py:66
  10.2 1.0 %collective-permute-done.1.refs_2_ = bf16[2,4640]{1,0:T(2,128)(2,1)S(1)} collective-permute-done((bf16[2,4640]{1,0:T(2,128)(2,1)S(1)}, bf16[2,4640]{1,0:T(2,128)(2,1)S(1)}, u32[]{:S(2)}, u32[]{:S(2)}) %collective-permute-start.1) | collective-permute-done | bytes 18592 | tf_op jit(solution)/shard_map/ppermute | solution.py:20
  11.2 0.6 %mix.1 = (bf16[2,2048]{1,0:T(2,128)(2,1)S(1)}, f32[2,2560]{1,0:T(2,128)S(1)}, f32[1,3,2048]{2,1,0:T(4,128)S(1)}, f32[2,256]{1,0:T(2,128)S(1)}) custom-call(f32[2,4640]{1,0:T(2,128)S(1)} %get-tuple-element.38.refs_0_, bf16[2,4640]{1,0:T(2,128)(2,1)S(1)} %collective-permute-done.refs_1_, bf16[2,4640]{1,0:T(2,128)(2,1)S(1)} %collective-permute-done.1.refs_2_, ...), custom_call_target="tpu_custom_call" | custom-call | flops 4194304 | bytes 4194304 | tf_op jit(solution)/shard_map/mix/pallas_call | solution.py:66
  11.8 0.6 %collective-permute-start.5 = (bf16[2,2048]{1,0:T(2,128)(2,1)S(1)}, bf16[2,2048]{1,0:T(2,128)(2,1)S(1)}, u32[]{:S(2)}, u32[]{:S(2)}) collective-permute-start(bf16[2,2048]{1,0:T(2,128)(2,1)S(1)} %get-tuple-element.57.refs_0_), channel_id=1, source_target_pairs={{0,12},{4,8},{8,4},{12,0},{1,13},{5,9},{9,5},{13,1},{2,14},{6,10},... | collective-permute-start | bytes 24584 | tf_op jit(solution)/shard_map/ppermute | solution.py:20
  12.4 0.6 %collective-permute-start.4 = (bf16[2,2048]{1,0:T(2,128)(2,1)S(1)}, bf16[2,2048]{1,0:T(2,128)(2,1)S(1)}, u32[]{:S(2)}, u32[]{:S(2)}) collective-permute-start(bf16[2,2048]{1,0:T(2,128)(2,1)S(1)} %get-tuple-element.57.refs_0_), channel_id=1, source_target_pairs={{0,8},{4,12},{8,0},{12,4},{1,9},{5,13},{9,1},{13,5},{2,10},{6,14},... | collective-permute-start | bytes 24584 | tf_op jit(solution)/shard_map/ppermute | solution.py:20
  13.0 0.7 %collective-permute-start.3 = (bf16[2,2048]{1,0:T(2,128)(2,1)S(1)}, bf16[2,2048]{1,0:T(2,128)(2,1)S(1)}, u32[]{:S(2)}, u32[]{:S(2)}) collective-permute-start(bf16[2,2048]{1,0:T(2,128)(2,1)S(1)} %get-tuple-element.57.refs_0_), channel_id=1, source_target_pairs={{0,4},{4,0},{8,12},{12,8},{1,5},{5,1},{9,13},{13,9},{2,6},{6,2},{1... | collective-permute-start | bytes 24584 | tf_op jit(solution)/shard_map/ppermute | solution.py:20
  13.7 2.0 %fetch.1.refs_5_ = bf16[1536,1024]{1,0:T(8,128)(2,1)S(1)} custom-call(bf16[2048,1024]{1,0:T(8,128)(2,1)} %source.1, f32[2,256]{1,0:T(2,128)S(1)} %get-tuple-element.54.write_ref._), custom_call_target="tpu_custom_call" | custom-call | flops 8388608 | bytes 8388608 | tf_op jit(solution)/shard_map/fetch/pallas_call | solution.py:66
  15.8 0.3 collective-permute-done.4.refs_2_
  16.0 0.6 %project_out.1 = (f32[8,1024]{1,0:T(8,128)S(1)}, bf16[8,1024]{1,0:T(8,128)(2,1)S(1)}) custom-call(bf16[2,2048]{1,0:T(2,128)(2,1)S(1)} %get-tuple-element.57.refs_0_, bf16[2,2048]{1,0:T(2,128)(2,1)S(1)} %collective-permute-done.3.refs_1_, bf16[2,2048]{1,0:T(2,128)(2,1)S(1)} %collective-permute-done.4.refs_2_, ...), custom_call_target="tpu_custom_call" | custom-call | flops 4194304 | bytes 4194304 | tf_op jit(solution)/shard_map/project_out/pallas_call | solution.py:66
  16.7 1.6 %collective-permute-start.8 = (bf16[8,1024]{1,0:T(8,128)(2,1)S(1)}, bf16[8,1024]{1,0:T(8,128)(2,1)S(1)}, u32[]{:S(2)}, u32[]{:S(2)}) collective-permute-start(bf16[8,1024]{1,0:T(8,128)(2,1)S(1)} %get-tuple-element.60), channel_id=1, source_target_pairs={{0,1},{1,3},{2,0},{3,2},{4,5},{5,7},{6,4},{7,6},{8,9},{9,11},{10,8... | collective-permute-start | bytes 49160 | tf_op jit(solution)/shard_map/ppermute | solution.py:36
  18.3 2.5 %collective-permute-start.7 = (bf16[8,1024]{1,0:T(8,128)(2,1)S(1)}, bf16[8,1024]{1,0:T(8,128)(2,1)S(1)}, u32[]{:S(2)}, u32[]{:S(2)}) collective-permute-start(bf16[8,1024]{1,0:T(8,128)(2,1)S(1)} %get-tuple-element.60), channel_id=1, source_target_pairs={{0,3},{1,2},{2,1},{3,0},{4,7},{5,6},{6,5},{7,4},{8,11},{9,10},{10,... | collective-permute-start | bytes 49160 | tf_op jit(solution)/shard_map/ppermute | solution.py:36
  20.8 1.6 %collective-permute-start.6 = (bf16[8,1024]{1,0:T(8,128)(2,1)S(1)}, bf16[8,1024]{1,0:T(8,128)(2,1)S(1)}, u32[]{:S(2)}, u32[]{:S(2)}) collective-permute-start(bf16[8,1024]{1,0:T(8,128)(2,1)S(1)} %get-tuple-element.60), channel_id=1, source_target_pairs={{0,2},{1,0},{2,3},{3,1},{4,6},{5,4},{6,7},{7,5},{8,10},{9,8},{10,1... | collective-permute-start | bytes 49160 | tf_op jit(solution)/shard_map/ppermute | solution.py:36
  22.3 1.3 %renew.1 = (f32[1,32,64,128]{3,2,1,0:T(8,128)}, f32[8,1024]{1,0:T(8,128)S(1)}, bf16[1,3,2048]{2,1,0:T(4,128)(2,1)}, bf16[1,3,256]{2,1,0:T(4,128)(2,1)}, bf16[1,3,256]{2,1,0:T(4,128)(2,1)}) custom-call(f32[2,2560]{1,0:T(2,128)S(1)} %get-tuple-element.52.pre_ref, f32[1,3,2048]{2,1,0:T(4,128)S(1)} %get-tuple-element.53.coef_ref, ...), custom_call_target="tpu_custom_call" | custom-call | flops 4194304 | bytes 4194304 | tf_op jit(solution)/shard_map/renew/pallas_call | solution.py:66
  23.8 0.7 %collective-permute-done.6 = bf16[8,1024]{1,0:T(8,128)(2,1)S(1)} collective-permute-done((bf16[8,1024]{1,0:T(8,128)(2,1)S(1)}, bf16[8,1024]{1,0:T(8,128)(2,1)S(1)}, u32[]{:S(2)}, u32[]{:S(2)}) %collective-permute-start.6) | collective-permute-done | bytes 16416 | tf_op jit(solution)/shard_map/ppermute | solution.py:36
  24.6 0.8 %collective-permute-start.10 = (bf16[8,1024]{1,0:T(8,128)(2,1)S(1)}, bf16[8,1024]{1,0:T(8,128)(2,1)S(1)}, u32[]{:S(2)}, u32[]{:S(2)}) collective-permute-start(bf16[8,1024]{1,0:T(8,128)(2,1)S(1)} %get-tuple-element.73.refs_0_), channel_id=1, source_target_pairs={{0,8},{4,12},{8,0},{12,4},{1,9},{5,13},{9,1},{13,5},{2,10},{6,14},... | collective-permute-start | bytes 49160 | tf_op jit(solution)/shard_map/ppermute | solution.py:20
  25.4 1.1 %collective-permute-start.9 = (bf16[8,1024]{1,0:T(8,128)(2,1)S(1)}, bf16[8,1024]{1,0:T(8,128)(2,1)S(1)}, u32[]{:S(2)}, u32[]{:S(2)}) collective-permute-start(bf16[8,1024]{1,0:T(8,128)(2,1)S(1)} %get-tuple-element.73.refs_0_), channel_id=1, source_target_pairs={{0,4},{4,0},{8,12},{12,8},{1,5},{5,1},{9,13},{13,9},{2,6},{6,2},{1... | collective-permute-start | bytes 49160 | tf_op jit(solution)/shard_map/ppermute | solution.py:20
  26.5 0.4 expert_near.1.refs_3_
  26.8 0.9 %collective-permute-done.11.refs_2_ = bf16[8,1024]{1,0:T(8,128)(2,1)S(1)} collective-permute-done((bf16[8,1024]{1,0:T(8,128)(2,1)S(1)}, bf16[8,1024]{1,0:T(8,128)(2,1)S(1)}, u32[]{:S(2)}, u32[]{:S(2)}) %collective-permute-start.11) | collective-permute-done | bytes 16416 | tf_op jit(solution)/shard_map/ppermute | solution.py:20
  27.7 0.7 %collective-permute-done.10.refs_1_ = bf16[8,1024]{1,0:T(8,128)(2,1)S(1)} collective-permute-done((bf16[8,1024]{1,0:T(8,128)(2,1)S(1)}, bf16[8,1024]{1,0:T(8,128)(2,1)S(1)}, u32[]{:S(2)}, u32[]{:S(2)}) %collective-permute-start.10) | collective-permute-done | bytes 16416 | tf_op jit(solution)/shard_map/ppermute | solution.py:20
  28.4 1.8 %experts_far.1 = (bf16[4,8,256]{2,1,0:T(8,128)(2,1)S(1)}, bf16[8,1024]{1,0:T(8,128)(2,1)S(1)}, bf16[8,1024]{1,0:T(8,128)(2,1)S(1)}, bf16[8,1024]{1,0:T(8,128)(2,1)S(1)}) custom-call(bf16[8,1024]{1,0:T(8,128)(2,1)S(1)} %collective-permute-done.9.refs_0_, bf16[8,1024]{1,0:T(8,128)(2,1)S(1)} %collective-permute-done.10.refs_1_, ...), custom_call_target="tpu_custom_call" | custom-call | flops 16777216 | bytes 16777216 | tf_op jit(solution)/shard_map/experts_far/pallas_call | solution.py:66
  30.2 0.7 %collective-permute-start.12 = (bf16[8,1024]{1,0:T(8,128)(2,1)S(1)}, bf16[8,1024]{1,0:T(8,128)(2,1)S(1)}, u32[]{:S(2)}, u32[]{:S(2)}) collective-permute-start(bf16[8,1024]{1,0:T(8,128)(2,1)S(1)} %get-tuple-element.64), channel_id=1, source_target_pairs={{0,8},{4,12},{8,0},{12,4},{1,9},{5,13},{9,1},{13,5},{2,10},{6,14},... | collective-permute-start | bytes 49160 | tf_op jit(solution)/shard_map/ppermute | solution.py:20
  31.2 1.2 %collective-permute-start.14 = (bf16[8,1024]{1,0:T(8,128)(2,1)S(1)}, bf16[8,1024]{1,0:T(8,128)(2,1)S(1)}, u32[]{:S(2)}, u32[]{:S(2)}) collective-permute-start(bf16[8,1024]{1,0:T(8,128)(2,1)S(1)} %get-tuple-element.66), channel_id=1, source_target_pairs={{0,4},{4,0},{8,12},{12,8},{1,5},{5,1},{9,13},{13,9},{2,6},{6,2},{1... | collective-permute-start | bytes 49160 | tf_op jit(solution)/shard_map/ppermute | solution.py:20
  32.4 0.4 experts_close.1
  32.8 1.2 %collective-permute-done.12 = bf16[8,1024]{1,0:T(8,128)(2,1)S(1)} collective-permute-done((bf16[8,1024]{1,0:T(8,128)(2,1)S(1)}, bf16[8,1024]{1,0:T(8,128)(2,1)S(1)}, u32[]{:S(2)}, u32[]{:S(2)}) %collective-permute-start.12) | collective-permute-done | bytes 16416 | tf_op jit(solution)/shard_map/ppermute | solution.py:20
  34.3 1.9 %collective-permute-start.17 = (bf16[8,1024]{1,0:T(8,128)(2,1)S(1)}, bf16[8,1024]{1,0:T(8,128)(2,1)S(1)}, u32[]{:S(2)}, u32[]{:S(2)}) collective-permute-start(bf16[8,1024]{1,0:T(8,128)(2,1)S(1)} %get-tuple-element.71), channel_id=1, source_target_pairs={{0,3},{1,2},{2,1},{3,0},{4,7},{5,6},{6,5},{7,4},{8,11},{9,10},{10,... | collective-permute-start | bytes 49160 | tf_op jit(solution)/shard_map/ppermute | solution.py:36
  36.1 0.8 %collective-permute-start.16 = (bf16[8,1024]{1,0:T(8,128)(2,1)S(1)}, bf16[8,1024]{1,0:T(8,128)(2,1)S(1)}, u32[]{:S(2)}, u32[]{:S(2)}) collective-permute-start(bf16[8,1024]{1,0:T(8,128)(2,1)S(1)} %get-tuple-element.71), channel_id=1, source_target_pairs={{0,2},{1,3},{2,0},{3,1},{4,6},{5,7},{6,4},{7,5},{8,10},{9,11},{10,... | collective-permute-start | bytes 49160 | tf_op jit(solution)/shard_map/ppermute | solution.py:36
  36.9 1.8 %collective-permute-start.15 = (bf16[8,1024]{1,0:T(8,128)(2,1)S(1)}, bf16[8,1024]{1,0:T(8,128)(2,1)S(1)}, u32[]{:S(2)}, u32[]{:S(2)}) collective-permute-start(bf16[8,1024]{1,0:T(8,128)(2,1)S(1)} %get-tuple-element.71), channel_id=1, source_target_pairs={{0,1},{1,0},{2,3},{3,2},{4,5},{5,4},{6,7},{7,6},{8,9},{9,8},{10,11... | collective-permute-start | bytes 49160 | tf_op jit(solution)/shard_map/ppermute | solution.py:36
  38.7 1.1 %collective-permute-done.17.refs_4_ = bf16[8,1024]{1,0:T(8,128)(2,1)S(1)} collective-permute-done((bf16[8,1024]{1,0:T(8,128)(2,1)S(1)}, bf16[8,1024]{1,0:T(8,128)(2,1)S(1)}, u32[]{:S(2)}, u32[]{:S(2)}) %collective-permute-start.17) | collective-permute-done | bytes 16416 | tf_op jit(solution)/shard_map/ppermute | solution.py:36
  39.9 0.9 %collective-permute-done.16.refs_3_ = bf16[8,1024]{1,0:T(8,128)(2,1)S(1)} collective-permute-done((bf16[8,1024]{1,0:T(8,128)(2,1)S(1)}, bf16[8,1024]{1,0:T(8,128)(2,1)S(1)}, u32[]{:S(2)}, u32[]{:S(2)}) %collective-permute-start.16) | collective-permute-done | bytes 16416 | tf_op jit(solution)/shard_map/ppermute | solution.py:36
  40.8 0.6 %finish.1 = bf16[2,4,1024]{2,1,0:T(4,128)(2,1)} custom-call(f32[8,1024]{1,0:T(8,128)S(1)} %get-tuple-element.74.refs_0_, f32[8,1024]{1,0:T(8,128)S(1)} %get-tuple-element.72.refs_1_, bf16[8,1024]{1,0:T(8,128)(2,1)S(1)} %collective-permute-done.15.refs_2_, bf16[8,1024]{1,0:T(8,128)(2,1)S(1)} %collective-permute-done.16.refs_3_, ...), custom_call_target="tpu_custom_call" | custom-call | flops 1048576 | bytes 1048576 | tf_op jit(solution)/shard_map/finish/pallas_call | solution.py:66
  (26 shorter events, 1.0 us)
Async XLA Ops:
  5.0 5.2 %collective-permute-start = (bf16[2,4640]{1,0:T(2,128)(2,1)S(1)}, bf16[2,4640]{1,0:T(2,128)(2,1)S(1)}, u32[]{:S(2)}, u32[]{:S(2)}) collective-permute-start(bf16[2,4640]{1,0:T(2,128)(2,1)S(1)} %get-tuple-element.39), channel_id=1, source_target_pairs={{0,8},{4,12},{8,0},{12,4},{1,9},{5,13},{9,1},{13,5},{2,10},{6,14},... | collective-permute-start | bytes 55688 | tf_op jit(solution)/shard_map/ppermute | solution.py:20
  8.0 3.2 %collective-permute-start.1 = (bf16[2,4640]{1,0:T(2,128)(2,1)S(1)}, bf16[2,4640]{1,0:T(2,128)(2,1)S(1)}, u32[]{:S(2)}, u32[]{:S(2)}) collective-permute-start(bf16[2,4640]{1,0:T(2,128)(2,1)S(1)} %get-tuple-element.40), channel_id=1, source_target_pairs={{0,12},{4,8},{8,4},{12,0},{1,13},{5,9},{9,5},{13,1},{2,14},{6,10},... | collective-permute-start | bytes 55688 | tf_op jit(solution)/shard_map/ppermute | solution.py:20
  8.0 3.2 %collective-permute-start.2 = (bf16[2,4640]{1,0:T(2,128)(2,1)S(1)}, bf16[2,4640]{1,0:T(2,128)(2,1)S(1)}, u32[]{:S(2)}, u32[]{:S(2)}) collective-permute-start(bf16[2,4640]{1,0:T(2,128)(2,1)S(1)} %get-tuple-element.41), channel_id=1, source_target_pairs={{0,4},{4,0},{8,12},{12,8},{1,5},{5,1},{9,13},{13,9},{2,6},{6,2},{1... | collective-permute-start | bytes 55688 | tf_op jit(solution)/shard_map/ppermute | solution.py:20
  8.2 18.3 %slice-start = ((s8[8388608]{0:T(1024)(128)(4,1)}), s8[4194304]{0:T(1024)(128)(4,1)S(1)}, s32[]{:S(2)}) async-start(s8[8388608]{0:T(1024)(128)(4,1)} %bitcast.5), calls=%async_computation | async-start | bytes 8388608
  11.8 4.0 %collective-permute-start.5 = (bf16[2,2048]{1,0:T(2,128)(2,1)S(1)}, bf16[2,2048]{1,0:T(2,128)(2,1)S(1)}, u32[]{:S(2)}, u32[]{:S(2)}) collective-permute-start(bf16[2,2048]{1,0:T(2,128)(2,1)S(1)} %get-tuple-element.57.refs_0_), channel_id=1, source_target_pairs={{0,12},{4,8},{8,4},{12,0},{1,13},{5,9},{9,5},{13,1},{2,14},{6,10},... | collective-permute-start | bytes 24584 | tf_op jit(solution)/shard_map/ppermute | solution.py:20
  12.4 3.7 %collective-permute-start.4 = (bf16[2,2048]{1,0:T(2,128)(2,1)S(1)}, bf16[2,2048]{1,0:T(2,128)(2,1)S(1)}, u32[]{:S(2)}, u32[]{:S(2)}) collective-permute-start(bf16[2,2048]{1,0:T(2,128)(2,1)S(1)} %get-tuple-element.57.refs_0_), channel_id=1, source_target_pairs={{0,8},{4,12},{8,0},{12,4},{1,9},{5,13},{9,1},{13,5},{2,10},{6,14},... | collective-permute-start | bytes 24584 | tf_op jit(solution)/shard_map/ppermute | solution.py:20
  13.0 3.0 %collective-permute-start.3 = (bf16[2,2048]{1,0:T(2,128)(2,1)S(1)}, bf16[2,2048]{1,0:T(2,128)(2,1)S(1)}, u32[]{:S(2)}, u32[]{:S(2)}) collective-permute-start(bf16[2,2048]{1,0:T(2,128)(2,1)S(1)} %get-tuple-element.57.refs_0_), channel_id=1, source_target_pairs={{0,4},{4,0},{8,12},{12,8},{1,5},{5,1},{9,13},{13,9},{2,6},{6,2},{1... | collective-permute-start | bytes 24584 | tf_op jit(solution)/shard_map/ppermute | solution.py:20
  13.7 12.8 %slice-start.1 = ((s8[8388608]{0:T(1024)(128)(4,1)}), s8[4194304]{0:T(1024)(128)(4,1)S(1)}, s32[]{:S(2)}) async-start(s8[8388608]{0:T(1024)(128)(4,1)} %bitcast.5), calls=%async_computation.1 | async-start | bytes 8388608
  13.7 14.7 %slice-start.2 = ((s8[8388608]{0:T(1024)(128)(4,1)}), s8[4194304]{0:T(1024)(128)(4,1)S(1)}, s32[]{:S(2)}) async-start(s8[8388608]{0:T(1024)(128)(4,1)} %bitcast.7), calls=%async_computation.2 | async-start | bytes 8388608
  16.0 12.4 %slice-start.3 = ((s8[8388608]{0:T(1024)(128)(4,1)}), s8[4194304]{0:T(1024)(128)(4,1)S(1)}, s32[]{:S(2)}) async-start(s8[8388608]{0:T(1024)(128)(4,1)} %bitcast.7), calls=%async_computation.3 | async-start | bytes 8388608
  16.7 7.0 %collective-permute-start.8 = (bf16[8,1024]{1,0:T(8,128)(2,1)S(1)}, bf16[8,1024]{1,0:T(8,128)(2,1)S(1)}, u32[]{:S(2)}, u32[]{:S(2)}) collective-permute-start(bf16[8,1024]{1,0:T(8,128)(2,1)S(1)} %get-tuple-element.60), channel_id=1, source_target_pairs={{0,1},{1,3},{2,0},{3,2},{4,5},{5,7},{6,4},{7,6},{8,9},{9,11},{10,8... | collective-permute-start | bytes 49160 | tf_op jit(solution)/shard_map/ppermute | solution.py:36
  18.3 5.5 %collective-permute-start.7 = (bf16[8,1024]{1,0:T(8,128)(2,1)S(1)}, bf16[8,1024]{1,0:T(8,128)(2,1)S(1)}, u32[]{:S(2)}, u32[]{:S(2)}) collective-permute-start(bf16[8,1024]{1,0:T(8,128)(2,1)S(1)} %get-tuple-element.60), channel_id=1, source_target_pairs={{0,3},{1,2},{2,1},{3,0},{4,7},{5,6},{6,5},{7,4},{8,11},{9,10},{10,... | collective-permute-start | bytes 49160 | tf_op jit(solution)/shard_map/ppermute | solution.py:36
  20.8 3.7 %collective-permute-start.6 = (bf16[8,1024]{1,0:T(8,128)(2,1)S(1)}, bf16[8,1024]{1,0:T(8,128)(2,1)S(1)}, u32[]{:S(2)}, u32[]{:S(2)}) collective-permute-start(bf16[8,1024]{1,0:T(8,128)(2,1)S(1)} %get-tuple-element.60), channel_id=1, source_target_pairs={{0,2},{1,0},{2,3},{3,1},{4,6},{5,4},{6,7},{7,5},{8,10},{9,8},{10,1... | collective-permute-start | bytes 49160 | tf_op jit(solution)/shard_map/ppermute | solution.py:36
  24.5 3.2 %collective-permute-start.11 = (bf16[8,1024]{1,0:T(8,128)(2,1)S(1)}, bf16[8,1024]{1,0:T(8,128)(2,1)S(1)}, u32[]{:S(2)}, u32[]{:S(2)}) collective-permute-start(bf16[8,1024]{1,0:T(8,128)(2,1)S(1)} %get-tuple-element.73.refs_0_), channel_id=1, source_target_pairs={{0,12},{4,8},{8,4},{12,0},{1,13},{5,9},{9,5},{13,1},{2,14},{6,10},... | collective-permute-start | bytes 49160 | tf_op jit(solution)/shard_map/ppermute | solution.py:20
  24.6 3.8 %collective-permute-start.10 = (bf16[8,1024]{1,0:T(8,128)(2,1)S(1)}, bf16[8,1024]{1,0:T(8,128)(2,1)S(1)}, u32[]{:S(2)}, u32[]{:S(2)}) collective-permute-start(bf16[8,1024]{1,0:T(8,128)(2,1)S(1)} %get-tuple-element.73.refs_0_), channel_id=1, source_target_pairs={{0,8},{4,12},{8,0},{12,4},{1,9},{5,13},{9,1},{13,5},{2,10},{6,14},... | collective-permute-start | bytes 49160 | tf_op jit(solution)/shard_map/ppermute | solution.py:20
  25.4 3.0 %collective-permute-start.9 = (bf16[8,1024]{1,0:T(8,128)(2,1)S(1)}, bf16[8,1024]{1,0:T(8,128)(2,1)S(1)}, u32[]{:S(2)}, u32[]{:S(2)}) collective-permute-start(bf16[8,1024]{1,0:T(8,128)(2,1)S(1)} %get-tuple-element.73.refs_0_), channel_id=1, source_target_pairs={{0,4},{4,0},{8,12},{12,8},{1,5},{5,1},{9,13},{13,9},{2,6},{6,2},{1... | collective-permute-start | bytes 49160 | tf_op jit(solution)/shard_map/ppermute | solution.py:20
  30.2 3.8 %collective-permute-start.12 = (bf16[8,1024]{1,0:T(8,128)(2,1)S(1)}, bf16[8,1024]{1,0:T(8,128)(2,1)S(1)}, u32[]{:S(2)}, u32[]{:S(2)}) collective-permute-start(bf16[8,1024]{1,0:T(8,128)(2,1)S(1)} %get-tuple-element.64), channel_id=1, source_target_pairs={{0,8},{4,12},{8,0},{12,4},{1,9},{5,13},{9,1},{13,5},{2,10},{6,14},... | collective-permute-start | bytes 49160 | tf_op jit(solution)/shard_map/ppermute | solution.py:20
  30.9 3.3 %collective-permute-start.13 = (bf16[8,1024]{1,0:T(8,128)(2,1)S(1)}, bf16[8,1024]{1,0:T(8,128)(2,1)S(1)}, u32[]{:S(2)}, u32[]{:S(2)}) collective-permute-start(bf16[8,1024]{1,0:T(8,128)(2,1)S(1)} %get-tuple-element.65), channel_id=1, source_target_pairs={{0,12},{4,8},{8,4},{12,0},{1,13},{5,9},{9,5},{13,1},{2,14},{6,10},... | collective-permute-start | bytes 49160 | tf_op jit(solution)/shard_map/ppermute | solution.py:20
  31.2 3.1 %collective-permute-start.14 = (bf16[8,1024]{1,0:T(8,128)(2,1)S(1)}, bf16[8,1024]{1,0:T(8,128)(2,1)S(1)}, u32[]{:S(2)}, u32[]{:S(2)}) collective-permute-start(bf16[8,1024]{1,0:T(8,128)(2,1)S(1)} %get-tuple-element.66), channel_id=1, source_target_pairs={{0,4},{4,0},{8,12},{12,8},{1,5},{5,1},{9,13},{13,9},{2,6},{6,2},{1... | collective-permute-start | bytes 49160 | tf_op jit(solution)/shard_map/ppermute | solution.py:20
  34.3 5.6 %collective-permute-start.17 = (bf16[8,1024]{1,0:T(8,128)(2,1)S(1)}, bf16[8,1024]{1,0:T(8,128)(2,1)S(1)}, u32[]{:S(2)}, u32[]{:S(2)}) collective-permute-start(bf16[8,1024]{1,0:T(8,128)(2,1)S(1)} %get-tuple-element.71), channel_id=1, source_target_pairs={{0,3},{1,2},{2,1},{3,0},{4,7},{5,6},{6,5},{7,4},{8,11},{9,10},{10,... | collective-permute-start | bytes 49160 | tf_op jit(solution)/shard_map/ppermute | solution.py:36
  36.1 4.7 %collective-permute-start.16 = (bf16[8,1024]{1,0:T(8,128)(2,1)S(1)}, bf16[8,1024]{1,0:T(8,128)(2,1)S(1)}, u32[]{:S(2)}, u32[]{:S(2)}) collective-permute-start(bf16[8,1024]{1,0:T(8,128)(2,1)S(1)} %get-tuple-element.71), channel_id=1, source_target_pairs={{0,2},{1,3},{2,0},{3,1},{4,6},{5,7},{6,4},{7,5},{8,10},{9,11},{10,... | collective-permute-start | bytes 49160 | tf_op jit(solution)/shard_map/ppermute | solution.py:36
  36.9 3.9 %collective-permute-start.15 = (bf16[8,1024]{1,0:T(8,128)(2,1)S(1)}, bf16[8,1024]{1,0:T(8,128)(2,1)S(1)}, u32[]{:S(2)}, u32[]{:S(2)}) collective-permute-start(bf16[8,1024]{1,0:T(8,128)(2,1)S(1)} %get-tuple-element.71), channel_id=1, source_target_pairs={{0,1},{1,0},{2,3},{3,2},{4,5},{5,4},{6,7},{7,6},{8,9},{9,8},{10,11... | collective-permute-start | bytes 49160 | tf_op jit(solution)/shard_map/ppermute | solution.py:36

commit v7 on v6

--- a/solution.py
+++ b/solution.py
@@ -91,8 +91,8 @@
     return jax.ShapeDtypeStruct(tuple(shape), dtype)
 
 
-def sent_narrow(shape, slots):
-    return [shaped(shape)] + [shaped(shape, jnp.bfloat16)] * (slots - 1)
+def kept_and_sent(shape, slots):
+    return [shaped(shape)] * slots
 
 
 def project(owners, tokens, weights, step_weights):
@@ -169,7 +169,7 @@
     return local_kernel(
         body,
         "project",
-        sent_narrow((block, columns), owners),
+        kept_and_sent((block, columns), owners),
         [(tokens, IN_HBM), (step_weights, IN_HBM)] + [(w, IN_HBM) for w in weights],
         [
             pltpu.VMEM(tokens.shape, jnp.bfloat16),
@@ -443,12 +443,12 @@
             base += ref.shape[0]
         total = added(products)
         out_ref[...] = total
-        sent_ref[...] = total.astype(jnp.bfloat16)
+        sent_ref[...] = total.astype(sent_ref.dtype)
 
     return local_kernel(
         body,
         "project_out",
-        sent_narrow((rows * steps, parts[0].shape[1]), 2),
+        kept_and_sent((rows * steps, parts[0].shape[1]), 2),
         [(a, IN_VMEM) for a in (*normed, *parts)],
         [pltpu.VMEM((rows * steps, inner), jnp.float32)],
         bytes_accessed=4 << 20,
@@ -546,7 +546,7 @@
         body,
         "experts_far",
         [shaped((local_experts, many, hidden_width), jnp.bfloat16)]
-        + sent_narrow((many, width), 1 + len(far))[1:],
+        + kept_and_sent((many, width), 1 + len(far))[1:],
         [(a, IN_VMEM) for a in (*moe_in, near, chosen, gates, expert_up, expert_down)],
         bytes_accessed=16 << 20,
     )
@@ -566,7 +566,7 @@
     return local_kernel(
         body,
         "experts_close",
-        sent_narrow((many, width), 1),
+        kept_and_sent((many, width), 1),
         [(a, IN_VMEM) for a in (hidden, chosen, gates, expert_down)],
         bytes_accessed=4 << 20,
     )
@@ -648,7 +648,7 @@
     )
     moe_sum = [*experts_close(hidden, expert_ids, route_gates, expert_down, owners), *far]
     moe_sum = added(scatter_parts(moe_sum, "expert"))
-    mixed_out = finish([residual] + sum_parts(moe_sum, "tensor", moe_sum.astype(jnp.bfloat16), ((1, 0, 3, 2), (2, 3, 0, 1), (3, 2, 1, 0))), tokens.shape)
+    mixed_out = finish([residual] + sum_parts(moe_sum, "tensor", moe_sum, ((1, 0, 3, 2), (2, 3, 0, 1), (3, 2, 1, 0))), tokens.shape)
     return (mixed_out, ssm_final, *finals)
 
 

time: 41.7 us -> 43.2 us (1.036)
  waiting for transfers between devices: 7.27 us -> 8.52 us
    ppermute x6, waiting for transfers between devices: 2.91 us -> 3.57 us  [sum_parts(): lax.ppermute(sent, axis, list(enumerate(p)))]
    ppermute x12, waiting for transfers between devices: 4.35 us -> 4.95 us  [swap(): return lax.ppermute(values, axis, [(i, i ^ distance) for i in range(size)])]
  transfers between devices with their start and end apart: 18 -> 18, of which waited for: 10 -> 10; matrix products, arithmetic and copies ran while one was open for 0% -> 0% of each run, Pallas kernels for 15% -> 14%
where the time goes in v7:
time: 43.2 us; the launch traced here: 43 us
  starting transfers between devices  19.6 us (45%)
  Pallas kernels  14.1 us (33%)
  waiting for transfers between devices  8.52 us (20%)
  between operations  0.75 us (2%)
    pallas_call x10, Pallas kernels, local_kernel(): pl.pallas_call(body, out_shape=out_shape, in_specs=[spec for _, spec in i...  14.1 us
    ppermute x6, starting transfers between devices, sum_parts(): lax.ppermute(sent, axis, list(enumerate(p)))  10.4 us
    ppermute x12, starting transfers between devices, swap(): return lax.ppermute(values, axis, [(i, i ^ distance) for i in range(size)])  9.21 us
    ppermute x12, waiting for transfers between devices, swap(): return lax.ppermute(values, axis, [(i, i ^ distance) for i in range(size)])  4.95 us
    ppermute x6, waiting for transfers between devices, sum_parts(): lax.ppermute(sent, axis, list(enumerate(p)))  3.57 us
  transfers between devices with their start and end apart: 18, of which 10 were waited for; matrix products, arithmetic and copies ran while one was open for 0% of the time, Pallas kernels for 14%

profile of v7, /device:TPU:0, one launch (start us, length us, event | category | flops | bytes accessed | tf_op | source)
XLA Modules:
  0.0 43.0 jit_solution(15408399830573510180)
XLA Ops:
  0.6 4.3 %project.1 = (f32[2,4640]{1,0:T(2,128)S(1)}, f32[2,4640]{1,0:T(2,128)S(1)}, f32[2,4640]{1,0:T(2,128)S(1)}, f32[2,4640]{1,0:T(2,128)S(1)}) custom-call(bf16[2,4,1024]{2,1,0:T(4,128)(2,1)} %refs_11_.1, bf16[32,1024]{1,0:T(8,128)(2,1)} %bitcast.9, bf16[1024,2048]{1,0:T(8,128)(2,1)} %refs_2_.1, bf16[1024,2048]{1,0:T(8,128)(2,1)} %refs_3_.2, ...), custom_call_target="tpu_custom_call" | custom-call | flops 10485760 | bytes 10485760 | tf_op jit(solution)/shard_map/project/pallas_call | solution.py:66
  5.0 3.0 %collective-permute-start = (f32[2,4640]{1,0:T(2,128)S(1)}, f32[2,4640]{1,0:T(2,128)S(1)}, u32[]{:S(2)}, u32[]{:S(2)}) collective-permute-start(f32[2,4640]{1,0:T(2,128)S(1)} %get-tuple-element.39), channel_id=1, source_target_pairs={{0,8},{4,12},{8,0},{12,4},{1,9},{5,13},{9,1},{13,5},{2,10},{6,14},... | collective-permute-start | bytes 111368 | tf_op jit(solution)/shard_map/ppermute | solution.py:20
  8.2 2.0 %prepare.1 = (f32[3,2048]{1,0:T(4,128)S(1)}, bf16[32,2048]{1,0:T(8,128)(2,1)S(1)}, f32[4,2048]{1,0:T(4,128)S(1)}, f32[4,256]{1,0:T(4,128)S(1)}, f32[4,256]{1,0:T...) custom-call(f32[1,32]{1,0:T(1,128)} %bitcast.11, ...), custom_call_target="tpu_custom_call" | custom-call | flops 4194304 | bytes 4194304 | tf_op jit(solution)/shard_map/prepare/pallas_call | solution.py:66
  10.1 1.4 %collective-permute-done.1.refs_2_ = f32[2,4640]{1,0:T(2,128)S(1)} collective-permute-done((f32[2,4640]{1,0:T(2,128)S(1)}, f32[2,4640]{1,0:T(2,128)S(1)}, u32[]{:S(2)}, u32[]{:S(2)}) %collective-permute-start.1) | collective-permute-done | bytes 37152 | tf_op jit(solution)/shard_map/ppermute | solution.py:20
  11.5 0.6 %mix.1 = (bf16[2,2048]{1,0:T(2,128)(2,1)S(1)}, f32[2,2560]{1,0:T(2,128)S(1)}, f32[1,3,2048]{2,1,0:T(4,128)S(1)}, f32[2,256]{1,0:T(2,128)S(1)}) custom-call(f32[2,4640]{1,0:T(2,128)S(1)} %get-tuple-element.38.refs_0_, f32[2,4640]{1,0:T(2,128)S(1)} %collective-permute-done.refs_1_, f32[2,4640]{1,0:T(2,128)S(1)} %collective-permute-done.1.refs_2_, ...), custom_call_target="tpu_custom_call" | custom-call | flops 4194304 | bytes 4194304 | tf_op jit(solution)/shard_map/mix/pallas_call | solution.py:66
  12.4 1.2 %collective-permute-start.4 = (bf16[2,2048]{1,0:T(2,128)(2,1)S(1)}, bf16[2,2048]{1,0:T(2,128)(2,1)S(1)}, u32[]{:S(2)}, u32[]{:S(2)}) collective-permute-start(bf16[2,2048]{1,0:T(2,128)(2,1)S(1)} %get-tuple-element.57.refs_0_), channel_id=1, source_target_pairs={{0,8},{4,12},{8,0},{12,4},{1,9},{5,13},{9,1},{13,5},{2,10},{6,14},... | collective-permute-start | bytes 24584 | tf_op jit(solution)/shard_map/ppermute | solution.py:20
  13.6 0.4 collective-permute-start.3
  14.0 2.0 %fetch.1.refs_5_ = bf16[1536,1024]{1,0:T(8,128)(2,1)S(1)} custom-call(bf16[2048,1024]{1,0:T(8,128)(2,1)} %source.1, f32[2,256]{1,0:T(2,128)S(1)} %get-tuple-element.54.write_ref._), custom_call_target="tpu_custom_call" | custom-call | flops 8388608 | bytes 8388608 | tf_op jit(solution)/shard_map/fetch/pallas_call | solution.py:66
  16.1 0.6 %project_out.1 = (f32[8,1024]{1,0:T(8,128)S(1)}, f32[8,1024]{1,0:T(8,128)S(1)}) custom-call(bf16[2,2048]{1,0:T(2,128)(2,1)S(1)} %get-tuple-element.57.refs_0_, bf16[2,2048]{1,0:T(2,128)(2,1)S(1)} %collective-permute-done.3.refs_1_, bf16[2,2048]{1,0:T(2,128)(2,1)S(1)} %collective-permute-done.4.refs_2_, bf16[2,2048]{1,0:T(2,128)(2,1)S(1)} %collective-permute-done.5.refs_3_, ...), custom_call_target="tpu_custom_call" | custom-call | flops 4194304 | bytes 4194304 | tf_op jit(solution)/shard_map/project_out/pallas_call | solution.py:66
  16.8 1.9 %collective-permute-start.8 = (f32[8,1024]{1,0:T(8,128)S(1)}, f32[8,1024]{1,0:T(8,128)S(1)}, u32[]{:S(2)}, u32[]{:S(2)}) collective-permute-start(f32[8,1024]{1,0:T(8,128)S(1)} %get-tuple-element.60), channel_id=1, source_target_pairs={{0,1},{1,3},{2,0},{3,2},{4,5},{5,7},{6,4},{7,6},{8,9},{9,11},{10,8... | collective-permute-start | bytes 98312 | tf_op jit(solution)/shard_map/ppermute | solution.py:36
  18.7 2.5 %collective-permute-start.7 = (f32[8,1024]{1,0:T(8,128)S(1)}, f32[8,1024]{1,0:T(8,128)S(1)}, u32[]{:S(2)}, u32[]{:S(2)}) collective-permute-start(f32[8,1024]{1,0:T(8,128)S(1)} %get-tuple-element.60), channel_id=1, source_target_pairs={{0,3},{1,2},{2,1},{3,0},{4,7},{5,6},{6,5},{7,4},{8,11},{9,10},{10,... | collective-permute-start | bytes 98312 | tf_op jit(solution)/shard_map/ppermute | solution.py:36
  21.2 1.6 %collective-permute-start.6 = (f32[8,1024]{1,0:T(8,128)S(1)}, f32[8,1024]{1,0:T(8,128)S(1)}, u32[]{:S(2)}, u32[]{:S(2)}) collective-permute-start(f32[8,1024]{1,0:T(8,128)S(1)} %get-tuple-element.60), channel_id=1, source_target_pairs={{0,2},{1,0},{2,3},{3,1},{4,6},{5,4},{6,7},{7,5},{8,10},{9,8},{10,1... | collective-permute-start | bytes 98312 | tf_op jit(solution)/shard_map/ppermute | solution.py:36
  22.7 1.3 %renew.1 = (f32[1,32,64,128]{3,2,1,0:T(8,128)}, f32[8,1024]{1,0:T(8,128)S(1)}, bf16[1,3,2048]{2,1,0:T(4,128)(2,1)}, bf16[1,3,256]{2,1,0:T(4,128)(2,1)}, bf16[1,3,256]{2,1,0:T(4,128)(2,1)}) custom-call(f32[2,2560]{1,0:T(2,128)S(1)} %get-tuple-element.52.pre_ref, f32[1,3,2048]{2,1,0:T(4,128)S(1)} %get-tuple-element.53.coef_ref, ...), custom_call_target="tpu_custom_call" | custom-call | flops 4194304 | bytes 4194304 | tf_op jit(solution)/shard_map/renew/pallas_call | solution.py:66
  24.1 0.4 collective-permute-done.7
  24.4 0.6 %collective-permute-done.6 = f32[8,1024]{1,0:T(8,128)S(1)} collective-permute-done((f32[8,1024]{1,0:T(8,128)S(1)}, f32[8,1024]{1,0:T(8,128)S(1)}, u32[]{:S(2)}, u32[]{:S(2)}) %collective-permute-start.6) | collective-permute-done | bytes 32800 | tf_op jit(solution)/shard_map/ppermute | solution.py:36
  25.2 0.9 %collective-permute-start.10 = (bf16[8,1024]{1,0:T(8,128)(2,1)S(1)}, bf16[8,1024]{1,0:T(8,128)(2,1)S(1)}, u32[]{:S(2)}, u32[]{:S(2)}) collective-permute-start(bf16[8,1024]{1,0:T(8,128)(2,1)S(1)} %get-tuple-element.71.refs_0_), channel_id=1, source_target_pairs={{0,8},{4,12},{8,0},{12,4},{1,9},{5,13},{9,1},{13,5},{2,10},{6,14},... | collective-permute-start | bytes 49160 | tf_op jit(solution)/shard_map/ppermute | solution.py:20
  26.1 0.9 %collective-permute-start.9 = (bf16[8,1024]{1,0:T(8,128)(2,1)S(1)}, bf16[8,1024]{1,0:T(8,128)(2,1)S(1)}, u32[]{:S(2)}, u32[]{:S(2)}) collective-permute-start(bf16[8,1024]{1,0:T(8,128)(2,1)S(1)} %get-tuple-element.71.refs_0_), channel_id=1, source_target_pairs={{0,4},{4,0},{8,12},{12,8},{1,5},{5,1},{9,13},{13,9},{2,6},{6,2},{1... | collective-permute-start | bytes 49160 | tf_op jit(solution)/shard_map/ppermute | solution.py:20
  27.0 0.4 expert_near.1.refs_3_
  27.4 0.9 %collective-permute-done.11.refs_2_ = bf16[8,1024]{1,0:T(8,128)(2,1)S(1)} collective-permute-done((bf16[8,1024]{1,0:T(8,128)(2,1)S(1)}, bf16[8,1024]{1,0:T(8,128)(2,1)S(1)}, u32[]{:S(2)}, u32[]{:S(2)}) %collective-permute-start.11) | collective-permute-done | bytes 16416 | tf_op jit(solution)/shard_map/ppermute | solution.py:20
  28.3 0.8 %collective-permute-done.10.refs_1_ = bf16[8,1024]{1,0:T(8,128)(2,1)S(1)} collective-permute-done((bf16[8,1024]{1,0:T(8,128)(2,1)S(1)}, bf16[8,1024]{1,0:T(8,128)(2,1)S(1)}, u32[]{:S(2)}, u32[]{:S(2)}) %collective-permute-start.10) | collective-permute-done | bytes 16416 | tf_op jit(solution)/shard_map/ppermute | solution.py:20
  29.1 1.8 %experts_far.1 = (bf16[4,8,256]{2,1,0:T(8,128)(2,1)S(1)}, f32[8,1024]{1,0:T(8,128)S(1)}, f32[8,1024]{1,0:T(8,128)S(1)}, f32[8,1024]{1,0:T(8,128)S(1)}) custom-call(bf16[8,1024]{1,0:T(8,128)(2,1)S(1)} %collective-permute-done.9.refs_0_, bf16[8,1024]{1,0:T(8,128)(2,1)S(1)} %collective-permute-done.10.refs_1_, ...), custom_call_target="tpu_custom_call" | custom-call | flops 16777216 | bytes 16777216 | tf_op jit(solution)/shard_map/experts_far/pallas_call | solution.py:66
  30.9 0.8 %collective-permute-start.12 = (f32[8,1024]{1,0:T(8,128)S(1)}, f32[8,1024]{1,0:T(8,128)S(1)}, u32[]{:S(2)}, u32[]{:S(2)}) collective-permute-start(f32[8,1024]{1,0:T(8,128)S(1)} %get-tuple-element.64), channel_id=1, source_target_pairs={{0,8},{4,12},{8,0},{12,4},{1,9},{5,13},{9,1},{13,5},{2,10},{6,14},... | collective-permute-start | bytes 98312 | tf_op jit(solution)/shard_map/ppermute | solution.py:20
  31.7 0.6 %collective-permute-start.13 = (f32[8,1024]{1,0:T(8,128)S(1)}, f32[8,1024]{1,0:T(8,128)S(1)}, u32[]{:S(2)}, u32[]{:S(2)}) collective-permute-start(f32[8,1024]{1,0:T(8,128)S(1)} %get-tuple-element.65), channel_id=1, source_target_pairs={{0,12},{4,8},{8,4},{12,0},{1,13},{5,9},{9,5},{13,1},{2,14},{6,10},... | collective-permute-start | bytes 98312 | tf_op jit(solution)/shard_map/ppermute | solution.py:20
  32.3 0.7 %collective-permute-start.14 = (f32[8,1024]{1,0:T(8,128)S(1)}, f32[8,1024]{1,0:T(8,128)S(1)}, u32[]{:S(2)}, u32[]{:S(2)}) collective-permute-start(f32[8,1024]{1,0:T(8,128)S(1)} %get-tuple-element.66), channel_id=1, source_target_pairs={{0,4},{4,0},{8,12},{12,8},{1,5},{5,1},{9,13},{13,9},{2,6},{6,2},{1... | collective-permute-start | bytes 98312 | tf_op jit(solution)/shard_map/ppermute | solution.py:20
  33.0 0.4 experts_close.1
  33.4 1.5 %collective-permute-done.12 = f32[8,1024]{1,0:T(8,128)S(1)} collective-permute-done((f32[8,1024]{1,0:T(8,128)S(1)}, f32[8,1024]{1,0:T(8,128)S(1)}, u32[]{:S(2)}, u32[]{:S(2)}) %collective-permute-start.12) | collective-permute-done | bytes 32800 | tf_op jit(solution)/shard_map/ppermute | solution.py:20
  35.4 2.0 %collective-permute-start.17 = (f32[8,1024]{1,0:T(8,128)S(1)}, f32[8,1024]{1,0:T(8,128)S(1)}, u32[]{:S(2)}, u32[]{:S(2)}) collective-permute-start(f32[8,1024]{1,0:T(8,128)S(1)} %add_add_fusion.refs_1_), channel_id=1, source_target_pairs={{0,3},{1,2},{2,1},{3,0},{4,7},{5,6},{6,5},{7,4},{8,11},{9,10},{10,... | collective-permute-start | bytes 98312 | tf_op jit(solution)/shard_map/ppermute | solution.py:36
  37.4 0.6 %collective-permute-start.16 = (f32[8,1024]{1,0:T(8,128)S(1)}, f32[8,1024]{1,0:T(8,128)S(1)}, u32[]{:S(2)}, u32[]{:S(2)}) collective-permute-start(f32[8,1024]{1,0:T(8,128)S(1)} %add_add_fusion.refs_1_), channel_id=1, source_target_pairs={{0,2},{1,3},{2,0},{3,1},{4,6},{5,7},{6,4},{7,5},{8,10},{9,11},{10,... | collective-permute-start | bytes 98312 | tf_op jit(solution)/shard_map/ppermute | solution.py:36
  38.0 1.9 %collective-permute-start.15 = (f32[8,1024]{1,0:T(8,128)S(1)}, f32[8,1024]{1,0:T(8,128)S(1)}, u32[]{:S(2)}, u32[]{:S(2)}) collective-permute-start(f32[8,1024]{1,0:T(8,128)S(1)} %add_add_fusion.refs_1_), channel_id=1, source_target_pairs={{0,1},{1,0},{2,3},{3,2},{4,5},{5,4},{6,7},{7,6},{8,9},{9,8},{10,11... | collective-permute-start | bytes 98312 | tf_op jit(solution)/shard_map/ppermute | solution.py:36
  39.8 1.5 %collective-permute-done.17.refs_4_ = f32[8,1024]{1,0:T(8,128)S(1)} collective-permute-done((f32[8,1024]{1,0:T(8,128)S(1)}, f32[8,1024]{1,0:T(8,128)S(1)}, u32[]{:S(2)}, u32[]{:S(2)}) %collective-permute-start.17) | collective-permute-done | bytes 32800 | tf_op jit(solution)/shard_map/ppermute | solution.py:36
  41.3 0.9 %collective-permute-done.16.refs_3_ = f32[8,1024]{1,0:T(8,128)S(1)} collective-permute-done((f32[8,1024]{1,0:T(8,128)S(1)}, f32[8,1024]{1,0:T(8,128)S(1)}, u32[]{:S(2)}, u32[]{:S(2)}) %collective-permute-start.16) | collective-permute-done | bytes 32800 | tf_op jit(solution)/shard_map/ppermute | solution.py:36
  42.4 0.6 %finish.1 = bf16[2,4,1024]{2,1,0:T(4,128)(2,1)} custom-call(f32[8,1024]{1,0:T(8,128)S(1)} %get-tuple-element.72.refs_0_, f32[8,1024]{1,0:T(8,128)S(1)} %add_add_fusion.refs_1_, f32[8,1024]{1,0:T(8,128)S(1)} %collective-permute-done.15.refs_2_, f32[8,1024]{1,0:T(8,128)S(1)} %collective-permute-done.16.refs_3_, f32[8,1024]{1,0:T(8,128)S(1)} %collective-permute-done.17.refs_4_), custom_call_target="tpu_custom_call" | custom-call | flops 1048576 | bytes 1048576 | tf_op jit(solution)/shard_map/finish/pallas_call | solution.py:66
  (26 shorter events, 1.2 us)
Async XLA Ops:
  5.0 5.2 %collective-permute-start = (f32[2,4640]{1,0:T(2,128)S(1)}, f32[2,4640]{1,0:T(2,128)S(1)}, u32[]{:S(2)}, u32[]{:S(2)}) collective-permute-start(f32[2,4640]{1,0:T(2,128)S(1)} %get-tuple-element.39), channel_id=1, source_target_pairs={{0,8},{4,12},{8,0},{12,4},{1,9},{5,13},{9,1},{13,5},{2,10},{6,14},... | collective-permute-start | bytes 111368 | tf_op jit(solution)/shard_map/ppermute | solution.py:20
  8.0 3.5 %collective-permute-start.1 = (f32[2,4640]{1,0:T(2,128)S(1)}, f32[2,4640]{1,0:T(2,128)S(1)}, u32[]{:S(2)}, u32[]{:S(2)}) collective-permute-start(f32[2,4640]{1,0:T(2,128)S(1)} %get-tuple-element.40), channel_id=1, source_target_pairs={{0,12},{4,8},{8,4},{12,0},{1,13},{5,9},{9,5},{13,1},{2,14},{6,10},... | collective-permute-start | bytes 111368 | tf_op jit(solution)/shard_map/ppermute | solution.py:20
  8.0 3.5 %collective-permute-start.2 = (f32[2,4640]{1,0:T(2,128)S(1)}, f32[2,4640]{1,0:T(2,128)S(1)}, u32[]{:S(2)}, u32[]{:S(2)}) collective-permute-start(f32[2,4640]{1,0:T(2,128)S(1)} %get-tuple-element.41), channel_id=1, source_target_pairs={{0,4},{4,0},{8,12},{12,8},{1,5},{5,1},{9,13},{13,9},{2,6},{6,2},{1... | collective-permute-start | bytes 111368 | tf_op jit(solution)/shard_map/ppermute | solution.py:20
  8.2 18.9 %slice-start = ((s8[8388608]{0:T(1024)(128)(4,1)}), s8[4194304]{0:T(1024)(128)(4,1)S(1)}, s32[]{:S(2)}) async-start(s8[8388608]{0:T(1024)(128)(4,1)} %bitcast.5), calls=%async_computation | async-start | bytes 8388608
  12.1 4.0 %collective-permute-start.5 = (bf16[2,2048]{1,0:T(2,128)(2,1)S(1)}, bf16[2,2048]{1,0:T(2,128)(2,1)S(1)}, u32[]{:S(2)}, u32[]{:S(2)}) collective-permute-start(bf16[2,2048]{1,0:T(2,128)(2,1)S(1)} %get-tuple-element.57.refs_0_), channel_id=1, source_target_pairs={{0,12},{4,8},{8,4},{12,0},{1,13},{5,9},{9,5},{13,1},{2,14},{6,10},... | collective-permute-start | bytes 24584 | tf_op jit(solution)/shard_map/ppermute | solution.py:20
  12.4 3.7 %collective-permute-start.4 = (bf16[2,2048]{1,0:T(2,128)(2,1)S(1)}, bf16[2,2048]{1,0:T(2,128)(2,1)S(1)}, u32[]{:S(2)}, u32[]{:S(2)}) collective-permute-start(bf16[2,2048]{1,0:T(2,128)(2,1)S(1)} %get-tuple-element.57.refs_0_), channel_id=1, source_target_pairs={{0,8},{4,12},{8,0},{12,4},{1,9},{5,13},{9,1},{13,5},{2,10},{6,14},... | collective-permute-start | bytes 24584 | tf_op jit(solution)/shard_map/ppermute | solution.py:20
  13.6 2.5 %collective-permute-start.3 = (bf16[2,2048]{1,0:T(2,128)(2,1)S(1)}, bf16[2,2048]{1,0:T(2,128)(2,1)S(1)}, u32[]{:S(2)}, u32[]{:S(2)}) collective-permute-start(bf16[2,2048]{1,0:T(2,128)(2,1)S(1)} %get-tuple-element.57.refs_0_), channel_id=1, source_target_pairs={{0,4},{4,0},{8,12},{12,8},{1,5},{5,1},{9,13},{13,9},{2,6},{6,2},{1... | collective-permute-start | bytes 24584 | tf_op jit(solution)/shard_map/ppermute | solution.py:20
  14.0 13.0 %slice-start.1 = ((s8[8388608]{0:T(1024)(128)(4,1)}), s8[4194304]{0:T(1024)(128)(4,1)S(1)}, s32[]{:S(2)}) async-start(s8[8388608]{0:T(1024)(128)(4,1)} %bitcast.5), calls=%async_computation.1 | async-start | bytes 8388608
  14.0 15.1 %slice-start.2 = ((s8[8388608]{0:T(1024)(128)(4,1)}), s8[4194304]{0:T(1024)(128)(4,1)S(1)}, s32[]{:S(2)}) async-start(s8[8388608]{0:T(1024)(128)(4,1)} %bitcast.7), calls=%async_computation.2 | async-start | bytes 8388608
  16.1 13.0 %slice-start.3 = ((s8[8388608]{0:T(1024)(128)(4,1)}), s8[4194304]{0:T(1024)(128)(4,1)S(1)}, s32[]{:S(2)}) async-start(s8[8388608]{0:T(1024)(128)(4,1)} %bitcast.7), calls=%async_computation.3 | async-start | bytes 8388608
  16.8 7.3 %collective-permute-start.8 = (f32[8,1024]{1,0:T(8,128)S(1)}, f32[8,1024]{1,0:T(8,128)S(1)}, u32[]{:S(2)}, u32[]{:S(2)}) collective-permute-start(f32[8,1024]{1,0:T(8,128)S(1)} %get-tuple-element.60), channel_id=1, source_target_pairs={{0,1},{1,3},{2,0},{3,2},{4,5},{5,7},{6,4},{7,6},{8,9},{9,11},{10,8... | collective-permute-start | bytes 98312 | tf_op jit(solution)/shard_map/ppermute | solution.py:36
  18.7 5.8 %collective-permute-start.7 = (f32[8,1024]{1,0:T(8,128)S(1)}, f32[8,1024]{1,0:T(8,128)S(1)}, u32[]{:S(2)}, u32[]{:S(2)}) collective-permute-start(f32[8,1024]{1,0:T(8,128)S(1)} %get-tuple-element.60), channel_id=1, source_target_pairs={{0,3},{1,2},{2,1},{3,0},{4,7},{5,6},{6,5},{7,4},{8,11},{9,10},{10,... | collective-permute-start | bytes 98312 | tf_op jit(solution)/shard_map/ppermute | solution.py:36
  21.2 3.9 %collective-permute-start.6 = (f32[8,1024]{1,0:T(8,128)S(1)}, f32[8,1024]{1,0:T(8,128)S(1)}, u32[]{:S(2)}, u32[]{:S(2)}) collective-permute-start(f32[8,1024]{1,0:T(8,128)S(1)} %get-tuple-element.60), channel_id=1, source_target_pairs={{0,2},{1,0},{2,3},{3,1},{4,6},{5,4},{6,7},{7,5},{8,10},{9,8},{10,1... | collective-permute-start | bytes 98312 | tf_op jit(solution)/shard_map/ppermute | solution.py:36
  25.1 3.2 %collective-permute-start.11 = (bf16[8,1024]{1,0:T(8,128)(2,1)S(1)}, bf16[8,1024]{1,0:T(8,128)(2,1)S(1)}, u32[]{:S(2)}, u32[]{:S(2)}) collective-permute-start(bf16[8,1024]{1,0:T(8,128)(2,1)S(1)} %get-tuple-element.71.refs_0_), channel_id=1, source_target_pairs={{0,12},{4,8},{8,4},{12,0},{1,13},{5,9},{9,5},{13,1},{2,14},{6,10},... | collective-permute-start | bytes 49160 | tf_op jit(solution)/shard_map/ppermute | solution.py:20
  25.2 3.9 %collective-permute-start.10 = (bf16[8,1024]{1,0:T(8,128)(2,1)S(1)}, bf16[8,1024]{1,0:T(8,128)(2,1)S(1)}, u32[]{:S(2)}, u32[]{:S(2)}) collective-permute-start(bf16[8,1024]{1,0:T(8,128)(2,1)S(1)} %get-tuple-element.71.refs_0_), channel_id=1, source_target_pairs={{0,8},{4,12},{8,0},{12,4},{1,9},{5,13},{9,1},{13,5},{2,10},{6,14},... | collective-permute-start | bytes 49160 | tf_op jit(solution)/shard_map/ppermute | solution.py:20
  26.1 3.0 %collective-permute-start.9 = (bf16[8,1024]{1,0:T(8,128)(2,1)S(1)}, bf16[8,1024]{1,0:T(8,128)(2,1)S(1)}, u32[]{:S(2)}, u32[]{:S(2)}) collective-permute-start(bf16[8,1024]{1,0:T(8,128)(2,1)S(1)} %get-tuple-element.71.refs_0_), channel_id=1, source_target_pairs={{0,4},{4,0},{8,12},{12,8},{1,5},{5,1},{9,13},{13,9},{2,6},{6,2},{1... | collective-permute-start | bytes 49160 | tf_op jit(solution)/shard_map/ppermute | solution.py:20
  30.9 4.1 %collective-permute-start.12 = (f32[8,1024]{1,0:T(8,128)S(1)}, f32[8,1024]{1,0:T(8,128)S(1)}, u32[]{:S(2)}, u32[]{:S(2)}) collective-permute-start(f32[8,1024]{1,0:T(8,128)S(1)} %get-tuple-element.64), channel_id=1, source_target_pairs={{0,8},{4,12},{8,0},{12,4},{1,9},{5,13},{9,1},{13,5},{2,10},{6,14},... | collective-permute-start | bytes 98312 | tf_op jit(solution)/shard_map/ppermute | solution.py:20
  31.7 3.7 %collective-permute-start.13 = (f32[8,1024]{1,0:T(8,128)S(1)}, f32[8,1024]{1,0:T(8,128)S(1)}, u32[]{:S(2)}, u32[]{:S(2)}) collective-permute-start(f32[8,1024]{1,0:T(8,128)S(1)} %get-tuple-element.65), channel_id=1, source_target_pairs={{0,12},{4,8},{8,4},{12,0},{1,13},{5,9},{9,5},{13,1},{2,14},{6,10},... | collective-permute-start | bytes 98312 | tf_op jit(solution)/shard_map/ppermute | solution.py:20
  32.3 3.0 %collective-permute-start.14 = (f32[8,1024]{1,0:T(8,128)S(1)}, f32[8,1024]{1,0:T(8,128)S(1)}, u32[]{:S(2)}, u32[]{:S(2)}) collective-permute-start(f32[8,1024]{1,0:T(8,128)S(1)} %get-tuple-element.66), channel_id=1, source_target_pairs={{0,4},{4,0},{8,12},{12,8},{1,5},{5,1},{9,13},{13,9},{2,6},{6,2},{1... | collective-permute-start | bytes 98312 | tf_op jit(solution)/shard_map/ppermute | solution.py:20
  35.4 5.9 %collective-permute-start.17 = (f32[8,1024]{1,0:T(8,128)S(1)}, f32[8,1024]{1,0:T(8,128)S(1)}, u32[]{:S(2)}, u32[]{:S(2)}) collective-permute-start(f32[8,1024]{1,0:T(8,128)S(1)} %add_add_fusion.refs_1_), channel_id=1, source_target_pairs={{0,3},{1,2},{2,1},{3,0},{4,7},{5,6},{6,5},{7,4},{8,11},{9,10},{10,... | collective-permute-start | bytes 98312 | tf_op jit(solution)/shard_map/ppermute | solution.py:36
  37.4 4.9 %collective-permute-start.16 = (f32[8,1024]{1,0:T(8,128)S(1)}, f32[8,1024]{1,0:T(8,128)S(1)}, u32[]{:S(2)}, u32[]{:S(2)}) collective-permute-start(f32[8,1024]{1,0:T(8,128)S(1)} %add_add_fusion.refs_1_), channel_id=1, source_target_pairs={{0,2},{1,3},{2,0},{3,1},{4,6},{5,7},{6,4},{7,5},{8,10},{9,11},{10,... | collective-permute-start | bytes 98312 | tf_op jit(solution)/shard_map/ppermute | solution.py:36
  38.0 4.4 %collective-permute-start.15 = (f32[8,1024]{1,0:T(8,128)S(1)}, f32[8,1024]{1,0:T(8,128)S(1)}, u32[]{:S(2)}, u32[]{:S(2)}) collective-permute-start(f32[8,1024]{1,0:T(8,128)S(1)} %add_add_fusion.refs_1_), channel_id=1, source_target_pairs={{0,1},{1,0},{2,3},{3,2},{4,5},{5,4},{6,7},{7,6},{8,9},{9,8},{10,11... | collective-permute-start | bytes 98312 | tf_op jit(solution)/shard_map/ppermute | solution.py:36

commit v8 on v6

--- a/solution.py
+++ b/solution.py
@@ -58,6 +58,7 @@
 IN_VMEM = pl.BlockSpec(memory_space=pltpu.VMEM)
 IN_HBM = pl.BlockSpec(memory_space=pltpu.HBM)
 CHUNK = 512 * 1024
+COLUMNS = 512
 FIRST = 4
 NEAR = 1
 
@@ -102,10 +103,19 @@
     heads = step_weights.shape[0]
     columns = sum(widths) + heads
     block = own_rows * steps
+    last = widths.index(max(widths), 1)
     pieces = []
     for index, width in enumerate(widths):
         size = max(16, min(depth, CHUNK // width))
-        pieces += [(index, start, min(size, depth - start)) for start in range(0, depth, size)]
+        if index != last:
+            pieces += [
+                (index, start, min(size, depth - start), 0, width)
+                for start in range(0, depth, size)
+            ]
+    pieces += [
+        (last, 0, depth, start, min(COLUMNS, widths[last] - start))
+        for start in range(0, widths[last], COLUMNS)
+    ]
     bases = [sum(widths[:index]) for index in range(len(widths))]
     count = len(weights)
 
@@ -120,11 +130,11 @@
         ]
         copies = [
             pltpu.make_async_copy(
-                weight_refs[index].at[pl.ds(start, size)],
-                weights_in[index].at[pl.ds(start, size)],
+                weight_refs[index].at[pl.ds(start, size), pl.ds(left, wide_by)],
+                weights_in[index].at[pl.ds(start, size), pl.ds(left, wide_by)],
                 sems.at[2 + i],
             )
-            for i, (index, start, size) in enumerate(pieces)
+            for i, (index, start, size, left, wide_by) in enumerate(pieces)
         ]
         for copy in first + copies:
             copy.start()
@@ -155,16 +165,16 @@
             ),
         )
         total = None
-        for copy, (index, start, size) in zip(copies, pieces):
+        for copy, (index, start, size, left, wide_by) in zip(copies, pieces):
             copy.wait()
             product = jnp.dot(
                 rows_in[:, start : start + size],
-                weights_in[index][pl.ds(start, size)],
+                weights_in[index][pl.ds(start, size), pl.ds(left, wide_by)],
                 preferred_element_type=jnp.float32,
             )
             total = product if start == 0 else total + product
             if start + size == depth:
-                put(bases[index], widths[index], total)
+                put(bases[index] + left, wide_by, total)
 
     return local_kernel(
         body,

time: 41.7 us -> 41.5 us (level)
  no operation moved by 1% of the time
where the time goes in v8:
time: 41.5 us; the launch traced here: 41.2 us
  starting transfers between devices  19.3 us (47%)
  Pallas kernels  13.9 us (33%)
  waiting for transfers between devices  7.27 us (18%)
  between operations  0.73 us (2%)
    pallas_call x10, Pallas kernels, local_kernel(): pl.pallas_call(body, out_shape=out_shape, in_specs=[spec for _, spec in i...  13.9 us
    ppermute x6, starting transfers between devices, sum_parts(): lax.ppermute(sent, axis, list(enumerate(p)))  10.1 us
    ppermute x12, starting transfers between devices, swap(): return lax.ppermute(values, axis, [(i, i ^ distance) for i in range(size)])  9.23 us
    ppermute x12, waiting for transfers between devices, swap(): return lax.ppermute(values, axis, [(i, i ^ distance) for i in range(size)])  4.35 us
    ppermute x6, waiting for transfers between devices, sum_parts(): lax.ppermute(sent, axis, list(enumerate(p)))  2.92 us
  transfers between devices with their start and end apart: 18, of which 10 were waited for; matrix products, arithmetic and copies ran while one was open for 0% of the time, Pallas kernels for 15%

profile of v8, /device:TPU:0, one launch (start us, length us, event | category | flops | bytes accessed | tf_op | source)
XLA Modules:
  0.0 41.2 jit_solution(14857779687505505802)
XLA Ops:
  0.6 4.1 %project.1 = (f32[2,4640]{1,0:T(2,128)S(1)}, bf16[2,4640]{1,0:T(2,128)(2,1)S(1)}, bf16[2,4640]{1,0:T(2,128)(2,1)S(1)}, bf16[2,4640]{1,0:T(2,128)(2,1)S(1)}) custom-call(bf16[2,4,1024]{2,1,0:T(4,128)(2,1)} %refs_11_.1, bf16[32,1024]{1,0:T(8,128)(2,1)} %bitcast.9, bf16[1024,2048]{1,0:T(8,128)(2,1)} %refs_2_.1, bf16[1024,2048]{1,0:T(8,128)(2,1)} %refs_3_.2, ...), custom_call_target="tpu_custom_call" | custom-call | flops 10485760 | bytes 10485760 | tf_op jit(solution)/shard_map/project/pallas_call | solution.py:67
  4.8 3.0 %collective-permute-start = (bf16[2,4640]{1,0:T(2,128)(2,1)S(1)}, bf16[2,4640]{1,0:T(2,128)(2,1)S(1)}, u32[]{:S(2)}, u32[]{:S(2)}) collective-permute-start(bf16[2,4640]{1,0:T(2,128)(2,1)S(1)} %get-tuple-element.39), channel_id=1, source_target_pairs={{0,8},{4,12},{8,0},{12,4},{1,9},{5,13},{9,1},{13,5},{2,10},{6,14},... | collective-permute-start | bytes 55688 | tf_op jit(solution)/shard_map/ppermute | solution.py:20
  8.0 2.0 %prepare.1 = (f32[3,2048]{1,0:T(4,128)S(1)}, bf16[32,2048]{1,0:T(8,128)(2,1)S(1)}, f32[4,2048]{1,0:T(4,128)S(1)}, f32[4,256]{1,0:T(4,128)S(1)}, f32[4,256]{1,0:T...) custom-call(f32[1,32]{1,0:T(1,128)} %bitcast.11, ...), custom_call_target="tpu_custom_call" | custom-call | flops 4194304 | bytes 4194304 | tf_op jit(solution)/shard_map/prepare/pallas_call | solution.py:67
  10.0 1.0 %collective-permute-done.1.refs_2_ = bf16[2,4640]{1,0:T(2,128)(2,1)S(1)} collective-permute-done((bf16[2,4640]{1,0:T(2,128)(2,1)S(1)}, bf16[2,4640]{1,0:T(2,128)(2,1)S(1)}, u32[]{:S(2)}, u32[]{:S(2)}) %collective-permute-start.1) | collective-permute-done | bytes 18592 | tf_op jit(solution)/shard_map/ppermute | solution.py:20
  11.0 0.6 %mix.1 = (bf16[2,2048]{1,0:T(2,128)(2,1)S(1)}, f32[2,2560]{1,0:T(2,128)S(1)}, f32[1,3,2048]{2,1,0:T(4,128)S(1)}, f32[2,256]{1,0:T(2,128)S(1)}) custom-call(f32[2,4640]{1,0:T(2,128)S(1)} %get-tuple-element.38.refs_0_, bf16[2,4640]{1,0:T(2,128)(2,1)S(1)} %collective-permute-done.refs_1_, bf16[2,4640]{1,0:T(2,128)(2,1)S(1)} %collective-permute-done.1.refs_2_, ...), custom_call_target="tpu_custom_call" | custom-call | flops 4194304 | bytes 4194304 | tf_op jit(solution)/shard_map/mix/pallas_call | solution.py:67
  11.6 0.6 %collective-permute-start.5 = (bf16[2,2048]{1,0:T(2,128)(2,1)S(1)}, bf16[2,2048]{1,0:T(2,128)(2,1)S(1)}, u32[]{:S(2)}, u32[]{:S(2)}) collective-permute-start(bf16[2,2048]{1,0:T(2,128)(2,1)S(1)} %get-tuple-element.57.refs_0_), channel_id=1, source_target_pairs={{0,12},{4,8},{8,4},{12,0},{1,13},{5,9},{9,5},{13,1},{2,14},{6,10},... | collective-permute-start | bytes 24584 | tf_op jit(solution)/shard_map/ppermute | solution.py:20
  12.2 0.6 %collective-permute-start.4 = (bf16[2,2048]{1,0:T(2,128)(2,1)S(1)}, bf16[2,2048]{1,0:T(2,128)(2,1)S(1)}, u32[]{:S(2)}, u32[]{:S(2)}) collective-permute-start(bf16[2,2048]{1,0:T(2,128)(2,1)S(1)} %get-tuple-element.57.refs_0_), channel_id=1, source_target_pairs={{0,8},{4,12},{8,0},{12,4},{1,9},{5,13},{9,1},{13,5},{2,10},{6,14},... | collective-permute-start | bytes 24584 | tf_op jit(solution)/shard_map/ppermute | solution.py:20
  12.8 0.7 %collective-permute-start.3 = (bf16[2,2048]{1,0:T(2,128)(2,1)S(1)}, bf16[2,2048]{1,0:T(2,128)(2,1)S(1)}, u32[]{:S(2)}, u32[]{:S(2)}) collective-permute-start(bf16[2,2048]{1,0:T(2,128)(2,1)S(1)} %get-tuple-element.57.refs_0_), channel_id=1, source_target_pairs={{0,4},{4,0},{8,12},{12,8},{1,5},{5,1},{9,13},{13,9},{2,6},{6,2},{1... | collective-permute-start | bytes 24584 | tf_op jit(solution)/shard_map/ppermute | solution.py:20
  13.5 2.0 %fetch.1.refs_5_ = bf16[1536,1024]{1,0:T(8,128)(2,1)S(1)} custom-call(bf16[2048,1024]{1,0:T(8,128)(2,1)} %source.1, f32[2,256]{1,0:T(2,128)S(1)} %get-tuple-element.54.write_ref._), custom_call_target="tpu_custom_call" | custom-call | flops 8388608 | bytes 8388608 | tf_op jit(solution)/shard_map/fetch/pallas_call | solution.py:67
  15.6 0.3 collective-permute-done.4.refs_2_
  15.9 0.6 %project_out.1 = (f32[8,1024]{1,0:T(8,128)S(1)}, bf16[8,1024]{1,0:T(8,128)(2,1)S(1)}) custom-call(bf16[2,2048]{1,0:T(2,128)(2,1)S(1)} %get-tuple-element.57.refs_0_, bf16[2,2048]{1,0:T(2,128)(2,1)S(1)} %collective-permute-done.3.refs_1_, bf16[2,2048]{1,0:T(2,128)(2,1)S(1)} %collective-permute-done.4.refs_2_, ...), custom_call_target="tpu_custom_call" | custom-call | flops 4194304 | bytes 4194304 | tf_op jit(solution)/shard_map/project_out/pallas_call | solution.py:67
  16.5 1.6 %collective-permute-start.8 = (bf16[8,1024]{1,0:T(8,128)(2,1)S(1)}, bf16[8,1024]{1,0:T(8,128)(2,1)S(1)}, u32[]{:S(2)}, u32[]{:S(2)}) collective-permute-start(bf16[8,1024]{1,0:T(8,128)(2,1)S(1)} %get-tuple-element.60), channel_id=1, source_target_pairs={{0,1},{1,3},{2,0},{3,2},{4,5},{5,7},{6,4},{7,6},{8,9},{9,11},{10,8... | collective-permute-start | bytes 49160 | tf_op jit(solution)/shard_map/ppermute | solution.py:36
  18.1 2.5 %collective-permute-start.7 = (bf16[8,1024]{1,0:T(8,128)(2,1)S(1)}, bf16[8,1024]{1,0:T(8,128)(2,1)S(1)}, u32[]{:S(2)}, u32[]{:S(2)}) collective-permute-start(bf16[8,1024]{1,0:T(8,128)(2,1)S(1)} %get-tuple-element.60), channel_id=1, source_target_pairs={{0,3},{1,2},{2,1},{3,0},{4,7},{5,6},{6,5},{7,4},{8,11},{9,10},{10,... | collective-permute-start | bytes 49160 | tf_op jit(solution)/shard_map/ppermute | solution.py:36
  20.6 1.6 %collective-permute-start.6 = (bf16[8,1024]{1,0:T(8,128)(2,1)S(1)}, bf16[8,1024]{1,0:T(8,128)(2,1)S(1)}, u32[]{:S(2)}, u32[]{:S(2)}) collective-permute-start(bf16[8,1024]{1,0:T(8,128)(2,1)S(1)} %get-tuple-element.60), channel_id=1, source_target_pairs={{0,2},{1,0},{2,3},{3,1},{4,6},{5,4},{6,7},{7,5},{8,10},{9,8},{10,1... | collective-permute-start | bytes 49160 | tf_op jit(solution)/shard_map/ppermute | solution.py:36
  22.2 1.3 %renew.1 = (f32[1,32,64,128]{3,2,1,0:T(8,128)}, f32[8,1024]{1,0:T(8,128)S(1)}, bf16[1,3,2048]{2,1,0:T(4,128)(2,1)}, bf16[1,3,256]{2,1,0:T(4,128)(2,1)}, bf16[1,3,256]{2,1,0:T(4,128)(2,1)}) custom-call(f32[2,2560]{1,0:T(2,128)S(1)} %get-tuple-element.52.pre_ref, f32[1,3,2048]{2,1,0:T(4,128)S(1)} %get-tuple-element.53.coef_ref, ...), custom_call_target="tpu_custom_call" | custom-call | flops 4194304 | bytes 4194304 | tf_op jit(solution)/shard_map/renew/pallas_call | solution.py:67
  23.6 0.7 %collective-permute-done.6 = bf16[8,1024]{1,0:T(8,128)(2,1)S(1)} collective-permute-done((bf16[8,1024]{1,0:T(8,128)(2,1)S(1)}, bf16[8,1024]{1,0:T(8,128)(2,1)S(1)}, u32[]{:S(2)}, u32[]{:S(2)}) %collective-permute-start.6) | collective-permute-done | bytes 16416 | tf_op jit(solution)/shard_map/ppermute | solution.py:36
  24.4 0.8 %collective-permute-start.10 = (bf16[8,1024]{1,0:T(8,128)(2,1)S(1)}, bf16[8,1024]{1,0:T(8,128)(2,1)S(1)}, u32[]{:S(2)}, u32[]{:S(2)}) collective-permute-start(bf16[8,1024]{1,0:T(8,128)(2,1)S(1)} %get-tuple-element.73.refs_0_), channel_id=1, source_target_pairs={{0,8},{4,12},{8,0},{12,4},{1,9},{5,13},{9,1},{13,5},{2,10},{6,14},... | collective-permute-start | bytes 49160 | tf_op jit(solution)/shard_map/ppermute | solution.py:20
  25.2 1.1 %collective-permute-start.9 = (bf16[8,1024]{1,0:T(8,128)(2,1)S(1)}, bf16[8,1024]{1,0:T(8,128)(2,1)S(1)}, u32[]{:S(2)}, u32[]{:S(2)}) collective-permute-start(bf16[8,1024]{1,0:T(8,128)(2,1)S(1)} %get-tuple-element.73.refs_0_), channel_id=1, source_target_pairs={{0,4},{4,0},{8,12},{12,8},{1,5},{5,1},{9,13},{13,9},{2,6},{6,2},{1... | collective-permute-start | bytes 49160 | tf_op jit(solution)/shard_map/ppermute | solution.py:20
  26.3 0.4 expert_near.1.refs_3_
  26.6 0.9 %collective-permute-done.11.refs_2_ = bf16[8,1024]{1,0:T(8,128)(2,1)S(1)} collective-permute-done((bf16[8,1024]{1,0:T(8,128)(2,1)S(1)}, bf16[8,1024]{1,0:T(8,128)(2,1)S(1)}, u32[]{:S(2)}, u32[]{:S(2)}) %collective-permute-start.11) | collective-permute-done | bytes 16416 | tf_op jit(solution)/shard_map/ppermute | solution.py:20
  27.6 0.7 %collective-permute-done.10.refs_1_ = bf16[8,1024]{1,0:T(8,128)(2,1)S(1)} collective-permute-done((bf16[8,1024]{1,0:T(8,128)(2,1)S(1)}, bf16[8,1024]{1,0:T(8,128)(2,1)S(1)}, u32[]{:S(2)}, u32[]{:S(2)}) %collective-permute-start.10) | collective-permute-done | bytes 16416 | tf_op jit(solution)/shard_map/ppermute | solution.py:20
  28.2 1.8 %experts_far.1 = (bf16[4,8,256]{2,1,0:T(8,128)(2,1)S(1)}, bf16[8,1024]{1,0:T(8,128)(2,1)S(1)}, bf16[8,1024]{1,0:T(8,128)(2,1)S(1)}, bf16[8,1024]{1,0:T(8,128)(2,1)S(1)}) custom-call(bf16[8,1024]{1,0:T(8,128)(2,1)S(1)} %collective-permute-done.9.refs_0_, bf16[8,1024]{1,0:T(8,128)(2,1)S(1)} %collective-permute-done.10.refs_1_, ...), custom_call_target="tpu_custom_call" | custom-call | flops 16777216 | bytes 16777216 | tf_op jit(solution)/shard_map/experts_far/pallas_call | solution.py:67
  30.0 0.7 %collective-permute-start.12 = (bf16[8,1024]{1,0:T(8,128)(2,1)S(1)}, bf16[8,1024]{1,0:T(8,128)(2,1)S(1)}, u32[]{:S(2)}, u32[]{:S(2)}) collective-permute-start(bf16[8,1024]{1,0:T(8,128)(2,1)S(1)} %get-tuple-element.64), channel_id=1, source_target_pairs={{0,8},{4,12},{8,0},{12,4},{1,9},{5,13},{9,1},{13,5},{2,10},{6,14},... | collective-permute-start | bytes 49160 | tf_op jit(solution)/shard_map/ppermute | solution.py:20
  31.0 1.2 %collective-permute-start.14 = (bf16[8,1024]{1,0:T(8,128)(2,1)S(1)}, bf16[8,1024]{1,0:T(8,128)(2,1)S(1)}, u32[]{:S(2)}, u32[]{:S(2)}) collective-permute-start(bf16[8,1024]{1,0:T(8,128)(2,1)S(1)} %get-tuple-element.66), channel_id=1, source_target_pairs={{0,4},{4,0},{8,12},{12,8},{1,5},{5,1},{9,13},{13,9},{2,6},{6,2},{1... | collective-permute-start | bytes 49160 | tf_op jit(solution)/shard_map/ppermute | solution.py:20
  32.2 0.4 experts_close.1
  32.6 1.2 %collective-permute-done.12 = bf16[8,1024]{1,0:T(8,128)(2,1)S(1)} collective-permute-done((bf16[8,1024]{1,0:T(8,128)(2,1)S(1)}, bf16[8,1024]{1,0:T(8,128)(2,1)S(1)}, u32[]{:S(2)}, u32[]{:S(2)}) %collective-permute-start.12) | collective-permute-done | bytes 16416 | tf_op jit(solution)/shard_map/ppermute | solution.py:20
  34.1 1.9 %collective-permute-start.17 = (bf16[8,1024]{1,0:T(8,128)(2,1)S(1)}, bf16[8,1024]{1,0:T(8,128)(2,1)S(1)}, u32[]{:S(2)}, u32[]{:S(2)}) collective-permute-start(bf16[8,1024]{1,0:T(8,128)(2,1)S(1)} %get-tuple-element.71), channel_id=1, source_target_pairs={{0,3},{1,2},{2,1},{3,0},{4,7},{5,6},{6,5},{7,4},{8,11},{9,10},{10,... | collective-permute-start | bytes 49160 | tf_op jit(solution)/shard_map/ppermute | solution.py:36
  35.9 0.8 %collective-permute-start.16 = (bf16[8,1024]{1,0:T(8,128)(2,1)S(1)}, bf16[8,1024]{1,0:T(8,128)(2,1)S(1)}, u32[]{:S(2)}, u32[]{:S(2)}) collective-permute-start(bf16[8,1024]{1,0:T(8,128)(2,1)S(1)} %get-tuple-element.71), channel_id=1, source_target_pairs={{0,2},{1,3},{2,0},{3,1},{4,6},{5,7},{6,4},{7,5},{8,10},{9,11},{10,... | collective-permute-start | bytes 49160 | tf_op jit(solution)/shard_map/ppermute | solution.py:36
  36.7 1.8 %collective-permute-start.15 = (bf16[8,1024]{1,0:T(8,128)(2,1)S(1)}, bf16[8,1024]{1,0:T(8,128)(2,1)S(1)}, u32[]{:S(2)}, u32[]{:S(2)}) collective-permute-start(bf16[8,1024]{1,0:T(8,128)(2,1)S(1)} %get-tuple-element.71), channel_id=1, source_target_pairs={{0,1},{1,0},{2,3},{3,2},{4,5},{5,4},{6,7},{7,6},{8,9},{9,8},{10,11... | collective-permute-start | bytes 49160 | tf_op jit(solution)/shard_map/ppermute | solution.py:36
  38.5 1.1 %collective-permute-done.17.refs_4_ = bf16[8,1024]{1,0:T(8,128)(2,1)S(1)} collective-permute-done((bf16[8,1024]{1,0:T(8,128)(2,1)S(1)}, bf16[8,1024]{1,0:T(8,128)(2,1)S(1)}, u32[]{:S(2)}, u32[]{:S(2)}) %collective-permute-start.17) | collective-permute-done | bytes 16416 | tf_op jit(solution)/shard_map/ppermute | solution.py:36
  39.7 0.9 %collective-permute-done.16.refs_3_ = bf16[8,1024]{1,0:T(8,128)(2,1)S(1)} collective-permute-done((bf16[8,1024]{1,0:T(8,128)(2,1)S(1)}, bf16[8,1024]{1,0:T(8,128)(2,1)S(1)}, u32[]{:S(2)}, u32[]{:S(2)}) %collective-permute-start.16) | collective-permute-done | bytes 16416 | tf_op jit(solution)/shard_map/ppermute | solution.py:36
  40.6 0.6 %finish.1 = bf16[2,4,1024]{2,1,0:T(4,128)(2,1)} custom-call(f32[8,1024]{1,0:T(8,128)S(1)} %get-tuple-element.74.refs_0_, f32[8,1024]{1,0:T(8,128)S(1)} %get-tuple-element.72.refs_1_, bf16[8,1024]{1,0:T(8,128)(2,1)S(1)} %collective-permute-done.15.refs_2_, bf16[8,1024]{1,0:T(8,128)(2,1)S(1)} %collective-permute-done.16.refs_3_, ...), custom_call_target="tpu_custom_call" | custom-call | flops 1048576 | bytes 1048576 | tf_op jit(solution)/shard_map/finish/pallas_call | solution.py:67
  (26 shorter events, 1.0 us)
Async XLA Ops:
  4.8 5.2 %collective-permute-start = (bf16[2,4640]{1,0:T(2,128)(2,1)S(1)}, bf16[2,4640]{1,0:T(2,128)(2,1)S(1)}, u32[]{:S(2)}, u32[]{:S(2)}) collective-permute-start(bf16[2,4640]{1,0:T(2,128)(2,1)S(1)} %get-tuple-element.39), channel_id=1, source_target_pairs={{0,8},{4,12},{8,0},{12,4},{1,9},{5,13},{9,1},{13,5},{2,10},{6,14},... | collective-permute-start | bytes 55688 | tf_op jit(solution)/shard_map/ppermute | solution.py:20
  7.8 3.2 %collective-permute-start.1 = (bf16[2,4640]{1,0:T(2,128)(2,1)S(1)}, bf16[2,4640]{1,0:T(2,128)(2,1)S(1)}, u32[]{:S(2)}, u32[]{:S(2)}) collective-permute-start(bf16[2,4640]{1,0:T(2,128)(2,1)S(1)} %get-tuple-element.40), channel_id=1, source_target_pairs={{0,12},{4,8},{8,4},{12,0},{1,13},{5,9},{9,5},{13,1},{2,14},{6,10},... | collective-permute-start | bytes 55688 | tf_op jit(solution)/shard_map/ppermute | solution.py:20
  7.8 3.2 %collective-permute-start.2 = (bf16[2,4640]{1,0:T(2,128)(2,1)S(1)}, bf16[2,4640]{1,0:T(2,128)(2,1)S(1)}, u32[]{:S(2)}, u32[]{:S(2)}) collective-permute-start(bf16[2,4640]{1,0:T(2,128)(2,1)S(1)} %get-tuple-element.41), channel_id=1, source_target_pairs={{0,4},{4,0},{8,12},{12,8},{1,5},{5,1},{9,13},{13,9},{2,6},{6,2},{1... | collective-permute-start | bytes 55688 | tf_op jit(solution)/shard_map/ppermute | solution.py:20
  8.0 18.3 %slice-start = ((s8[8388608]{0:T(1024)(128)(4,1)}), s8[4194304]{0:T(1024)(128)(4,1)S(1)}, s32[]{:S(2)}) async-start(s8[8388608]{0:T(1024)(128)(4,1)} %bitcast.5), calls=%async_computation | async-start | bytes 8388608
  11.6 4.0 %collective-permute-start.5 = (bf16[2,2048]{1,0:T(2,128)(2,1)S(1)}, bf16[2,2048]{1,0:T(2,128)(2,1)S(1)}, u32[]{:S(2)}, u32[]{:S(2)}) collective-permute-start(bf16[2,2048]{1,0:T(2,128)(2,1)S(1)} %get-tuple-element.57.refs_0_), channel_id=1, source_target_pairs={{0,12},{4,8},{8,4},{12,0},{1,13},{5,9},{9,5},{13,1},{2,14},{6,10},... | collective-permute-start | bytes 24584 | tf_op jit(solution)/shard_map/ppermute | solution.py:20
  12.2 3.7 %collective-permute-start.4 = (bf16[2,2048]{1,0:T(2,128)(2,1)S(1)}, bf16[2,2048]{1,0:T(2,128)(2,1)S(1)}, u32[]{:S(2)}, u32[]{:S(2)}) collective-permute-start(bf16[2,2048]{1,0:T(2,128)(2,1)S(1)} %get-tuple-element.57.refs_0_), channel_id=1, source_target_pairs={{0,8},{4,12},{8,0},{12,4},{1,9},{5,13},{9,1},{13,5},{2,10},{6,14},... | collective-permute-start | bytes 24584 | tf_op jit(solution)/shard_map/ppermute | solution.py:20
  12.8 3.0 %collective-permute-start.3 = (bf16[2,2048]{1,0:T(2,128)(2,1)S(1)}, bf16[2,2048]{1,0:T(2,128)(2,1)S(1)}, u32[]{:S(2)}, u32[]{:S(2)}) collective-permute-start(bf16[2,2048]{1,0:T(2,128)(2,1)S(1)} %get-tuple-element.57.refs_0_), channel_id=1, source_target_pairs={{0,4},{4,0},{8,12},{12,8},{1,5},{5,1},{9,13},{13,9},{2,6},{6,2},{1... | collective-permute-start | bytes 24584 | tf_op jit(solution)/shard_map/ppermute | solution.py:20
  13.5 12.8 %slice-start.1 = ((s8[8388608]{0:T(1024)(128)(4,1)}), s8[4194304]{0:T(1024)(128)(4,1)S(1)}, s32[]{:S(2)}) async-start(s8[8388608]{0:T(1024)(128)(4,1)} %bitcast.5), calls=%async_computation.1 | async-start | bytes 8388608
  13.5 14.7 %slice-start.2 = ((s8[8388608]{0:T(1024)(128)(4,1)}), s8[4194304]{0:T(1024)(128)(4,1)S(1)}, s32[]{:S(2)}) async-start(s8[8388608]{0:T(1024)(128)(4,1)} %bitcast.7), calls=%async_computation.2 | async-start | bytes 8388608
  15.9 12.4 %slice-start.3 = ((s8[8388608]{0:T(1024)(128)(4,1)}), s8[4194304]{0:T(1024)(128)(4,1)S(1)}, s32[]{:S(2)}) async-start(s8[8388608]{0:T(1024)(128)(4,1)} %bitcast.7), calls=%async_computation.3 | async-start | bytes 8388608
  16.5 7.0 %collective-permute-start.8 = (bf16[8,1024]{1,0:T(8,128)(2,1)S(1)}, bf16[8,1024]{1,0:T(8,128)(2,1)S(1)}, u32[]{:S(2)}, u32[]{:S(2)}) collective-permute-start(bf16[8,1024]{1,0:T(8,128)(2,1)S(1)} %get-tuple-element.60), channel_id=1, source_target_pairs={{0,1},{1,3},{2,0},{3,2},{4,5},{5,7},{6,4},{7,6},{8,9},{9,11},{10,8... | collective-permute-start | bytes 49160 | tf_op jit(solution)/shard_map/ppermute | solution.py:36
  18.1 5.5 %collective-permute-start.7 = (bf16[8,1024]{1,0:T(8,128)(2,1)S(1)}, bf16[8,1024]{1,0:T(8,128)(2,1)S(1)}, u32[]{:S(2)}, u32[]{:S(2)}) collective-permute-start(bf16[8,1024]{1,0:T(8,128)(2,1)S(1)} %get-tuple-element.60), channel_id=1, source_target_pairs={{0,3},{1,2},{2,1},{3,0},{4,7},{5,6},{6,5},{7,4},{8,11},{9,10},{10,... | collective-permute-start | bytes 49160 | tf_op jit(solution)/shard_map/ppermute | solution.py:36
  20.6 3.7 %collective-permute-start.6 = (bf16[8,1024]{1,0:T(8,128)(2,1)S(1)}, bf16[8,1024]{1,0:T(8,128)(2,1)S(1)}, u32[]{:S(2)}, u32[]{:S(2)}) collective-permute-start(bf16[8,1024]{1,0:T(8,128)(2,1)S(1)} %get-tuple-element.60), channel_id=1, source_target_pairs={{0,2},{1,0},{2,3},{3,1},{4,6},{5,4},{6,7},{7,5},{8,10},{9,8},{10,1... | collective-permute-start | bytes 49160 | tf_op jit(solution)/shard_map/ppermute | solution.py:36
  24.3 3.2 %collective-permute-start.11 = (bf16[8,1024]{1,0:T(8,128)(2,1)S(1)}, bf16[8,1024]{1,0:T(8,128)(2,1)S(1)}, u32[]{:S(2)}, u32[]{:S(2)}) collective-permute-start(bf16[8,1024]{1,0:T(8,128)(2,1)S(1)} %get-tuple-element.73.refs_0_), channel_id=1, source_target_pairs={{0,12},{4,8},{8,4},{12,0},{1,13},{5,9},{9,5},{13,1},{2,14},{6,10},... | collective-permute-start | bytes 49160 | tf_op jit(solution)/shard_map/ppermute | solution.py:20
  24.4 3.8 %collective-permute-start.10 = (bf16[8,1024]{1,0:T(8,128)(2,1)S(1)}, bf16[8,1024]{1,0:T(8,128)(2,1)S(1)}, u32[]{:S(2)}, u32[]{:S(2)}) collective-permute-start(bf16[8,1024]{1,0:T(8,128)(2,1)S(1)} %get-tuple-element.73.refs_0_), channel_id=1, source_target_pairs={{0,8},{4,12},{8,0},{12,4},{1,9},{5,13},{9,1},{13,5},{2,10},{6,14},... | collective-permute-start | bytes 49160 | tf_op jit(solution)/shard_map/ppermute | solution.py:20
  25.2 3.0 %collective-permute-start.9 = (bf16[8,1024]{1,0:T(8,128)(2,1)S(1)}, bf16[8,1024]{1,0:T(8,128)(2,1)S(1)}, u32[]{:S(2)}, u32[]{:S(2)}) collective-permute-start(bf16[8,1024]{1,0:T(8,128)(2,1)S(1)} %get-tuple-element.73.refs_0_), channel_id=1, source_target_pairs={{0,4},{4,0},{8,12},{12,8},{1,5},{5,1},{9,13},{13,9},{2,6},{6,2},{1... | collective-permute-start | bytes 49160 | tf_op jit(solution)/shard_map/ppermute | solution.py:20
  30.0 3.8 %collective-permute-start.12 = (bf16[8,1024]{1,0:T(8,128)(2,1)S(1)}, bf16[8,1024]{1,0:T(8,128)(2,1)S(1)}, u32[]{:S(2)}, u32[]{:S(2)}) collective-permute-start(bf16[8,1024]{1,0:T(8,128)(2,1)S(1)} %get-tuple-element.64), channel_id=1, source_target_pairs={{0,8},{4,12},{8,0},{12,4},{1,9},{5,13},{9,1},{13,5},{2,10},{6,14},... | collective-permute-start | bytes 49160 | tf_op jit(solution)/shard_map/ppermute | solution.py:20
  30.7 3.3 %collective-permute-start.13 = (bf16[8,1024]{1,0:T(8,128)(2,1)S(1)}, bf16[8,1024]{1,0:T(8,128)(2,1)S(1)}, u32[]{:S(2)}, u32[]{:S(2)}) collective-permute-start(bf16[8,1024]{1,0:T(8,128)(2,1)S(1)} %get-tuple-element.65), channel_id=1, source_target_pairs={{0,12},{4,8},{8,4},{12,0},{1,13},{5,9},{9,5},{13,1},{2,14},{6,10},... | collective-permute-start | bytes 49160 | tf_op jit(solution)/shard_map/ppermute | solution.py:20
  31.0 3.1 %collective-permute-start.14 = (bf16[8,1024]{1,0:T(8,128)(2,1)S(1)}, bf16[8,1024]{1,0:T(8,128)(2,1)S(1)}, u32[]{:S(2)}, u32[]{:S(2)}) collective-permute-start(bf16[8,1024]{1,0:T(8,128)(2,1)S(1)} %get-tuple-element.66), channel_id=1, source_target_pairs={{0,4},{4,0},{8,12},{12,8},{1,5},{5,1},{9,13},{13,9},{2,6},{6,2},{1... | collective-permute-start | bytes 49160 | tf_op jit(solution)/shard_map/ppermute | solution.py:20
  34.1 5.6 %collective-permute-start.17 = (bf16[8,1024]{1,0:T(8,128)(2,1)S(1)}, bf16[8,1024]{1,0:T(8,128)(2,1)S(1)}, u32[]{:S(2)}, u32[]{:S(2)}) collective-permute-start(bf16[8,1024]{1,0:T(8,128)(2,1)S(1)} %get-tuple-element.71), channel_id=1, source_target_pairs={{0,3},{1,2},{2,1},{3,0},{4,7},{5,6},{6,5},{7,4},{8,11},{9,10},{10,... | collective-permute-start | bytes 49160 | tf_op jit(solution)/shard_map/ppermute | solution.py:36
  35.9 4.7 %collective-permute-start.16 = (bf16[8,1024]{1,0:T(8,128)(2,1)S(1)}, bf16[8,1024]{1,0:T(8,128)(2,1)S(1)}, u32[]{:S(2)}, u32[]{:S(2)}) collective-permute-start(bf16[8,1024]{1,0:T(8,128)(2,1)S(1)} %get-tuple-element.71), channel_id=1, source_target_pairs={{0,2},{1,3},{2,0},{3,1},{4,6},{5,7},{6,4},{7,5},{8,10},{9,11},{10,... | collective-permute-start | bytes 49160 | tf_op jit(solution)/shard_map/ppermute | solution.py:36
  36.7 3.9 %collective-permute-start.15 = (bf16[8,1024]{1,0:T(8,128)(2,1)S(1)}, bf16[8,1024]{1,0:T(8,128)(2,1)S(1)}, u32[]{:S(2)}, u32[]{:S(2)}) collective-permute-start(bf16[8,1024]{1,0:T(8,128)(2,1)S(1)} %get-tuple-element.71), channel_id=1, source_target_pairs={{0,1},{1,0},{2,3},{3,2},{4,5},{5,4},{6,7},{7,6},{8,9},{9,8},{10,11... | collective-permute-start | bytes 49160 | tf_op jit(solution)/shard_map/ppermute | solution.py:36
